TPU v7x, 32 devices: a whole 2x2x4 slice. The times are simulated.
32 devices in a mesh: beam: 2 (over core), tx: 2 (over y), ty: 4 (over z), dom: 2 (over x).
Axes of the slice: x: 2, y: 2, z: 4, core: 2. Of those that a mesh axis runs over, the one named last changes fastest.
Arguments:
- cell_row: int32 [2, 262144], P('beam', ('tx', 'ty', 'dom')), may hold values from 0 to 1022
- cell_col: int32 [2, 262144], P('beam', ('tx', 'ty', 'dom')), may hold values from 0 to 510
- weights: float32 [2, 262144], P('beam', ('tx', 'ty', 'dom')), may hold values from -6 to 6
- momenta: float32 [2, 2, 262144], P('beam', None, ('tx', 'ty', 'dom')), may hold values from -6 to 6
Outputs:
- kicked: float32 [2, 2, 262144], P('beam', None, ('tx', 'ty', 'dom'))
Inputs may be any that keep to these rules, and one draw needn't show every extreme that they name: cell_row is a row within the tile of 1024 rows that holds the macroparticle, which lies on a device of that tile; its cloud also covers the next row. cell_col is a column within the tile of 512 columns that holds the macroparticle; its cloud also covers the next column.
All inputs are finite; a program needn't handle non-finite values.
Results may differ from a plain program's by a relative error of at most 0.00005.
Values sent between devices are 32-bit elements; how exact they have to be, the bound alone decides.
No kernel may reach another device: no remote copies, remote signals or barrier semaphores. Data moves between devices by JAX's collectives and lax.ppermute only.
A program may use at most 64 MiB of HBM per device.

v0:
```python
import jax
import jax.numpy as jnp
from jax import lax
from jax.sharding import PartitionSpec as P

GRID = 2048


highest = lax.Precision.HIGHEST
kick_gain = 2.0
block_rows = 1024


def partner(block, axis, stride):
    count = lax.axis_size(axis)
    route = []
    for low in range(count):
        high = low | 1 << stride
        if high != low and high < count:
            route += [(low, high), (high, low)]
    return lax.ppermute(block, axis, route)


def phase_angles(position, wavenum, points):
    period = 2 * (points + 1)
    phase_idx = (position + 1) * (wavenum + 1) % period
    return jnp.pi * phase_idx.astype(jnp.float32) / (points + 1)


def basis(position, wavenum, points):
    angles = phase_angles(position, wavenum, points)
    scaling = jnp.sqrt(jnp.float32(2.0) / (points + 1))
    return scaling * jnp.sin(angles)


def paired_tables(position, wavenum, points):
    angles = phase_angles(position, wavenum, points)
    scaling = jnp.sqrt(jnp.float32(2.0) / (points + 1))
    wavenumber = jnp.pi * (wavenum + 1).astype(jnp.float32) / (points + 1)
    return (scaling * jnp.sin(angles), -scaling * wavenumber * jnp.cos(angles))


def eigen_value(wavenum, points):
    halfsin = jnp.sin(jnp.pi * (wavenum + 1).astype(jnp.float32) / (2 * (points + 1)))
    return 4.0 * halfsin * halfsin


def green(row_modes, col_modes, points):
    return 1.0 / (eigen_value(row_modes, points) + eigen_value(col_modes, points))


def matmul(left, right):
    return jnp.dot(left, right, precision=highest, preferred_element_type=jnp.float32)


def shards(cell_row, cell_col, weights, momenta):
    tile_rows = GRID // lax.axis_size("tx")
    tile_cols = GRID // lax.axis_size("ty")
    share_cols = tile_cols // lax.axis_size("dom")
    count = cell_row.shape[1]
    step_rows = min(block_rows, count)
    turns = count // step_rows
    row_start = lax.axis_index("tx") * tile_rows
    col_group = lax.axis_index("ty") * lax.axis_size("dom") + lax.axis_index("dom")
    my_rows = row_start + jnp.arange(tile_rows, dtype=jnp.int32)
    my_cols = col_group * share_cols + jnp.arange(share_cols, dtype=jnp.int32)
    row_cells = jnp.arange(tile_rows, dtype=jnp.int32)
    col_cells = jnp.arange(tile_cols, dtype=jnp.int32)

    def spread(step_no):
        offset = step_no * step_rows
        rows_here = lax.dynamic_slice_in_dim(cell_row[0], offset, step_rows)
        cols_here = lax.dynamic_slice_in_dim(cell_col[0], offset, step_rows)
        row_w = 0.75 * (rows_here[:, None] == row_cells[None, :]).astype(jnp.float32) + 0.25 * (
            rows_here[:, None] + 1 == row_cells[None, :]
        ).astype(jnp.float32)
        col_w = 0.625 * (cols_here[:, None] == col_cells[None, :]).astype(jnp.float32) + 0.375 * (
            cols_here[:, None] + 1 == col_cells[None, :]
        ).astype(jnp.float32)
        return (row_w, col_w, offset)

    def deposit(step_no, running):
        row_w, col_w, offset = spread(step_no)
        charges = lax.dynamic_slice_in_dim(weights[0], offset, step_rows)
        return running + lax.dot_general(
            row_w,
            col_w * charges[:, None],
            (((0,), (0,)), ((), ())),
            precision=highest,
            preferred_element_type=jnp.float32,
        )

    tile_charge = lax.fori_loop(0, turns, deposit, jnp.zeros((tile_rows, tile_cols), jnp.float32))
    charge = lax.psum_scatter(tile_charge, "dom", scatter_dimension=1, tiled=True)
    segment = lax.all_gather(charge, "tx", axis=0, tiled=True)
    wave_in = jnp.arange(segment.shape[0], dtype=jnp.int32)
    row_done = matmul(basis(my_rows[:, None], wave_in[None, :], GRID), segment)
    segment = lax.all_gather(row_done, ("ty", "dom"), axis=1, tiled=True)
    positions = jnp.arange(segment.shape[1], dtype=jnp.int32)
    spectrum = matmul(segment, basis(positions[:, None], my_cols[None, :], GRID))
    potential_hat = green(my_rows[:, None], my_cols[None, :], GRID) * spectrum
    segment = lax.all_gather(potential_hat, ("ty", "dom"), axis=1, tiled=True)
    wave_in = jnp.arange(segment.shape[1], dtype=jnp.int32)
    sine_part, slope_part = paired_tables(my_cols[None, :], wave_in[:, None], GRID)
    along = matmul(segment, sine_part)
    across = matmul(segment, slope_part)
    pieces = (
        lax.all_gather(along, "tx", axis=0, tiled=True),
        lax.all_gather(across, "tx", axis=0, tiled=True),
    )
    wave_in = jnp.arange(pieces[0].shape[0], dtype=jnp.int32)
    sine_part, slope_part = paired_tables(my_rows[:, None], wave_in[None, :], GRID)
    field_x = matmul(slope_part, pieces[0])
    field_y = matmul(sine_part, pieces[1])
    stacked = jnp.stack([field_x, field_y])
    stacked = partner(stacked, "beam", 0)
    full_field = lax.all_gather(stacked, "dom", axis=2, tiled=True)

    def sample(step_no, kicks):
        row_w, col_w, offset = spread(step_no)
        near_x = matmul(row_w, full_field[0])
        near_y = matmul(row_w, full_field[1])
        paired = jnp.stack([jnp.sum(near_x * col_w, axis=1), jnp.sum(near_y * col_w, axis=1)])
        return lax.dynamic_update_slice_in_dim(kicks, paired, offset, 1)

    kicks = lax.fori_loop(0, turns, sample, jnp.zeros((2, count), jnp.float32))
    return momenta + kick_gain * kicks[None]


def solution(mesh):
    placed = (
        P("beam", ("tx", "ty", "dom")),
        P("beam", ("tx", "ty", "dom")),
        P("beam", ("tx", "ty", "dom")),
        P("beam", None, ("tx", "ty", "dom")),
    )
    return jax.shard_map(
        shards,
        mesh=mesh,
        in_specs=placed,
        out_specs=P("beam", None, ("tx", "ty", "dom")),
        check_vma=False,
    )
```

profile of v0, /device:TPU:0, one launch (start us, length us, event | category | flops | bytes accessed | tf_op | source)
XLA Modules:
  0.0 1097.5 jit_solution(1950408104414940122)
XLA Ops:
  6.5 164.6 %while.31 = (s32[]{:T(128)}, f32[1024,512]{1,0:T(8,128)S(1)}, s32[1,16384]{1,0:T(1,128)}, s32[1,16384]{1,0:T(1,128)}, f32[1,16384]{1,0:T(1,128)}, /*index=5*/s32[]{:T(128)}, s32[]{:T(128)}, s32[]{:T(128)}, s32[]{:T(128)}) while((s32[]{:T(128)}, f32[1024,512]{1,0:T(8,128)S(1)}, s32[1,16384]{1,0:T(1,128)}, ...), condition=%wide.region_1.0_spmd.clone.clone, body=%wide.region_0.0_spmd.clone.clone.sunk | while | flops 6451890176 | bytes 4255909 | solution.py:93
  28.5 8.9 select_add_fusion.14
  59.4 8.9 select_add_fusion.14
  172.5 34.6 %reduce-scatter.2.cloned.1.call-done = f32[1024,256]{1,0:T(8,128)} async-done(((f32[1024,512]{1,0:T(8,128)}), f32[1024,256]{1,0:T(8,128)}) %reduce-scatter.2.cloned.1.call-update) | async-done | bytes 1048592 | tf_op jit(solution)/shard_map/reduce_scatter | solution.py:94
  207.2 34.7 %all-gather.7.cloned.1.call-done = f32[2048,256]{1,0:T(8,128)} async-done(((f32[1024,256]{1,0:T(8,128)}), f32[2048,256]{1,0:T(8,128)}) %all-gather.7.cloned.1.call-update) | async-done | bytes 2097168 | tf_op jit(solution)/shard_map/all_gather | solution.py:95
  241.9 55.4 %fusion.72 = f32[1024,256]{1,0:T(8,128)} fusion(f32[2048,256]{1,0:T(8,128)} %all-gather.7.cloned.1.call-done, s32[2048]{0:T(1024)S(1)} %iota_add_fusion, s32[1024]{0:T(1024)S(1)} %add_add_fusion), kind=kOutput, calls=%fused_computation.85 | convolution fusion | flops 6463422464 | bytes 3158016 | tf_op jit(solution)/shard_map/dot_general | solution.py:53
  297.5 125.4 %all-gather.9.cloned.1.call-done = f32[1024,2048]{1,0:T(8,128)} async-done(((f32[1024,256]{1,0:T(8,128)}), f32[1024,2048]{1,0:T(8,128)}) %all-gather.9.cloned.1.call-update) | async-done | bytes 8388624 | tf_op jit(solution)/shard_map/all_gather | solution.py:98
  422.9 19.0 %fusion.106 = f32[1024,256]{1,0:T(8,128)} fusion(f32[1024,2048]{1,0:T(8,128)} %all-gather.9.cloned.1.call-done, s32[256]{0:T(256)S(1)} %add_add_fusion.1, s32[2048]{0:T(1024)S(1)} %iota_add_fusion, f32[256]{0:T(256)S(1)} %multiply_multiply_fusion.1, f32[1024]{0:T(1024)S(1)} %multiply_multiply_fusion), kind=kOutput, calls=%fused_computation.117 | convolution fusion | flops 6448480256 | bytes 9451520 | tf_op jit(solution)/shard_map/dot_general | solution.py:53
  441.9 123.7 %all-gather.11.cloned.1.call-done = f32[1024,2048]{1,0:T(8,128)} async-done(((f32[1024,256]{1,0:T(8,128)}), f32[1024,2048]{1,0:T(8,128)}) %all-gather.11.cloned.1.call-update) | async-done | bytes 8388624 | tf_op jit(solution)/shard_map/all_gather | solution.py:102
  565.6 18.9 %fusion.100 = f32[1024,256]{1,0:T(8,128)} fusion(f32[1024,2048]{1,0:T(8,128)} %all-gather.11.cloned.1.call-done, s32[256]{0:T(256)S(1)} %add_add_fusion.1, s32[2048]{0:T(1024)S(1)} %iota_add_fusion), kind=kOutput, calls=%fused_computation.113 | convolution fusion | flops 6447693824 | bytes 9446400 | tf_op jit(solution)/shard_map/dot_general | solution.py:53
  584.6 19.5 %fusion.93 = f32[1024,256]{1,0:T(8,128)} fusion(f32[1024,2048]{1,0:T(8,128)} %all-gather.11.cloned.1.call-done, f32[2048]{0:T(1024)S(1)} %convert_multiply_fusion, s32[256]{0:T(256)S(1)} %add_add_fusion.1, s32[2048]{0:T(1024)S(1)} %iota_add_fusion), kind=kOutput, calls=%fused_computation.105 | convolution fusion | flops 6447693824 | bytes 9454592 | tf_op jit(solution)/shard_map/dot_general | solution.py:53
  604.2 11.9 %all-gather.13.cloned.1.call-done = f32[2048,256]{1,0:T(8,128)} async-done(((f32[1024,256]{1,0:T(8,128)}), f32[2048,256]{1,0:T(8,128)}) %all-gather.13.cloned.1.call-update) | async-done | bytes 2097168 | tf_op jit(solution)/shard_map/all_gather | solution.py:108
  616.0 40.3 %fusion.103 = f32[1,1024,256]{2,1,0:T(8,128)S(1)} fusion(f32[2048,256]{1,0:T(8,128)} %all-gather.13.cloned.1.call-done, s32[2048]{0:T(1024)S(1)} %iota_add_fusion, s32[1024]{0:T(1024)S(1)} %add_add_fusion, f32[2048]{0:T(1024)S(1)} %convert_multiply_fusion), kind=kOutput, calls=%fused_computation.116 | convolution fusion | flops 6463422464 | bytes 3166208 | tf_op jit(solution)/shard_map/dot_general | solution.py:53
  656.4 66.6 %fusion.102 = f32[1,1024,256]{2,1,0:T(8,128)S(1)} fusion(f32[2048,256]{1,0:T(8,128)} %all-gather.15.cloned.1.call-done, s32[2048]{0:T(1024)S(1)} %iota_add_fusion, s32[1024]{0:T(1024)S(1)} %add_add_fusion), kind=kOutput, calls=%fused_computation.115 | convolution fusion | flops 6463422464 | bytes 3158016 | tf_op jit(solution)/shard_map/dot_general | solution.py:53
  728.8 56.9 %all-gather.17.cloned.1.call-done = f32[2,1024,512]{2,1,0:T(8,128)} async-done(((f32[2,1024,256]{2,1,0:T(8,128)}), f32[2,1024,512]{2,1,0:T(8,128)}) %all-gather.17.cloned.1.call-update) | async-done | bytes 4194320 | tf_op jit(solution)/shard_map/all_gather | solution.py:117
  785.7 303.9 %while.30 = (s32[]{:T(128)}, f32[2,16384]{1,0:T(2,128)S(1)}, s32[1,16384]{1,0:T(1,128)}, f32[2,1024,512]{2,1,0:T(8,128)}, s32[1,16384]{1,0:T(1,128)}, /*index=5*/s32[]{:T(128)}, s32[]{:T(128)}, s32[]{:T(128)}, s32[]{:T(128)}) while((s32[]{:T(128)}, f32[2,16384]{1,0:T(2,128)S(1)}, s32[1,16384]{1,0:T(1,128)}, ...), condition=%wide.region_6.7_spmd.clone.clone, body=%wide.region_3.6_spmd.clone.clone.sunk | while | flops 12902729728 | bytes 21061808 | solution.py:126
  786.5 10.0 multiply_reduce_fusion.5
  805.5 10.0 multiply_reduce_fusion.5
  824.5 10.0 multiply_reduce_fusion.5
  843.5 10.0 multiply_reduce_fusion.5
  862.5 10.0 multiply_reduce_fusion.5
  881.5 10.0 multiply_reduce_fusion.5
  900.5 10.0 multiply_reduce_fusion.5
  919.4 10.0 multiply_reduce_fusion.5
  938.4 10.0 multiply_reduce_fusion.5
  957.4 10.0 multiply_reduce_fusion.5
  976.4 10.0 multiply_reduce_fusion.5
  995.4 10.0 multiply_reduce_fusion.5
  1014.4 10.0 multiply_reduce_fusion.5
  1033.4 10.0 multiply_reduce_fusion.5
  1052.4 10.0 multiply_reduce_fusion.5
  1071.4 10.0 multiply_reduce_fusion.5
  (223 shorter events, 298.4 us)
Async XLA Ops:
  6.5 200.6 %reduce-scatter.2.cloned.1.call-start = ((), (), s32[]{:S(2)}) async-start(), calls=%async_computation.1 | async-start | bytes 3145728 | tf_op jit(solution)/shard_map/reduce_scatter | solution.py:94
  171.1 1.3 copy-start.1
  172.5 69.4 %all-gather.7.cloned.1.call-start = ((), (), s32[]{:S(2)}) async-start(), calls=%async_computation.2 | async-start | bytes 3145728 | tf_op jit(solution)/shard_map/all_gather | solution.py:95
  207.2 215.7 %all-gather.9.cloned.1.call-start = ((), (), s32[]{:S(2)}) async-start(), calls=%async_computation.3 | async-start | bytes 9437184 | tf_op jit(solution)/shard_map/all_gather | solution.py:98
  297.3 268.3 %all-gather.11.cloned.1.call-start = ((), (), s32[]{:S(2)}) async-start(), calls=%async_computation.4 | async-start | bytes 9437184 | tf_op jit(solution)/shard_map/all_gather | solution.py:102
  441.9 174.2 %all-gather.13.cloned.1.call-start = ((), (), s32[]{:S(2)}) async-start(), calls=%async_computation.5 | async-start | bytes 3145728 | tf_op jit(solution)/shard_map/all_gather | solution.py:108
  584.6 71.8 %all-gather.15.cloned.1.call-start = ((), (), s32[]{:S(2)}) async-start(), calls=%async_computation.6 | async-start | bytes 3145728 | tf_op jit(solution)/shard_map/all_gather | solution.py:109
  604.1 181.5 %all-gather.17.cloned.1.call-start = ((), (), s32[]{:S(2)}) async-start(), calls=%async_computation.7 | async-start | bytes 6291456 | tf_op jit(solution)/shard_map/all_gather | solution.py:117
  723.2 4.2 collective-permute-start
  727.4 1.3 copy-start
  785.7 304.0 %copy-start.2 = (f32[1,2,16384]{2,1,0:T(2,128)S(1)}, f32[1,2,16384]{2,1,0:T(2,128)}, u32[]{:S(2)}) copy-start(f32[1,2,16384]{2,1,0:T(2,128)} %param.11) | copy-start | bytes 393220
  786.5 10.0 copy-start.3
  805.5 10.0 copy-start.3
  824.5 10.0 copy-start.3
  843.5 10.0 copy-start.3
  862.5 10.0 copy-start.3
  881.5 10.0 copy-start.3
  900.5 10.0 copy-start.3
  919.4 10.0 copy-start.3
  938.4 10.0 copy-start.3
  957.4 10.0 copy-start.3
  976.4 10.0 copy-start.3
  995.4 10.0 copy-start.3
  1014.4 10.0 copy-start.3
  1033.4 10.0 copy-start.3
  1052.4 10.0 copy-start.3
  1071.4 10.0 copy-start.3
Sparse Core Ops, SparseCore 0:
  172.6 34.4 reduce-scatter.1
  208.8 33.1 all-gather.6
  297.4 125.3 all-gather.8
  442.0 123.5 all-gather.10
  584.7 31.3 all-gather.12
  617.5 33.1 all-gather.14
  728.9 56.7 all-gather.16
where the time goes:
time: 1110 us; the launch traced here: 1100 us
  matrix products  653 us (59%)
  waiting for transfers between devices  391 us (35%)
  local copies, waits for them, and re-layouts  36.5 us (3%)
  between operations  13.8 us (1%)
    dot_general x38, matrix products, matmul(): jnp.dot(left, right, precision=highest, preferred_element_type=jnp.float32)  511 us
    dot_general x16, matrix products, deposit(): lax.dot_general(row_w, col_w * charges[:, None], (((0,), (0,)), ((), ()))...  142 us
    all_gather x1, waiting for transfers between devices, shards(): segment = lax.all_gather(row_done, ('ty', 'dom'), axis=1, tiled=True)  125 us
    all_gather x1, waiting for transfers between devices, shards(): segment = lax.all_gather(potential_hat, ('ty', 'dom'), axis=1, tiled=True)  124 us
    all_gather x1, waiting for transfers between devices, shards(): full_field = lax.all_gather(stacked, 'dom', axis=2, tiled=True)  56.9 us
    all_gather x1, waiting for transfers between devices, shards(): segment = lax.all_gather(charge, 'tx', axis=0, tiled=True)  34.7 us
    reduce_scatter x1, waiting for transfers between devices, shards(): lax.psum_scatter(tile_charge, 'dom', scatter_dimension=1, tiled=True)  34.6 us
    dynamic_slice x32, local copies, waits for them, and re-layouts, spread(): cols_here = lax.dynamic_slice_in_dim(cell_col[0], offset, step_rows)  22.7 us
  transfers between devices with their start and end apart: 8, of which 7 were waited for; matrix products, arithmetic and copies ran while one was open for 5% of the time, Pallas kernels for 0%

commit v1 on v0

v1 whole, which is shorter than its diff:
```python
import functools

import jax
import jax.numpy as jnp
import ml_dtypes
import numpy as np
from jax import lax
from jax.experimental import pallas as pl
from jax.experimental.pallas import tpu as pltpu
from jax.sharding import Mesh
from jax.sharding import PartitionSpec as P

GRID = 2048
HALF = GRID // 2
kick_gain = 2.0
block = 512
window = 256
cube = ("q", "tx", "lo", "dom")
vmem_limit = 48 * 1024 * 1024


def split_table(values):
    high = values.astype(ml_dtypes.bfloat16)
    low = (values - high.astype(np.float64)).astype(ml_dtypes.bfloat16)
    return (high, low)


@functools.lru_cache(maxsize=None)
def basis_tables():
    points = GRID + 1
    position = np.arange(HALF + 1)[:, None] + 1
    wave = np.arange(GRID)[None, :] + 1
    angles = np.pi * ((position * wave) % (2 * points)) / points
    scaling = np.sqrt(2.0 / points)
    sine = scaling * np.sin(angles)
    slope = -scaling * (np.pi * wave / points) * np.cos(angles)
    return (sine[:, 0::2], sine[:, 1::2], slope[:, 0::2], slope[:, 1::2])


def split(values):
    high = lax.reduce_precision(values, 8, 7)
    return (high.astype(jnp.bfloat16), (values - high).astype(jnp.bfloat16))


def dot(left, right, dims):
    return lax.dot_general(left, right, (dims, ((), ())), preferred_element_type=jnp.float32)


def table_left(table, values, contract):
    high, low = split(values)
    width = values.shape[1]
    both = dot(table[0], jnp.concatenate([high, low], 1), ((contract,), (0,)))
    return both[:, :width] + both[:, width:] + dot(table[1], high, ((contract,), (0,)))


def table_right(values, table, contract):
    high, low = split(values)
    rows = values.shape[0]
    both = dot(jnp.concatenate([high, low], 0), table[0], ((1,), (contract,)))
    return both[:rows] + both[rows:] + dot(high, table[1], ((1,), (contract,)))


def pair_weights(index, first, second, shape):
    rows = lax.broadcasted_iota(jnp.int32, shape, 0)
    return jnp.where(rows == index, first, jnp.where(rows == index + 1, second, 0.0))


def deposit_kernel(strips, halves, meta, scalars, weights, lists, charge):
    pad_cols = charge.shape[1]
    blocks = lists.shape[2] // block
    charge[...] = jnp.zeros_like(charge)

    def one_block(turn, carry):
        which = turn // blocks
        offset = pl.multiple_of((turn % blocks) * block, block)
        here = pl.ds(offset, block)
        half = jnp.where(which >= halves, 1, 0)
        start = meta[0, turn]

        def one_window(step, carry):
            at = pl.multiple_of(start + step * window, 128)
            row = lists[which, 0:1, here].astype(jnp.int32) - at
            col = lists[which, 1:2, here].astype(jnp.int32) - scalars[0]
            col = jnp.where((col >= 0) & (col < strips), col, -10)
            amount = lists[which, 2:3, here]
            near, far = (weights[which, 2] * amount, weights[which, 3] * amount)
            near_high = near.astype(jnp.bfloat16).astype(jnp.float32)
            far_high = far.astype(jnp.bfloat16).astype(jnp.float32)
            cols = jnp.concatenate(
                [
                    pair_weights(col, near_high, far_high, (pad_cols, block)),
                    pair_weights(col, near - near_high, far - far_high, (pad_cols, block)),
                ],
                0,
            ).astype(jnp.bfloat16)
            rows = pair_weights(row, weights[which, 0], weights[which, 1], (window, block)).astype(jnp.bfloat16)
            both = dot(cols, rows, ((1,), (1,)))
            charge[half, :, pl.ds(at, window)] += both[:pad_cols] + both[pad_cols:]
            return carry

        return lax.fori_loop(0, meta[1, turn], one_window, carry)

    lax.fori_loop(0, lists.shape[0] * blocks, one_block, 0)


def sample_kernel(strips, halves, meta, scalars, weights, lists, field_high, field_low, kicks):
    pad_cols = field_high.shape[1] // 2
    blocks = lists.shape[2] // block
    kicks[...] = jnp.zeros_like(kicks)

    def one_block(turn, carry):
        which = turn // blocks
        offset = pl.multiple_of((turn % blocks) * block, block)
        here = pl.ds(offset, block)
        half = jnp.where(which >= halves, 1, 0)
        start = meta[0, turn]

        def one_window(step, carry):
            at = pl.multiple_of(start + step * window, 128)
            row = lists[which, 0:1, here].astype(jnp.int32) - at
            col = lists[which, 1:2, here].astype(jnp.int32) - scalars[0]
            col = jnp.where((col >= 0) & (col < strips), col, -10)
            rows = pair_weights(row, weights[which, 0], weights[which, 1], (window, block)).astype(jnp.bfloat16)
            fields = jnp.concatenate(
                [field_high[half, :, pl.ds(at, window)], field_low[half, :, pl.ds(at, window)]], 1
            )
            near = dot(fields, jnp.concatenate([rows, rows], 0), ((1,), (0,)))
            cols = pair_weights(col, weights[which, 2], weights[which, 3], (pad_cols, block))
            kicks[which, 0:1, here] += jnp.sum(near[:pad_cols] * cols, axis=0, keepdims=True)
            kicks[which, 1:2, here] += jnp.sum(near[pad_cols:] * cols, axis=0, keepdims=True)
            return carry

        return lax.fori_loop(0, meta[1, turn], one_window, carry)

    lax.fori_loop(0, lists.shape[0] * blocks, one_block, 0)


def window_meta(row, col, strip_start, strips):
    shape = (row.shape[0], row.shape[1] // block, block)
    row, col = (row.reshape(shape), col.reshape(shape))
    inside = (col >= strip_start) & (col < strip_start + strips)
    least = jnp.min(jnp.where(inside, row, 2.0 * GRID), axis=2).astype(jnp.int32)
    most = jnp.max(jnp.where(inside, row, -1.0), axis=2).astype(jnp.int32)
    start = least // 128 * 128
    count = jnp.where(most < 0, 0, (most + 1 - start) // window + 1)
    return jnp.stack([jnp.where(most < 0, 0, start).reshape(-1), count.reshape(-1)])


def shards(cell_row, cell_col, weights, momenta):
    n_tx, n_lo, n_dom = (lax.axis_size(name) for name in ("tx", "lo", "dom"))
    tile_rows = GRID // n_tx
    tile_cols = HALF // n_lo
    lists = n_tx * n_dom
    strips = tile_cols // lists
    pad_cols = strips + 8
    devices = 2 * n_lo * lists
    modes = GRID // devices
    count = cell_row.shape[1]
    q, hi, lo, tx, dom = (lax.axis_index(name) for name in ("q", "hi", "lo", "tx", "dom"))

    row, col, amount = (cell_row[0], cell_col[0], weights[0])
    row = jnp.where(tx >= n_tx // 2, (n_tx - 1 - tx) * tile_rows + (tile_rows - 2) - row, tx * tile_rows + row)
    col = jnp.where(hi == 1, tile_cols - 2 - col, col)
    key = (col // strips * HALF + row) * strips + col % strips
    key, amount, order = lax.sort((key, amount, lax.iota(jnp.int32, count)), num_keys=1, is_stable=False)
    row = (key // strips) % HALF
    col = key // (strips * HALF) * strips + key % strips
    row, col = (row.astype(jnp.float32), col.astype(jnp.float32))

    own_route = [(b * 2 + t, t * 2 + b) for b in range(2) for t in range(2)]
    other_route = [(b * 2 + t, t * 2 + 1 - b) for b in range(2) for t in range(2)]
    back_route = [(there, here) for here, there in other_route]
    own = lax.ppermute(jnp.stack([row, col, amount]), ("q", "hi"), own_route)
    own = lax.all_gather(own, ("tx", "dom"), axis=0)
    other = lax.ppermute(jnp.stack([row, col]), ("q", "hi"), other_route)
    other = lax.all_gather(other, ("tx", "dom"), axis=0)

    strip_start = (tx * n_dom + dom) * strips
    flipped_rows = jnp.arange(lists)[:, None] // n_dom >= n_tx // 2
    row_pair = jnp.where(flipped_rows, jnp.array([[0.25, 0.75]]), jnp.array([[0.75, 0.25]]))
    col_pair = jnp.where(q == 1, jnp.array([[0.375, 0.625]]), jnp.array([[0.625, 0.375]]))
    pairs = jnp.concatenate([row_pair, jnp.broadcast_to(col_pair, (lists, 2))], 1).astype(jnp.float32)
    scalars = strip_start.astype(jnp.int32).reshape(1)
    smem, vmem = (pl.BlockSpec(memory_space=pltpu.SMEM), pl.BlockSpec(memory_space=pltpu.VMEM))
    params = pltpu.CompilerParams(vmem_limit_bytes=vmem_limit)

    own_meta = window_meta(own[:, 0], own[:, 1], strip_start.astype(jnp.float32), strips)
    charge = pl.pallas_call(
        functools.partial(deposit_kernel, strips, lists // 2),
        out_shape=jax.ShapeDtypeStruct((2, pad_cols, HALF + window), jnp.float32),
        in_specs=[smem, smem, smem, vmem],
        out_specs=vmem,
        compiler_params=params,
        name="deposit",
    )(own_meta, scalars, pairs, own)[:, :, :HALF]

    sine_even, sine_odd, slope_even, slope_odd = basis_tables()
    sine_e, sine_o, slope_e, slope_o = (
        tuple(jnp.asarray(part) for part in split_table(table[:HALF])) for table in basis_tables()
    )
    starts = np.array([b * tile_cols + (a * n_dom + c) * strips for a in range(n_tx) for b in range(n_lo) for c in range(n_dom)])
    offsets = np.arange(pad_cols)
    picked = np.where(offsets <= strips, starts[:, None] + offsets, 0).reshape(-1)
    used = np.broadcast_to(offsets <= strips, (len(starts), pad_cols)).reshape(-1, 1)
    strip_sine_e, strip_sine_o, strip_slope_e, strip_slope_o = (
        tuple(jnp.asarray(part) for part in split_table(table[picked] * used)) for table in basis_tables()
    )

    even = table_right(charge[0] + charge[1], sine_e, 0)
    odd = table_right(charge[0] - charge[1], sine_o, 0)
    by_mode = jnp.concatenate([even, odd], 1).reshape(pad_cols, devices, modes).transpose(1, 0, 2)
    by_mode = lax.all_to_all(by_mode, cube, 0, 0, tiled=True)

    def flip(part):
        return part.reshape(n_tx, n_lo, n_dom, pad_cols, modes)[:, ::-1].reshape(devices // 2, pad_cols, modes)

    near, far = (by_mode[: devices // 2], flip(by_mode[devices // 2 :]))
    folded = (devices // 2 * pad_cols, modes)
    spectrum_e = table_left(strip_sine_e, (near + far).reshape(folded), 0)
    spectrum_o = table_left(strip_sine_o, (near - far).reshape(folded), 0)
    angles = np.pi * (np.arange(GRID) + 1) / (2 * (GRID + 1))
    lam = (4.0 * np.sin(angles) ** 2).astype(np.float32)
    lam_e, lam_o = (lam[0::2], lam[1::2])
    lam_k = lax.dynamic_slice_in_dim(jnp.asarray(np.concatenate([lam_e, lam_o])), lax.axis_index(cube) * modes, modes)
    hat_e = spectrum_e * (1.0 / (lam_e[:, None] + lam_k[None, :]))
    hat_o = spectrum_o * (1.0 / (lam_o[:, None] + lam_k[None, :]))
    shape = (devices // 2, pad_cols, modes)
    along_e = table_left(strip_sine_e, hat_e, 1).reshape(shape)
    along_o = table_left(strip_sine_o, hat_o, 1).reshape(shape)
    across_e = table_left(strip_slope_e, hat_e, 1).reshape(shape)
    across_o = table_left(strip_slope_o, hat_o, 1).reshape(shape)
    halves = jnp.concatenate(
        [
            jnp.stack([along_e + along_o, across_e + across_o], 1),
            jnp.stack([flip(along_e - along_o), flip(across_o - across_e)], 1),
        ],
        0,
    )
    halves = lax.all_to_all(halves, cube, 0, 0, tiled=True)

    halves = halves.transpose(1, 2, 0, 3).reshape(2, pad_cols, GRID)
    x_e = table_right(halves[0, :, :HALF], slope_e, 1)
    x_o = table_right(halves[0, :, HALF:], slope_o, 1)
    y_e = table_right(halves[1, :, :HALF], sine_e, 1)
    y_o = table_right(halves[1, :, HALF:], sine_o, 1)
    field = jnp.stack([jnp.concatenate([x_e + x_o, y_e + y_o], 0), jnp.concatenate([x_o - x_e, y_e - y_o], 0)])
    field = jnp.pad(field, ((0, 0), (0, 0), (0, window)))
    field_high, field_low = split(field)

    other_meta = window_meta(other[:, 0], other[:, 1], strip_start.astype(jnp.float32), strips)
    kicks = pl.pallas_call(
        functools.partial(sample_kernel, strips, lists // 2),
        out_shape=jax.ShapeDtypeStruct((lists, 2, count), jnp.float32),
        in_specs=[smem, smem, smem, vmem, vmem, vmem],
        out_specs=vmem,
        compiler_params=params,
        name="sample",
    )(other_meta, scalars, pairs, other, field_high, field_low)
    kicks = jnp.sum(lax.all_to_all(kicks, ("tx", "dom"), 0, 0, tiled=True), axis=0)
    kicks = lax.ppermute(kicks, ("q", "hi"), back_route)
    _, kick_x, kick_y = lax.sort((order, kicks[0], kicks[1]), num_keys=1, is_stable=False)
    return momenta + kick_gain * jnp.stack([kick_x, kick_y])[None]


def solution(mesh):
    n_beam, n_tx, n_ty, n_dom = (mesh.shape[name] for name in ("beam", "tx", "ty", "dom"))
    split_mesh = Mesh(mesh.devices.reshape(n_beam, n_tx, 2, n_ty // 2, n_dom), ("q", "tx", "hi", "lo", "dom"))
    where = ("tx", "hi", "lo", "dom")
    placed = (P("q", where), P("q", where), P("q", where), P("q", None, where))
    return jax.shard_map(
        shards,
        mesh=split_mesh,
        in_specs=placed,
        out_specs=P("q", None, where),
        check_vma=False,
    )
```

time: 1110 us -> 217 us (0.20)
  matrix products: 653 us -> 24 us
  waiting for transfers between devices: 391 us -> 47.8 us
  blocking collectives: 0 us -> 40.1 us
  Pallas kernels: 0 us -> 33.2 us
  other arithmetic: 1.62 us -> 31 us
  starting transfers between devices: 0.32 us -> 17.5 us
  local copies, waits for them, and re-layouts: 36.5 us -> 21.1 us
  between operations: 13.8 us -> 0.6 us
    dot_general x54 -> x24, matrix products: 653 us -> 24 us  [dot(): lax.dot_general(left, right, (dims, ((), ())), preferred_element_type=jnp...]
    all_gather x6 -> x0, waiting for transfers between devices: 353 us -> none  [the longest x1 125 us: shards(): segment = lax.all_gather(row_done, ('ty', 'dom'), axis=1, tiled=True)]
    all_to_all x0 -> x2, waiting for transfers between devices: none -> 41.4 us  [the longest x1 26.6 us: shards(): halves = lax.all_to_all(halves, cube, 0, 0, tiled=True)]
    reduce_scatter x1 -> x0, waiting for transfers between devices: 34.6 us -> none  [shards(): lax.psum_scatter(tile_charge, 'dom', scatter_dimension=1, tiled=True)]
    pallas_call x0 -> x2, Pallas kernels: none -> 33.2 us  [the longest x1 16.6 us: shards(): pl.pallas_call(functools.partial(sample_kernel, strips, lists // 2), out_...]
    dynamic_slice x48 -> x1, local copies, waits for them, and re-layouts: 33.7 us -> 0.77 us  [shards(): lax.dynamic_slice_in_dim(jnp.asarray(np.concatenate([lam_e, lam_o])), lax...]
    all_gather x0 -> x2, blocking collectives: none -> 24.5 us  [the longest x1 13.2 us: shards(): own = lax.all_gather(own, ('tx', 'dom'), axis=0)]
    all_to_all x0 -> x1, blocking collectives: none -> 15.6 us  [shards(): lax.all_to_all(kicks, ('tx', 'dom'), 0, 0, tiled=True)]
  transfers between devices with their start and end apart: 8 -> 5, of which waited for: 7 -> 4; matrix products, arithmetic and copies ran while one was open for 5% -> 1% of each run, Pallas kernels for 0% -> 0%
where the time goes in v1:
time: 217 us; the launch traced here: 215 us
  waiting for transfers between devices  47.8 us (22%)
  blocking collectives  40.1 us (18%)
  Pallas kernels  33.2 us (15%)
  other arithmetic  31 us (14%)
  matrix products  24 us (11%)
  local copies, waits for them, and re-layouts  21.1 us (10%)
  starting transfers between devices  17.5 us (8%)
    all_to_all x1, waiting for transfers between devices, shards(): halves = lax.all_to_all(halves, cube, 0, 0, tiled=True)  26.6 us
    dot_general x24, matrix products, dot(): lax.dot_general(left, right, (dims, ((), ())), preferred_element_type=jnp...  24 us
    pallas_call x1, Pallas kernels, shards(): pl.pallas_call(functools.partial(sample_kernel, strips, lists // 2), out_...  16.6 us
    pallas_call x1, Pallas kernels, shards(): pl.pallas_call(functools.partial(deposit_kernel, strips, lists // 2), out...  16.5 us
    all_to_all x1, blocking collectives, shards(): lax.all_to_all(kicks, ('tx', 'dom'), 0, 0, tiled=True)  15.6 us
    all_to_all x1, waiting for transfers between devices, shards(): by_mode = lax.all_to_all(by_mode, cube, 0, 0, tiled=True)  14.8 us
    all_gather x1, blocking collectives, shards(): own = lax.all_gather(own, ('tx', 'dom'), axis=0)  13.2 us
    all_gather x1, blocking collectives, shards(): other = lax.all_gather(other, ('tx', 'dom'), axis=0)  11.3 us
  transfers between devices with their start and end apart: 5, of which 4 were waited for; matrix products, arithmetic and copies ran while one was open for 1% of the time, Pallas kernels for 0%

profile of v1, /device:TPU:0, one launch (start us, length us, event | category | flops | bytes accessed | tf_op | source)
XLA Modules:
  0.0 215.3 jit_solution(6994380995319885499)
XLA Ops:
  0.0 0.9 broadcast_select_fusion
  0.9 0.9 fusion.47
  1.8 7.5 %sort.42 = (s32[16384]{0:T(1024)S(1)}, f32[16384]{0:T(1024)S(1)}, s32[16384]{0:T(1024)S(1)}) sort(s32[16384]{0:T(1024)S(1)} %fusion.47, f32[16384]{0:T(1024)} %bitcast.151, s32[16384]{0:T(1024)S(1)} %iota.8), dimensions={0}, to_apply=%region_0.1 | sort | flops 229376 | bytes 393216 | tf_op jit(solution)/shard_map/sort | solution.py:165
  9.6 4.1 %collective-permute-start = (f32[2,16384]{1,0:T(2,128)S(1)}, f32[2,16384]{1,0:T(2,128)S(1)}, u32[]{:S(2)}, u32[]{:S(2)}) collective-permute-start(f32[2,16384]{1,0:T(2,128)S(1)} %pad_maximum_fusion.11), channel_id=1, source_target_pairs={{0,4},{4,20},{16,0},{20,16},{1,5},{5,21},{17,1},{21,17},{2,6},{6,2... | collective-permute-start | bytes 393224 | tf_op jit(solution)/shard_map/ppermute | solution.py:175
  16.2 11.3 %all-gather.2.lists = f32[4,2,16384]{2,1,0:T(2,128)S(1)} all-gather(f32[1,2,16384]{2,1,0:T(2,128)S(1)} %bitcast.149), channel_id=2, replica_groups=mesh['q'=2,'tx'=2,'hi'=2,'lo'=2,'dom'=2] {'tx','dom'}, dimensions={0}, use_global_device_ids=true | all-gather | bytes 655360 | tf_op jit(solution)/shard_map/all_gather | solution.py:176
  27.6 13.2 %all-gather.3.lists = f32[4,3,16384]{2,1,0:T(4,128)S(1)} all-gather(f32[1,3,16384]{2,1,0:T(4,128)S(1)} %bitcast.145), channel_id=3, replica_groups=mesh['q'=2,'tx'=2,'hi'=2,'lo'=2,'dom'=2] {'tx','dom'}, dimensions={0}, use_global_device_ids=true | all-gather | bytes 983040 | tf_op jit(solution)/shard_map/all_gather | solution.py:174
  40.7 4.0 %select_reduce_fusion = (f32[4,16384]{1,0:T(4,128)S(1)}, f32[4,16384]{1,0:T(4,128)S(1)}, f32[4,16384]{1,0:T(4,128)}, f32[4,16384]{1,0:T(4,128)}) fusion(f32[4,3,16384]{2,1,0:T(4,128)S(1)} %all-gather.3.lists, f32[]{:T(128)S(6)} %add.303, f32[]{:T(128)S(6)} %convert_element_type.148, f32[4,2,16384]{2,1,0:T(2,128)S(1)} %all-gather.2.lists), kind=kLoop, calls=%fused_computation.116 | loop fusion | flops 655360 | bytes 2097160 | tf_op jit(solution)/shard_map/jit(_where)/select_n | solution.py:142
  45.4 16.5 %deposit.1 = f32[2,136,1280]{2,1,0:T(8,128)S(1)} custom-call(s32[2,128]{1,0:T(2,128)S(1)} %pad_add_fusion.1.meta, s32[1]{0:T(128)} %bitcast.6.scalars, f32[4,4]{1,0:T(4,128)S(1)} %pad_maximum_fusion.12.weights, f32[4,3,16384]{2,1,0:T(4,128)S(1)} %all-gather.3.lists), custom_call_target="tpu_custom_call" | custom-call | tf_op jit(solution)/shard_map/deposit/pallas_call | solution.py:188
  64.3 1.1 copy-done.11
  67.5 1.1 bitcast_bitcast_fusion
  68.5 7.5 %all-to-all-start = ((f32[16,136,128]{2,1,0:T(8,128)}), f32[16,136,128]{2,1,0:T(8,128)}, u32[]{:S(2)}, u32[]{:S(2)}) async-start(f32[16,136,128]{2,1,0:T(8,128)} %bitcast_bitcast_fusion), calls=%async_computation | async-start | bytes 2228224 | tf_op jit(solution)/shard_map/all_to_all | solution.py:212
  76.9 14.8 %all-to-all-done = f32[16,136,128]{2,1,0:T(8,128)} async-done(((f32[16,136,128]{2,1,0:T(8,128)}), f32[16,136,128]{2,1,0:T(8,128)}, u32[]{:S(2)}, u32[]{:S(2)}) %all-to-all-start) | async-done | bytes 1114144 | tf_op jit(solution)/shard_map/all_to_all | solution.py:212
  91.6 1.9 slice.168
  93.6 1.1 rev.9
  94.7 1.3 bitcast_add_fusion
  96.5 0.9 fusion.36
  98.7 1.8 fusion.42
  104.4 1.8 fusion.40
  109.4 1.6 fusion.83
  111.0 1.9 rev.11
  112.9 2.9 %convolution_add_fusion.2 = f32[1088,128]{1,0:T(8,128)S(1)} fusion(bf16[1088,1024]{1,0:T(8,128)(2,1)} %constant.223.clone, bf16[1024,128]{0,1:T(8,128)(2,1)} %copy-done.16, f32[1088,256]{1,0:T(8,128)} %fusion.40), kind=kOutput, calls=%fused_computation.7 | convolution fusion | flops 285491200 | bytes 4161536 | tf_op jit(solution)/shard_map/dot_general | solution.py:46
  115.9 1.8 fusion.82
  117.6 1.9 rev.10
  119.5 2.9 %maximum_maximum_fusion = f32[16,2,136,128]{3,2,1,0:T(8,128)} fusion(f32[8,1,136,128]{3,2,1,0:T(8,128)} %bitcast.132, f32[8,1,136,128]{3,2,1,0:T(8,128)} %bitcast.134, f32[8,1,136,128]{3,2,1,0:T(8,128)S(1)} %bitcast.130, f32[8,1,136,128]{3,2,1,0:T(8,128)} %bitcast.131), kind=kLoop, calls=%fused_computation.10 | loop fusion | flops 1671168 | bytes 4456448 | tf_op jit(solution)/shard_map/concatenate | solution.py:232
  122.5 4.8 %all-to-all-start.1 = ((f32[16,2,136,128]{3,2,1,0:T(8,128)}), f32[16,2,136,128]{3,2,1,0:T(8,128)}, u32[]{:S(2)}, u32[]{:S(2)}) async-start(f32[16,2,136,128]{3,2,1,0:T(8,128)} %maximum_maximum_fusion), calls=%async_computation.1 | async-start | bytes 4456448 | tf_op jit(solution)/shard_map/all_to_all | solution.py:239
  128.0 26.6 %all-to-all-done.1 = f32[16,2,136,128]{3,2,1,0:T(8,128)} async-done(((f32[16,2,136,128]{3,2,1,0:T(8,128)}), f32[16,2,136,128]{3,2,1,0:T(8,128)}, u32[]{:S(2)}, u32[]{:S(2)}) %all-to-all-start.1) | async-done | bytes 2228256 | tf_op jit(solution)/shard_map/all_to_all | solution.py:239
  154.6 1.9 copy_bitcast_fusion
  156.9 1.1 copy-done.12
  167.9 16.6 %sample.1 = f32[4,2,16384]{2,1,0:T(2,128)S(1)} custom-call(s32[2,128]{1,0:T(2,128)S(1)} %pad_add_fusion.meta, s32[1]{0:T(128)} %bitcast.6.scalars, f32[4,4]{1,0:T(4,128)S(1)} %pad_maximum_fusion.12.weights, f32[4,2,16384]{2,1,0:T(2,128)S(1)} %all-gather.2.lists, bf16[2,272,1280]{2,1,0:T(8,128)(2,1)S(1)} %get-tuple-element.24.field_high, ...), custom_call_target="tpu_custom_call" | custom-call | tf_op jit(solution)/shard_map/sample/pallas_call | solution.py:251
  184.6 15.6 %all_to_all.15 = f32[4,2,16384]{2,1,0:T(2,128)S(1)} all-to-all(f32[4,2,16384]{2,1,0:T(2,128)S(1)} %sample.1), channel_id=1, replica_groups=mesh['q'=2,'tx'=2,'hi'=2,'lo'=2,'dom'=2] {'tx','dom'}, dimensions={0} | all-to-all | bytes 1048576 | tf_op jit(solution)/shard_map/all_to_all | solution.py:259
  200.8 6.3 %collective-permute-done.2 = f32[2,16384]{1,0:T(2,128)S(1)} collective-permute-done((f32[2,16384]{1,0:T(2,128)S(1)}, f32[2,16384]{1,0:T(2,128)S(1)}, u32[]{:S(2)}, u32[]{:S(2)}) %collective-permute-start.2) | collective-permute-done | bytes 131104 | tf_op jit(solution)/shard_map/ppermute | solution.py:260
  207.2 7.3 %sort.43 = (s32[16384]{0:T(1024)}, f32[16384]{0:T(1024)S(1)}, f32[16384]{0:T(1024)S(1)}) sort(s32[16384]{0:T(1024)S(1)} %get-tuple-element.10, f32[16384]{0:T(1024)S(1)} %bitcast.148, f32[16384]{0:T(1024)S(1)} %bitcast.147), dimensions={0}, to_apply=%region_6.7 | sort | flops 229376 | bytes 393216 | tf_op jit(solution)/shard_map/sort | solution.py:261
  (116 shorter events, 29.8 us)
Async XLA Ops:
  9.6 6.6 %collective-permute-start = (f32[2,16384]{1,0:T(2,128)S(1)}, f32[2,16384]{1,0:T(2,128)S(1)}, u32[]{:S(2)}, u32[]{:S(2)}) collective-permute-start(f32[2,16384]{1,0:T(2,128)S(1)} %pad_maximum_fusion.11), channel_id=1, source_target_pairs={{0,4},{4,20},{16,0},{20,16},{1,5},{5,21},{17,1},{21,17},{2,6},{6,2... | collective-permute-start | bytes 393224 | tf_op jit(solution)/shard_map/ppermute | solution.py:175
  13.9 13.7 %collective-permute-start.1 = (f32[3,16384]{1,0:T(4,128)S(1)}, f32[3,16384]{1,0:T(4,128)S(1)}, u32[]{:S(2)}, u32[]{:S(2)}) collective-permute-start(f32[3,16384]{1,0:T(4,128)S(1)} %pad_maximum_fusion.10), channel_id=1, source_target_pairs={{0,0},{4,16},{16,4},{20,20},{1,1},{5,17},{17,5},{21,21},{2,2},{6,1... | collective-permute-start | bytes 589832 | tf_op jit(solution)/shard_map/ppermute | solution.py:173
  45.4 16.8 %copy-start.8 = (bf16[1024,1024]{1,0:T(8,128)(2,1)S(1)}, bf16[1024,1024]{1,0:T(8,128)(2,1)}, u32[]{:S(2)}) copy-start(bf16[1024,1024]{1,0:T(8,128)(2,1)} %constant.212.clone) | copy-start | bytes 6291460
  62.2 1.6 copy-start
  63.8 1.6 copy-start.11
  65.4 1.6 copy-start.1
  68.5 23.1 %all-to-all-start = ((f32[16,136,128]{2,1,0:T(8,128)}), f32[16,136,128]{2,1,0:T(8,128)}, u32[]{:S(2)}, u32[]{:S(2)}) async-start(f32[16,136,128]{2,1,0:T(8,128)} %bitcast_bitcast_fusion), calls=%async_computation | async-start | bytes 2228224 | tf_op jit(solution)/shard_map/all_to_all | solution.py:212
  94.7 1.8 copy-start.23
  96.5 1.6 copy-start.5
  96.5 1.6 copy-start.26
  98.7 1.8 copy-start.24
  100.5 1.6 copy-start.21
  102.1 1.6 copy-start.3
  102.1 1.6 copy-start.25
  104.4 2.6 %copy-start.16 = (bf16[1024,128]{0,1:T(8,128)(2,1)}, bf16[1024,128]{0,1:T(8,128)(2,1)S(1)}, u32[]{:S(2)}) copy-start(bf16[1024,128]{0,1:T(8,128)(2,1)S(1)} %get-tuple-element.54) | copy-start | bytes 786436
  104.4 1.8 copy-start.22
  106.2 1.6 copy-start.4
  107.8 1.6 copy-start.7
  112.9 2.9 %copy-start.6 = (bf16[1088,1024]{1,0:T(8,128)(2,1)S(1)}, bf16[1088,1024]{1,0:T(8,128)(2,1)}, u32[]{:S(2)}) copy-start(bf16[1088,1024]{1,0:T(8,128)(2,1)} %constant.221.clone) | copy-start | bytes 6684676
  112.9 3.0 %copy-start.19 = (f32[1088,256]{1,0:T(8,128)S(1)}, f32[1088,256]{1,0:T(8,128)}, u32[]{:S(2)}) copy-start(f32[1088,256]{1,0:T(8,128)} %fusion.42) | copy-start | bytes 3342340
  122.5 4.8 %copy-start.18 = (f32[4,16384]{1,0:T(4,128)S(1)}, f32[4,16384]{1,0:T(4,128)}, u32[]{:S(2)}) copy-start(f32[4,16384]{1,0:T(4,128)} %get-tuple-element.63) | copy-start | bytes 786436
  122.5 5.2 %copy-start.17 = (f32[4,16384]{1,0:T(4,128)S(1)}, f32[4,16384]{1,0:T(4,128)}, u32[]{:S(2)}) copy-start(f32[4,16384]{1,0:T(4,128)} %get-tuple-element.64) | copy-start | bytes 786436
  122.5 32.1 %all-to-all-start.1 = ((f32[16,2,136,128]{3,2,1,0:T(8,128)}), f32[16,2,136,128]{3,2,1,0:T(8,128)}, u32[]{:S(2)}, u32[]{:S(2)}) async-start(f32[16,2,136,128]{3,2,1,0:T(8,128)} %maximum_maximum_fusion), calls=%async_computation.1 | async-start | bytes 4456448 | tf_op jit(solution)/shard_map/all_to_all | solution.py:239
  156.5 1.6 copy-start.12
  156.9 1.9 copy-start.2
  158.8 1.6 copy-start.9
  161.2 1.6 copy-start.13
  162.1 1.8 copy-start.15
  163.9 1.6 copy-start.10
  164.7 1.8 copy-start.14
  167.9 46.6 %copy-start.20 = (f32[1,2,16384]{2,1,0:T(2,128)S(1)}, f32[1,2,16384]{2,1,0:T(2,128)}, u32[]{:S(2)}) copy-start(f32[1,2,16384]{2,1,0:T(2,128)} %param.30) | copy-start | bytes 393220
  200.4 6.7 %collective-permute-start.2 = (f32[2,16384]{1,0:T(2,128)S(1)}, f32[2,16384]{1,0:T(2,128)S(1)}, u32[]{:S(2)}, u32[]{:S(2)}) collective-permute-start(f32[2,16384]{1,0:T(2,128)S(1)} %reduce_sum.9), channel_id=1, source_target_pairs={{4,0},{20,4},{0,16},{16,20},{5,1},{21,5},{1,17},{17,21},{6,2},{22,... | collective-permute-start | bytes 393224 | tf_op jit(solution)/shard_map/ppermute | solution.py:260

commit v2 on v1

v2 whole, which is shorter than its diff:
```python
import functools

import jax
import jax.numpy as jnp
import ml_dtypes
import numpy as np
from jax import lax
from jax.experimental import pallas as pl
from jax.experimental.pallas import tpu as pltpu
from jax.sharding import Mesh
from jax.sharding import PartitionSpec as P

GRID = 2048
HALF = GRID // 2
kick_gain = 2.0
block = 512
window = 256
pieces = 4
piece_rows = HALF // pieces
cube = ("q", "tx", "lo", "dom")
vmem_limit = 48 * 1024 * 1024


def split_table(values):
    high = values.astype(ml_dtypes.bfloat16)
    low = (values - high.astype(np.float64)).astype(ml_dtypes.bfloat16)
    return (high, low)


@functools.lru_cache(maxsize=None)
def basis_tables():
    points = GRID + 1
    position = np.arange(HALF)[:, None] + 1
    wave = np.arange(GRID)[None, :] + 1
    angles = np.pi * ((position * wave) % (2 * points)) / points
    scaling = np.sqrt(2.0 / points)
    sine = scaling * np.sin(angles)
    slope = -scaling * (np.pi * wave / points) * np.cos(angles)
    return (sine[:, 0::2], sine[:, 1::2], slope[:, 0::2], slope[:, 1::2])


def split(values):
    high = lax.reduce_precision(values, 8, 7)
    return (high.astype(jnp.bfloat16), (values - high).astype(jnp.bfloat16))


def dot(left, right, dims):
    return lax.dot_general(left, right, (dims, ((), ())), preferred_element_type=jnp.float32)


def table_left(table, values, contract):
    high, low = split(values)
    width = values.shape[1]
    both = dot(table[0], jnp.concatenate([high, low], 1), ((contract,), (0,)))
    return both[:, :width] + both[:, width:] + dot(table[1], high, ((contract,), (0,)))


def table_right(values, table, contract):
    high, low = split(values)
    rows = values.shape[0]
    both = dot(jnp.concatenate([high, low], 0), table[0], ((1,), (contract,)))
    return both[:rows] + both[rows:] + dot(high, table[1], ((1,), (contract,)))


def pair_weights(index, first, second, rows):
    shape = (rows, index.shape[1])
    at = lax.broadcasted_iota(jnp.int32, shape, 0).astype(jnp.float32).astype(index.dtype)
    one, zero = (jnp.ones((), index.dtype), jnp.zeros((), first.dtype))
    return jnp.where(at == index, first, jnp.where(at == index + one, second, zero))


def short(values):
    return values.astype(jnp.float32).astype(jnp.bfloat16)


def dot_parts(table_high, table_low, values, dims):
    high = values.astype(jnp.bfloat16).astype(jnp.float32)
    rows = values.shape[0]
    both = dot(jnp.concatenate([high, values - high], 0).astype(jnp.bfloat16), table_high, dims)
    return both[:rows] + both[rows:] + dot(high.astype(jnp.bfloat16), table_low, dims)


def windows(strips, start, first, last, which, turn):
    first_row, first_col = (first[which, 0, turn], first[which, 1, turn])
    last_row, last_col = (last[which, 0, turn], last[which, 1, turn])
    least = jnp.where(first_col >= start, first_row, 0) // 128 * 128
    most = jnp.where(last_col < start + strips, last_row, HALF - 2)
    return (least, (most + 1 - least) // window + 1)


def each_window(strips, scalars, first, last, group, item):
    start = scalars[0]

    def bounds(turn, found):
        return tuple(
            (
                low + jnp.where(last[which, 1, turn] < start, 1, 0),
                high + jnp.where(first[which, 1, turn] < start + strips, 1, 0),
            )
            for which, (low, high) in zip(group, found, strict=True)
        )

    found = lax.fori_loop(0, first.shape[2], bounds, tuple((0, 0) for _ in group))
    turns = functools.reduce(jnp.maximum, [high - low for low, high in found])

    def one_turn(step, carry):
        more = []
        for place, (which, (low, high)) in enumerate(zip(group, found, strict=True)):
            valid = low + step < high
            turn = jnp.minimum(low + step, first.shape[2] - 1)
            at, count = windows(strips, start, first, last, which, turn)
            item(place, which, turn, pl.multiple_of(at, 128), valid)
            more.append((place, which, turn, at, jnp.where(valid, count, 0)))
        for place, which, turn, at, count in more:

            def one_window(extra, carry, place=place, which=which, turn=turn, at=at):
                item(place, which, turn, pl.multiple_of(at + extra * window, 128), True)
                return carry

            lax.fori_loop(1, count, one_window, 0)
        return carry

    lax.fori_loop(0, turns, one_turn, 0)


def cells_of(strips, scalars, lists, which, here, at, valid):
    row = lists[which, 0:1, here].astype(jnp.int32) - at
    row = jnp.where((row >= -1) & (row < window) & valid, row, -10)
    col = lists[which, 1:2, here].astype(jnp.int32) - scalars[0]
    col = jnp.where((col >= 0) & (col < strips), col, -10)
    return (row, col)


def groups_of(count):
    return [tuple(range(first, min(first + 4, count))) for first in range(0, count, 4)]


def deposit_body(strips, scalars, first, last, weights, lists, charge, parts):
    pad_cols = charge.shape[1]
    tall = -(-pad_cols // 16) * 16
    count = lists.shape[0]
    for part in parts:
        part[...] = jnp.zeros_like(part)

    def half_of(which):
        return which // (count // 2)

    def item(place, which, turn, at, valid):
        here = pl.ds(pl.multiple_of(turn * block, block), block)
        row, col = cells_of(strips, scalars, lists, which, here, at, valid)
        amount = lists[which, 2:3, here]
        near, far = (weights[which, 2] * amount, weights[which, 3] * amount)
        near_high, far_high = (near.astype(jnp.bfloat16), far.astype(jnp.bfloat16))
        near_low = (near - near_high.astype(jnp.float32)).astype(jnp.bfloat16)
        far_low = (far - far_high.astype(jnp.float32)).astype(jnp.bfloat16)
        col = short(col)
        cols = jnp.concatenate(
            [pair_weights(col, near_high, far_high, tall), pair_weights(col, near_low, far_low, tall)], 0
        )
        rows = pair_weights(short(row), short(weights[which, 0]), short(weights[which, 1]), window)
        both = dot(cols, rows, ((1,), (1,)))
        half = half_of(which) if count > 4 else 0
        parts[place][half, :, pl.ds(at, window)] += both[:pad_cols] + both[tall : tall + pad_cols]

    for group in groups_of(count):
        each_window(strips, scalars, first, last, group, item)
    for half in range(2):
        if count > 4:
            used = [part[half] for part in parts]
        else:
            used = [part[0] for which, part in enumerate(parts) if half_of(which) == half]
        charge[half] = functools.reduce(jnp.add, used)


def deposit_parts(count, charge_shape):
    return [pltpu.VMEM((2 if count > 4 else 1, *charge_shape[1:]), jnp.float32)] * min(count, 4)


def sample_body(strips, scalars, first, last, weights, lists, field_high, field_low, kicks, begin):
    pad_cols = field_high.shape[1] // 2
    for kick in kicks:
        kick[...] = jnp.zeros_like(kick)

    def item(place, which, turn, at, valid):
        here = pl.ds(pl.multiple_of(turn * block, block), block)
        half = scalars[1 + which]
        kick = kicks[which - begin]
        row, col = cells_of(strips, scalars, lists, which, here, at, valid)
        rows = pair_weights(short(row), short(weights[which, 0]), short(weights[which, 1]), window)
        fields = jnp.concatenate([field_high[half, :, pl.ds(at, window)], field_low[half, :, pl.ds(at, window)]], 1)
        near = dot(fields, jnp.concatenate([rows, rows], 0), ((1,), (0,)))
        cols = pair_weights(col.astype(jnp.float32), weights[which, 2], weights[which, 3], pad_cols)
        kick[0:1, here] += jnp.sum(near[:pad_cols] * cols, axis=0, keepdims=True)
        kick[1:2, here] += jnp.sum(near[pad_cols:] * cols, axis=0, keepdims=True)

    for group in groups_of(len(kicks)):
        group = tuple(begin + which for which in group)
        each_window(strips, scalars, first, last, group, item)


def fetch(stored, tables, arrived, order):
    copies = {}
    for number, (part, piece) in enumerate(order):
        rows = pl.ds(piece * piece_rows, piece_rows)
        copies[part, piece] = pltpu.make_async_copy(stored.at[part, rows], tables.at[part, rows], arrived.at[number])
        copies[part, piece].start()

    def table(part, piece):
        copies[part, piece].wait()
        return tables[part, piece * piece_rows : (piece + 1) * piece_rows]

    return table


def modes_kernel(strips, scalars, first, last, weights, lists, stored, by_mode, charge, tables, arrived, *parts):
    table = fetch(stored, tables, arrived, [(part, piece) for part in range(4) for piece in range(pieces)])
    deposit_body(strips, scalars, first, last, weights, lists, charge, parts)
    devices, _, modes = by_mode.shape
    near, far = (charge[0, :, :HALF], charge[1, :, :HALF])
    for parity, part in enumerate((near + far, near - far)):
        high, low = (jnp.concatenate([table(2 * parity + i, piece) for piece in range(pieces)], 0) for i in range(2))
        done = dot_parts(high, low, part, ((1,), (0,)))
        for turn in range(devices // 2):
            by_mode[parity * (devices // 2) + turn] = done[:, turn * modes : (turn + 1) * modes]


def columns_kernel(order, flipped, per_tile, strips, by_mode, lam, lam_mine, stored, halves, tables, arrived, back_x, back_y, sent):
    forward = [(2 * parity + i, piece) for parity in range(2) for piece in range(pieces) for i in range(2)]
    backward = [(part, piece) for piece in range(pieces) for part in range(4, 8)]
    table = fetch(stored, tables, arrived, forward + backward)
    modes = by_mode.shape[2]
    near, far = ([], [])
    for place in range(len(order)):
        pair = []
        for here, before in ((order, 0), (flipped, len(order))):
            body = by_mode[before + here[place], :strips]
            if place % per_tile:
                halo = by_mode[before + here[place - 1], strips:]
                body = jnp.concatenate([body[:8] + halo, body[8:]], 0)
            pair.append(body)
        near.append(pair[0] + pair[1])
        far.append(pair[0] - pair[1])
    hats = []
    for parity, part in enumerate((near, far)):
        part = jnp.concatenate(part, 0).T
        spectrum = 0.0
        for piece in range(pieces):
            high, low = (table(2 * parity + i, piece) for i in range(2))
            spectrum += dot_parts(high, low, part[:, piece * piece_rows : (piece + 1) * piece_rows], ((1,), (0,)))
        hat = (spectrum * (1.0 / (lam[parity : parity + 1, :] + lam_mine[...]))).T
        high = hat.astype(jnp.bfloat16)
        hats.append((high, jnp.concatenate([high, (hat - high.astype(jnp.float32)).astype(jnp.bfloat16)], 1)))

    def back(table_high, table_low, parity):
        high, both = hats[parity]
        done = dot(table_high, both, ((1,), (0,)))
        return done[:, :modes] + done[:, modes:] + dot(table_low, high, ((1,), (0,)))

    copies = []
    for component, (outgoing, sign) in enumerate(((back_x, 1), (back_y, -1))):
        for piece in range(pieces):
            if component == 0:
                rows = slice(piece * piece_rows, (piece + 1) * piece_rows)
                parts = [tables[i, rows] for i in range(4)]
            else:
                parts = [table(4 + i, piece) for i in range(4)]
            even, odd = (back(parts[0], parts[1], 0), back(parts[2], parts[3], 1))
            for before, whose, value in (
                (0, order, even + odd),
                (len(order), flipped, even - odd if sign == 1 else odd - even),
            ):
                for turn in range(piece_rows // strips):
                    place = piece * piece_rows // strips + turn
                    mine = value[turn * strips : (turn + 1) * strips]
                    outgoing[before + whose[place], :strips] = mine
                    if place % per_tile:
                        outgoing[before + whose[place - 1], strips:] = mine[:8]
                    if place % per_tile == per_tile - 1:
                        outgoing[before + whose[place], strips:] = jnp.zeros_like(mine[:8])
        copies.append(pltpu.make_async_copy(outgoing, halves.at[:, component], sent.at[component]))
        copies[-1].start()
    for copy in copies:
        copy.wait()


def kicks_kernel(strips, scalars, first, last, weights, lists, halves, stored, *refs):
    kicks, (field_high, field_low, tables, arrived) = (refs[:-4], refs[-4:])
    order = [(part, piece) for parts in ((4, 5, 6, 7), (0, 1, 2, 3)) for piece in range(pieces) for part in parts]
    table = fetch(stored, tables, arrived, order)
    devices, _, pad_cols, _ = halves.shape
    wide = 2 * pad_cols
    fields = {}
    for component, (which, sign) in enumerate(((4, -1), (0, 1))):
        sides = []
        for start in (0, devices // 2):
            part = jnp.concatenate([halves[start + turn, component] for turn in range(devices // 2)], 1)
            high = part.astype(jnp.bfloat16)
            low = part - high.astype(jnp.float32)
            sides.append((jnp.concatenate([high.astype(jnp.float32), low], 0).astype(jnp.bfloat16), high))
        for piece in range(pieces):
            pair = []
            for parity, (both, high) in enumerate(sides):
                table_high, table_low = (table(which + 2 * parity + i, piece) for i in range(2))
                done = dot(both, table_high, ((1,), (1,)))
                pair.append(done[:pad_cols] + done[pad_cols:] + dot(high, table_low, ((1,), (1,))))
            even, odd = pair
            fields[component, piece] = (even + odd, even - odd if sign == 1 else odd - even)
    for half in range(2):
        for piece in range(pieces):
            here = slice(piece * piece_rows, (piece + 1) * piece_rows)
            value = jnp.concatenate([fields[component, piece][half] for component in range(2)], 0)
            high = value.astype(jnp.bfloat16)
            field_high[half, :, here] = high
            field_low[half, :, here] = (value - high.astype(jnp.float32)).astype(jnp.bfloat16)
        beyond = jnp.zeros((wide, window), jnp.bfloat16)
        field_high[half, :, HALF:] = beyond
        field_low[half, :, HALF:] = beyond
    sample_body(strips, scalars, first, last, weights, lists, field_high, field_low, kicks, 0)


def block_ends(lists):
    ends = (lists[:, :2, 0::block], lists[:, :2, block - 1 :: block])
    return tuple(end.astype(jnp.int32) for end in ends)


def deposit_alone(strips, scalars, first, last, weights, lists, charge, *parts):
    deposit_body(strips, scalars, first, last, weights, lists, charge, parts)


def sample_alone(strips, begin, scalars, first, last, weights, lists, field_high, field_low, *kicks):
    sample_body(strips, scalars, first, last, weights, lists, field_high, field_low, kicks, begin)


def shifted(n_tx, n_dom, shift):
    return [
        ((a + shift[0]) % n_tx * n_dom + (c + shift[1]) % n_dom, a * n_dom + c) for a in range(n_tx) for c in range(n_dom)
    ]


def returned(route, n_tx, n_dom, shift):
    pairs = []
    for there, here in route:
        for a in range(n_tx):
            for c in range(n_dom):
                target = ((there // 2 * n_tx + (a + shift[0]) % n_tx) * 2 + there % 2) * n_dom + (c + shift[1]) % n_dom
                pairs.append((((here // 2 * n_tx + a) * 2 + here % 2) * n_dom + c, target))
    return pairs


def general(to_deposit, to_sample, tables, lam_e, lam_o, lam_k, sizes, charge_shape, kick_shape):
    n_tx, n_lo, n_dom = sizes
    devices = 2 * n_tx * n_lo * n_dom
    modes = GRID // devices
    tile_cols = HALF // n_lo
    strips = tile_cols // (n_tx * n_dom)
    pad_cols = charge_shape[1]
    smem, vmem = (pl.BlockSpec(memory_space=pltpu.SMEM), pl.BlockSpec(memory_space=pltpu.VMEM))
    params = pltpu.CompilerParams(vmem_limit_bytes=vmem_limit)
    sine_e, sine_o, slope_e, slope_o = tables
    starts = np.array([b * tile_cols + (a * n_dom + c) * strips for a in range(n_tx) for b in range(n_lo) for c in range(n_dom)])
    offsets = np.arange(pad_cols)
    columns = starts[:, None] + offsets
    kept = (offsets <= strips) & (columns < HALF)
    picked = np.where(kept, columns, 0).reshape(-1)
    used = kept.reshape(-1, 1)
    strip_sine_e, strip_sine_o, strip_slope_e, strip_slope_o = (
        tuple(jnp.asarray(part) for part in split_table(table[picked] * used)) for table in basis_tables()
    )

    charge = pl.pallas_call(
        functools.partial(deposit_alone, strips),
        out_shape=jax.ShapeDtypeStruct(charge_shape, jnp.float32),
        in_specs=[smem] * 4 + [vmem],
        out_specs=vmem,
        scratch_shapes=deposit_parts(n_tx * n_dom, charge_shape),
        compiler_params=params,
        name="deposit",
    )(*to_deposit)[:, :, :HALF]

    even = table_right(charge[0] + charge[1], sine_e, 0)
    odd = table_right(charge[0] - charge[1], sine_o, 0)
    by_mode = jnp.concatenate([even, odd], 1).reshape(pad_cols, devices, modes).transpose(1, 0, 2)
    by_mode = lax.all_to_all(by_mode, cube, 0, 0, tiled=True)

    def flip(part):
        return part.reshape(n_tx, n_lo, n_dom, pad_cols, modes)[:, ::-1].reshape(devices // 2, pad_cols, modes)

    near, far = (by_mode[: devices // 2], flip(by_mode[devices // 2 :]))
    folded = (devices // 2 * pad_cols, modes)
    spectrum_e = table_left(strip_sine_e, (near + far).reshape(folded), 0)
    spectrum_o = table_left(strip_sine_o, (near - far).reshape(folded), 0)
    hat_e = spectrum_e * (1.0 / (lam_e[:, None] + lam_k[None, :]))
    hat_o = spectrum_o * (1.0 / (lam_o[:, None] + lam_k[None, :]))
    shape = (devices // 2, pad_cols, modes)
    along_e = table_left(strip_sine_e, hat_e, 1).reshape(shape)
    along_o = table_left(strip_sine_o, hat_o, 1).reshape(shape)
    across_e = table_left(strip_slope_e, hat_e, 1).reshape(shape)
    across_o = table_left(strip_slope_o, hat_o, 1).reshape(shape)
    halves = jnp.concatenate(
        [
            jnp.stack([along_e + along_o, across_e + across_o], 1),
            jnp.stack([flip(along_e - along_o), flip(across_o - across_e)], 1),
        ],
        0,
    )
    halves = lax.all_to_all(halves, cube, 0, 0, tiled=True)

    halves = halves.transpose(1, 2, 0, 3).reshape(2, pad_cols, GRID)
    x_e = table_right(halves[0, :, :HALF], slope_e, 1)
    x_o = table_right(halves[0, :, HALF:], slope_o, 1)
    y_e = table_right(halves[1, :, :HALF], sine_e, 1)
    y_o = table_right(halves[1, :, HALF:], sine_o, 1)
    field = jnp.stack([jnp.concatenate([x_e + x_o, y_e + y_o], 0), jnp.concatenate([x_o - x_e, y_e - y_o], 0)])
    field = jnp.pad(field, ((0, 0), (0, 0), (0, window)))
    field_high, field_low = split(field)

    return pl.pallas_call(
        functools.partial(sample_alone, strips, 0),
        out_shape=[kick_shape] * (n_tx * n_dom),
        in_specs=[smem] * 4 + [vmem] * 3,
        out_specs=[vmem] * (n_tx * n_dom),
        compiler_params=params,
        name="sample",
    )(*to_sample, field_high, field_low)


def shards(cell_row, cell_col, weights, momenta):
    n_tx, n_lo, n_dom = (lax.axis_size(name) for name in ("tx", "lo", "dom"))
    tile_rows = GRID // n_tx
    tile_cols = HALF // n_lo
    lists = n_tx * n_dom
    strips = tile_cols // lists
    pad_cols = strips + 8
    devices = 2 * n_lo * lists
    modes = GRID // devices
    count = cell_row.shape[1]
    q, hi, lo, tx, dom = (lax.axis_index(name) for name in ("q", "hi", "lo", "tx", "dom"))

    row, col, amount = (cell_row[0], cell_col[0], weights[0])
    row = jnp.where(tx >= n_tx // 2, (n_tx - 1 - tx) * tile_rows + (tile_rows - 2) - row, tx * tile_rows + row)
    col = jnp.where(hi == 1, tile_cols - 2 - col, col)
    key = (col // strips * HALF + row) * strips + col % strips
    key, amount, order = lax.sort((key, amount, lax.iota(jnp.int32, count)), num_keys=1, is_stable=False)
    row = (key // strips) % HALF
    col = key // (strips * HALF) * strips + key % strips
    row, col = (row.astype(jnp.float32), col.astype(jnp.float32))

    own_route = [(b * 2 + t, t * 2 + b) for b in range(2) for t in range(2)]
    other_route = [(b * 2 + t, t * 2 + 1 - b) for b in range(2) for t in range(2)]
    own = lax.ppermute(jnp.stack([row, col, amount]), ("q", "hi"), own_route)
    mine, own = lax.optimization_barrier((jnp.stack([row, col]), own))
    other = lax.ppermute(mine, ("q", "hi"), other_route)
    own = lax.all_gather(own, ("tx", "dom"), axis=0)
    other, own = lax.optimization_barrier((other, own))
    shifts = [(a, c) for a in range(n_tx) for c in range(n_dom)][::-1]
    others = [lax.ppermute(other, ("tx", "dom"), shifted(n_tx, n_dom, shift)) if any(shift) else other for shift in shifts]
    sources_tx = jnp.stack([(tx + a) % n_tx for a, _ in shifts])

    strip_start = (tx * n_dom + dom) * strips
    col_pair = jnp.where(q == 1, jnp.array([[0.375, 0.625]]), jnp.array([[0.625, 0.375]]))

    def settings(list_tx):
        upper = list_tx >= n_tx // 2
        row_pair = jnp.where(upper[:, None], jnp.array([[0.25, 0.75]]), jnp.array([[0.75, 0.25]]))
        pairs = jnp.concatenate([row_pair, jnp.broadcast_to(col_pair, (lists, 2))], 1).astype(jnp.float32)
        return (jnp.concatenate([strip_start[None], upper]).astype(jnp.int32), pairs)

    own_scalars, own_pairs = settings(jnp.arange(lists) // n_dom)
    other_scalars, other_pairs = settings(sources_tx)
    smem, vmem = (pl.BlockSpec(memory_space=pltpu.SMEM), pl.BlockSpec(memory_space=pltpu.VMEM))
    params = pltpu.CompilerParams(vmem_limit_bytes=vmem_limit)

    to_deposit = (own_scalars, *block_ends(own), own_pairs, own)
    charge_shape = (2, pad_cols, HALF + window)
    kick_shape = jax.ShapeDtypeStruct((2, count), jnp.float32)

    angles = np.pi * (np.arange(GRID) + 1) / (2 * (GRID + 1))
    lam = (4.0 * np.sin(angles) ** 2).astype(np.float32)
    lam_e, lam_o = (lam[0::2], lam[1::2])
    lam_k = lax.dynamic_slice_in_dim(jnp.asarray(np.concatenate([lam_e, lam_o])), lax.axis_index(cube) * modes, modes)

    if modes % 128 == 0 and strips % 8 == 0 and piece_rows % strips == 0:
        stored = jnp.asarray(np.stack([part for table in basis_tables() for part in split_table(table)]))
        anywhere = pl.BlockSpec(memory_space=pl.ANY)
        fetched = [pltpu.VMEM(stored.shape, stored.dtype), pltpu.SemaphoreType.DMA((8 * pieces,))]
        outgoing = pltpu.VMEM((devices, pad_cols, modes), jnp.float32)
        by_mode = pl.pallas_call(
            functools.partial(modes_kernel, strips),
            out_shape=jax.ShapeDtypeStruct((devices, pad_cols, modes), jnp.float32),
            in_specs=[smem] * 4 + [vmem, anywhere],
            out_specs=vmem,
            scratch_shapes=[
                pltpu.VMEM(charge_shape, jnp.float32),
                pltpu.VMEM((4, HALF, HALF), jnp.bfloat16),
                fetched[1],
                *deposit_parts(lists, charge_shape),
            ],
            compiler_params=params,
            name="modes",
        )(*to_deposit, stored)
        by_mode, *others = lax.optimization_barrier((by_mode, *others))
        other = jnp.stack(others)
        by_mode = lax.all_to_all(by_mode, cube, 0, 0, tiled=True)
        natural = [(b, a * n_dom + c) for b in range(n_lo) for a in range(n_tx) for c in range(n_dom)]
        straight = [(j // n_dom * n_lo + b) * n_dom + j % n_dom for b, j in natural]
        flipped = [(j // n_dom * n_lo + n_lo - 1 - b) * n_dom + j % n_dom for b, j in natural]
        halves = pl.pallas_call(
            functools.partial(columns_kernel, straight, flipped, lists, strips),
            out_shape=jax.ShapeDtypeStruct((devices, 2, pad_cols, modes), jnp.float32),
            in_specs=[vmem] * 3 + [anywhere],
            out_specs=anywhere,
            scratch_shapes=[*fetched, outgoing, outgoing, pltpu.SemaphoreType.DMA((2,))],
            compiler_params=params,
            name="columns",
        )(by_mode, jnp.asarray(np.stack([lam_e, lam_o])), lam_k[:, None], stored)
        halves = lax.all_to_all(halves, cube, 0, 0, tiled=True)
        to_sample = (other_scalars, *block_ends(other), other_pairs, other)
        fields_shape = jax.ShapeDtypeStruct((2, 2 * pad_cols, HALF + window), jnp.bfloat16)
        early = lists // 2
        *kicks, field_high, field_low = pl.pallas_call(
            functools.partial(kicks_kernel, strips),
            out_shape=[kick_shape] * early + [fields_shape] * 2,
            in_specs=[smem] * 4 + [vmem] * 2 + [anywhere],
            out_specs=[vmem] * (early + 2),
            scratch_shapes=fetched,
            compiler_params=params,
            name="kicks",
        )(*to_sample, halves, stored)
        kicks += pl.pallas_call(
            functools.partial(sample_alone, strips, early),
            out_shape=[kick_shape] * (lists - early),
            in_specs=[smem] * 4 + [vmem] * 3,
            out_specs=[vmem] * (lists - early),
            compiler_params=params,
            name="sample",
        )(*to_sample, field_high, field_low)
    else:
        other = jnp.stack(others)
        to_sample = (other_scalars, *block_ends(other), other_pairs, other)
        tables = [tuple(jnp.asarray(part) for part in split_table(table)) for table in basis_tables()]
        kicks = general(to_deposit, to_sample, tables, lam_e, lam_o, lam_k, (n_tx, n_lo, n_dom), charge_shape, kick_shape)
    kicks = [
        lax.ppermute(kick, ("q", "tx", "hi", "dom"), returned(other_route, n_tx, n_dom, shift))
        for kick, shift in zip(kicks, shifts, strict=True)
    ]
    kicks = functools.reduce(jnp.add, kicks)
    _, kick_x, kick_y = lax.sort((order, kicks[0], kicks[1]), num_keys=1, is_stable=False)
    return momenta + kick_gain * jnp.stack([kick_x, kick_y])[None]


def solution(mesh):
    n_beam, n_tx, n_ty, n_dom = (mesh.shape[name] for name in ("beam", "tx", "ty", "dom"))
    split_mesh = Mesh(mesh.devices.reshape(n_beam, n_tx, 2, n_ty // 2, n_dom), ("q", "tx", "hi", "lo", "dom"))
    where = ("tx", "hi", "lo", "dom")
    placed = (P("q", where), P("q", where), P("q", where), P("q", None, where))
    return jax.shard_map(
        shards,
        mesh=split_mesh,
        in_specs=placed,
        out_specs=P("q", None, where),
        check_vma=False,
    )
```

time: 217 us -> 165 us (0.76)
  blocking collectives: 40.1 us -> 14.3 us
  matrix products: 24 us -> 0 us
  local copies, waits for them, and re-layouts: 21.1 us -> 2 us
  starting transfers between devices: 17.5 us -> 31.8 us
  Pallas kernels: 33.2 us -> 47.3 us
  other arithmetic: 31 us -> 18.6 us
    dot_general x24 -> x0, matrix products: 24 us -> none  [dot(): lax.dot_general(left, right, (dims, ((), ())), preferred_element_type=jnp...]
    all_to_all x1 -> x0, blocking collectives: 15.6 us -> none  [shards(): lax.all_to_all(kicks, ('tx', 'dom'), 0, 0, tiled=True)]
    ppermute x2 -> x8, starting transfers between devices: 4.47 us -> 20 us  [the longest x1 11.6 us: shards(): other = lax.ppermute(mine, ('q', 'hi'), other_route)]
    pallas_call x2 -> x4, Pallas kernels: 33.2 us -> 47.3 us  [the longest x1 17.1 us: shards(): pl.pallas_call(functools.partial(kicks_kernel, strips), out_shape=[kick_s...]
    all_gather x1 -> x0, blocking collectives: 11.3 us -> none  [shards(): other = lax.all_gather(other, ('tx', 'dom'), axis=0)]
    unnamed x54 -> x12, local copies, waits for them, and re-layouts: 11 us -> 0.03 us
    rev x3 -> x0, local copies, waits for them, and re-layouts: 4.87 us -> none  [flip(): part.reshape(n_tx, n_lo, n_dom, pad_cols, modes)[:, ::-1]]
    select_n x6 -> x1, other arithmetic: 4.83 us -> 0.07 us  [settings(): jnp.where(upper[:, None], jnp.array([[0.25, 0.75]]), jnp.array([[0.75, 0....]
  transfers between devices with their start and end apart: 5 -> 11, of which waited for: 4 -> 5; matrix products, arithmetic and copies ran while one was open for 1% -> 2% of each run, Pallas kernels for 0% -> 12%
where the time goes in v2:
time: 165 us; the launch traced here: 164 us
  waiting for transfers between devices  49.5 us (30%)
  Pallas kernels  47.3 us (29%)
  starting transfers between devices  31.8 us (19%)
  other arithmetic  18.6 us (11%)
  blocking collectives  14.3 us (9%)
  local copies, waits for them, and re-layouts  2 us (1%)
    all_to_all x1, waiting for transfers between devices, shards(): halves = lax.all_to_all(halves, cube, 0, 0, tiled=True)  26.4 us
    pallas_call x1, Pallas kernels, shards(): pl.pallas_call(functools.partial(kicks_kernel, strips), out_shape=[kick_s...  17.1 us
    all_to_all x1, waiting for transfers between devices, shards(): by_mode = lax.all_to_all(by_mode, cube, 0, 0, tiled=True)  14.6 us
    all_gather x1, blocking collectives, shards(): own = lax.all_gather(own, ('tx', 'dom'), axis=0)  14.3 us
    pallas_call x1, Pallas kernels, shards(): pl.pallas_call(functools.partial(modes_kernel, strips), out_shape=jax.Sha...  13.1 us
    ppermute x1, starting transfers between devices, shards(): other = lax.ppermute(mine, ('q', 'hi'), other_route)  11.6 us
    pallas_call x1, Pallas kernels, shards(): pl.pallas_call(functools.partial(columns_kernel, straight, flipped, lists...  10.8 us
    ppermute x4, waiting for transfers between devices, shards(): lax.ppermute(kick, ('q', 'tx', 'hi', 'dom'), returned(other_route, n_tx,...  8.5 us
  transfers between devices with their start and end apart: 11, of which 5 were waited for; matrix products, arithmetic and copies ran while one was open for 2% of the time, Pallas kernels for 12%

profile of v2, /device:TPU:0, one launch (start us, length us, event | category | flops | bytes accessed | tf_op | source)
XLA Modules:
  0.0 163.8 jit_solution(10912118215496507383)
XLA Ops:
  0.0 0.9 broadcast_select_fusion
  1.0 0.9 fusion.4
  1.9 7.5 %sort.42 = (s32[16384]{0:T(1024)S(1)}, f32[16384]{0:T(1024)S(1)}, s32[16384]{0:T(1024)S(1)}) sort(s32[16384]{0:T(1024)S(1)} %fusion.4, f32[16384]{0:T(1024)} %bitcast.35, s32[16384]{0:T(1024)S(1)} %iota.10), dimensions={0}, to_apply=%region_0.1 | sort | flops 229376 | bytes 393216 | tf_op jit(solution)/shard_map/sort | solution.py:443
  9.5 0.2 pad_maximum_fusion.1
  9.7 0.7 collective-permute-start
  10.9 11.6 %collective-permute-start.1 = (f32[2,16384]{1,0:T(2,128)S(1)}, f32[2,16384]{1,0:T(2,128)S(1)}, u32[]{:S(2)}, u32[]{:S(2)}) collective-permute-start(f32[2,16384]{1,0:T(2,128)S(1)} %pad_maximum_fusion.2), channel_id=1, source_target_pairs={{0,4},{4,20},{16,0},{20,16},{1,5},{5,21},{17,1},{21,17},{2,6},{6,2... | collective-permute-start | bytes 393224 | tf_op jit(solution)/shard_map/ppermute | solution.py:452
  22.5 14.3 %all-gather.1.lists = f32[4,3,16384]{2,1,0:T(4,128)S(1)} all-gather(f32[1,3,16384]{2,1,0:T(4,128)S(1)} %bitcast.26), channel_id=2, replica_groups=mesh['q'=2,'tx'=2,'hi'=2,'lo'=2,'dom'=2] {'tx','dom'}, dimensions={0}, use_global_device_ids=true | all-gather | bytes 983040 | tf_op jit(solution)/shard_map/all_gather | solution.py:453
  36.7 1.6 collective-permute-start.4
  38.3 0.5 collective-permute-start.3
  38.8 1.5 collective-permute-start.2
  40.4 0.2 slice.19
  40.6 0.2 slice.18
  40.8 13.1 %modes.1 = f32[16,136,128]{2,1,0:T(8,128)} custom-call(s32[5]{0:T(128)S(1)} %pad_add_fusion.1.scalars, s32[4,2,32]{2,1,0:T(2,128)S(1)} %convert_element_type.28.first, s32[4,2,32]{2,1,0:T(2,128)S(1)} %convert_element_type.29.last, f32[4,4]{1,0:T(4,128)S(1)} %get-tuple-element.54.weights, f32[4,3,16384]{2,1,0:T(4,128)S(1)} %all-gather.1.lists, ...), custom_call_target="tpu_custom_call" | custom-call | tf_op jit(solution)/shard_map/modes/pallas_call | solution.py:487
  54.0 7.2 %all-to-all-start = ((f32[16,136,128]{2,1,0:T(8,128)}), f32[16,136,128]{2,1,0:T(8,128)S(1)}, u32[]{:S(2)}, u32[]{:S(2)}) async-start(f32[16,136,128]{2,1,0:T(8,128)} %modes.1), calls=%async_computation | async-start | bytes 2228224 | tf_op jit(solution)/shard_map/all_to_all | solution.py:503
  61.2 0.8 dynamic-slice_bitcast_fusion
  62.1 14.6 %all-to-all-done.by_mode = f32[16,136,128]{2,1,0:T(8,128)S(1)} async-done(((f32[16,136,128]{2,1,0:T(8,128)}), f32[16,136,128]{2,1,0:T(8,128)S(1)}, u32[]{:S(2)}, u32[]{:S(2)}) %all-to-all-start) | async-done | bytes 1114144 | tf_op jit(solution)/shard_map/all_to_all | solution.py:503
  76.7 10.8 %columns.1 = f32[16,2,136,128]{3,2,1,0:T(8,128)} custom-call(f32[16,136,128]{2,1,0:T(8,128)S(1)} %all-to-all-done.by_mode, f32[2,1024]{1,0:T(2,128)S(1)} %copy-done, f32[128,1]{1,0:T(8,128)S(1)} %copy.15.lam_mine, bf16[8,1024,1024]{2,1,0:T(8,128)(2,1)} %constant.149.clone.stored), custom_call_target="tpu_custom_call" | custom-call | tf_op jit(solution)/shard_map/columns/pallas_call | solution.py:507
  87.5 4.0 %all-to-all-start.1 = ((f32[16,2,136,128]{3,2,1,0:T(8,128)}), f32[16,2,136,128]{3,2,1,0:T(8,128)S(1)}, u32[]{:S(2)}, u32[]{:S(2)}) async-start(f32[16,2,136,128]{3,2,1,0:T(8,128)} %columns.1), calls=%async_computation.1 | async-start | bytes 4456448 | tf_op jit(solution)/shard_map/all_to_all | solution.py:516
  91.5 0.2 pad_maximum_fusion.lists
  91.8 0.2 slice.21
  92.0 0.2 slice.20
  92.2 26.4 %all-to-all-done.1.halves = f32[16,2,136,128]{3,2,1,0:T(8,128)S(1)} async-done(((f32[16,2,136,128]{3,2,1,0:T(8,128)}), f32[16,2,136,128]{3,2,1,0:T(8,128)S(1)}, u32[]{:S(2)}, u32[]{:S(2)}) %all-to-all-start.1) | async-done | bytes 2228256 | tf_op jit(solution)/shard_map/all_to_all | solution.py:516
  118.7 17.1 %kicks.1 = (f32[2,16384]{1,0:T(2,128)S(1)}, f32[2,16384]{1,0:T(2,128)S(1)}, bf16[2,272,1280]{2,1,0:T(8,128)(2,1)S(1)}, bf16[2,272,1280]{2,1,0:T(8,128)(2,1)S(1)}) custom-call(s32[5]{0:T(128)S(1)} %pad_add_fusion.scalars, s32[4,2,32]{2,1,0:T(2,128)S(1)} %convert_element_type.30.first, s32[4,2,32]{2,1,0:T(2,128)S(1)} %convert_element_type.31.last, ...), custom_call_target="tpu_custom_call" | custom-call | tf_op jit(solution)/shard_map/kicks/pallas_call | solution.py:520
  135.8 3.5 %collective-permute-start.5 = (f32[2,16384]{1,0:T(2,128)S(1)}, f32[2,16384]{1,0:T(2,128)S(1)}, u32[]{:S(2)}, u32[]{:S(2)}) collective-permute-start(f32[2,16384]{1,0:T(2,128)S(1)} %get-tuple-element.37), channel_id=1, source_target_pairs={{4,9},{5,8},{12,1},{13,0},{20,13},{21,12},{28,5},{29,4},{0,25},{1,... | collective-permute-start | bytes 393224 | tf_op jit(solution)/shard_map/ppermute | solution.py:543
  139.2 6.3 %sample.1 = (f32[2,16384]{1,0:T(2,128)S(1)}, f32[2,16384]{1,0:T(2,128)S(1)}) custom-call(s32[5]{0:T(128)S(1)} %pad_add_fusion.scalars, s32[4,2,32]{2,1,0:T(2,128)S(1)} %convert_element_type.30.first, s32[4,2,32]{2,1,0:T(2,128)S(1)} %convert_element_type.31.last, f32[4,4]{1,0:T(4,128)S(1)} %get-tuple-element.53.weights, ...), custom_call_target="tpu_custom_call" | custom-call | tf_op jit(solution)/shard_map/sample/pallas_call | solution.py:529
  145.5 0.5 collective-permute-start.7
  146.0 0.9 collective-permute-start.8
  146.9 1.3 collective-permute-done.6
  148.2 6.7 %collective-permute-done.7 = f32[2,16384]{1,0:T(2,128)S(1)} collective-permute-done((f32[2,16384]{1,0:T(2,128)S(1)}, f32[2,16384]{1,0:T(2,128)S(1)}, u32[]{:S(2)}, u32[]{:S(2)}) %collective-permute-start.7) | collective-permute-done | bytes 131104 | tf_op jit(solution)/shard_map/ppermute | solution.py:543
  154.9 0.5 collective-permute-done.8
  155.7 7.3 %sort.43 = (s32[16384]{0:T(1024)}, f32[16384]{0:T(1024)S(1)}, f32[16384]{0:T(1024)S(1)}) sort(s32[16384]{0:T(1024)S(1)} %get-tuple-element.25, f32[16384]{0:T(1024)S(1)} %bitcast.29, f32[16384]{0:T(1024)S(1)} %bitcast.28), dimensions={0}, to_apply=%region_1.2 | sort | flops 229376 | bytes 393216 | tf_op jit(solution)/shard_map/sort | solution.py:547
  163.0 0.8 fusion
  (37 shorter events, 1.0 us)
Async XLA Ops:
  0.0 10.6 %copy-start.4 = (f32[1,2]{1,0:T(1,128)S(1)}, f32[1,2]{1,0:T(1,128)}, u32[]{:S(2)}) copy-start(f32[1,2]{1,0:T(1,128)} %constant.145.clone) | copy-start | bytes 28
  0.0 10.6 %copy-start.5 = (f32[1,2]{1,0:T(1,128)S(1)}, f32[1,2]{1,0:T(1,128)}, u32[]{:S(2)}) copy-start(f32[1,2]{1,0:T(1,128)} %constant.144.clone) | copy-start | bytes 28
  0.0 10.8 %copy-start.2 = (f32[2]{0:T(128)S(1)}, f32[2]{0:T(128)}, u32[]{:S(2)}) copy-start(f32[2]{0:T(128)} %constant.156) | copy-start | bytes 28
  0.0 10.8 %copy-start.3 = (f32[2]{0:T(128)S(1)}, f32[2]{0:T(128)}, u32[]{:S(2)}) copy-start(f32[2]{0:T(128)} %constant.155) | copy-start | bytes 28
  9.7 1.1 collective-permute-start
  10.9 25.9 %collective-permute-start.1 = (f32[2,16384]{1,0:T(2,128)S(1)}, f32[2,16384]{1,0:T(2,128)S(1)}, u32[]{:S(2)}, u32[]{:S(2)}) collective-permute-start(f32[2,16384]{1,0:T(2,128)S(1)} %pad_maximum_fusion.2), channel_id=1, source_target_pairs={{0,4},{4,20},{16,0},{20,16},{1,5},{5,21},{17,1},{21,17},{2,6},{6,2... | collective-permute-start | bytes 393224 | tf_op jit(solution)/shard_map/ppermute | solution.py:452
  36.7 17.2 %collective-permute-start.4 = (f32[2,16384]{1,0:T(2,128)S(1)}, f32[2,16384]{1,0:T(2,128)S(1)}, u32[]{:S(2)}, u32[]{:S(2)}) collective-permute-start(f32[2,16384]{1,0:T(2,128)S(1)} %collective-permute-done.1), channel_id=1, source_target_pairs={{1,0},{0,1},{9,8},{8,9},{3,2},{2,3},{11,10},{10,11},{5,4},{4,5},{1... | collective-permute-start | bytes 393224 | tf_op jit(solution)/shard_map/ppermute | solution.py:456
  38.3 15.7 %collective-permute-start.3 = (f32[2,16384]{1,0:T(2,128)S(1)}, f32[2,16384]{1,0:T(2,128)S(1)}, u32[]{:S(2)}, u32[]{:S(2)}) collective-permute-start(f32[2,16384]{1,0:T(2,128)S(1)} %collective-permute-done.1), channel_id=1, source_target_pairs={{8,0},{9,1},{0,8},{1,9},{10,2},{11,3},{2,10},{3,11},{12,4},{13,5},... | collective-permute-start | bytes 393224 | tf_op jit(solution)/shard_map/ppermute | solution.py:456
  38.8 15.2 %collective-permute-start.2 = (f32[2,16384]{1,0:T(2,128)S(1)}, f32[2,16384]{1,0:T(2,128)S(1)}, u32[]{:S(2)}, u32[]{:S(2)}) collective-permute-start(f32[2,16384]{1,0:T(2,128)S(1)} %collective-permute-done.1), channel_id=1, source_target_pairs={{9,0},{8,1},{1,8},{0,9},{11,2},{10,3},{3,10},{2,11},{13,4},{12,5},... | collective-permute-start | bytes 393224 | tf_op jit(solution)/shard_map/ppermute | solution.py:456
  54.0 22.7 %copy-start = (f32[2,1024]{1,0:T(2,128)S(1)}, f32[2,1024]{1,0:T(2,128)}, u32[]{:S(2)}) copy-start(f32[2,1024]{1,0:T(2,128)} %constant.150.clone.lam) | copy-start | bytes 24580
  54.0 22.6 %all-to-all-start = ((f32[16,136,128]{2,1,0:T(8,128)}), f32[16,136,128]{2,1,0:T(8,128)S(1)}, u32[]{:S(2)}, u32[]{:S(2)}) async-start(f32[16,136,128]{2,1,0:T(8,128)} %modes.1), calls=%async_computation | async-start | bytes 2228224 | tf_op jit(solution)/shard_map/all_to_all | solution.py:503
  87.5 31.2 %all-to-all-start.1 = ((f32[16,2,136,128]{3,2,1,0:T(8,128)}), f32[16,2,136,128]{3,2,1,0:T(8,128)S(1)}, u32[]{:S(2)}, u32[]{:S(2)}) async-start(f32[16,2,136,128]{3,2,1,0:T(8,128)} %columns.1), calls=%async_computation.1 | async-start | bytes 4456448 | tf_op jit(solution)/shard_map/all_to_all | solution.py:516
  135.8 11.2 %collective-permute-start.5 = (f32[2,16384]{1,0:T(2,128)S(1)}, f32[2,16384]{1,0:T(2,128)S(1)}, u32[]{:S(2)}, u32[]{:S(2)}) collective-permute-start(f32[2,16384]{1,0:T(2,128)S(1)} %get-tuple-element.37), channel_id=1, source_target_pairs={{4,9},{5,8},{12,1},{13,0},{20,13},{21,12},{28,5},{29,4},{0,25},{1,... | collective-permute-start | bytes 393224 | tf_op jit(solution)/shard_map/ppermute | solution.py:543
  139.2 9.0 %collective-permute-start.6 = (f32[2,16384]{1,0:T(2,128)S(1)}, f32[2,16384]{1,0:T(2,128)S(1)}, u32[]{:S(2)}, u32[]{:S(2)}) collective-permute-start(f32[2,16384]{1,0:T(2,128)S(1)} %get-tuple-element.38), channel_id=1, source_target_pairs={{4,8},{5,9},{12,0},{13,1},{20,12},{21,13},{28,4},{29,5},{0,24},{1,... | collective-permute-start | bytes 393224 | tf_op jit(solution)/shard_map/ppermute | solution.py:543
  139.2 23.8 %copy-start.1 = (f32[1,2,16384]{2,1,0:T(2,128)S(1)}, f32[1,2,16384]{2,1,0:T(2,128)}, u32[]{:S(2)}) copy-start(f32[1,2,16384]{2,1,0:T(2,128)} %param.16) | copy-start | bytes 393220
  145.5 9.4 %collective-permute-start.7 = (f32[2,16384]{1,0:T(2,128)S(1)}, f32[2,16384]{1,0:T(2,128)S(1)}, u32[]{:S(2)}, u32[]{:S(2)}) collective-permute-start(f32[2,16384]{1,0:T(2,128)S(1)} %get-tuple-element.41), channel_id=1, source_target_pairs={{4,1},{5,0},{12,9},{13,8},{20,5},{21,4},{28,13},{29,12},{0,17},{1,... | collective-permute-start | bytes 393224 | tf_op jit(solution)/shard_map/ppermute | solution.py:543
  146.0 9.4 %collective-permute-start.8 = (f32[2,16384]{1,0:T(2,128)S(1)}, f32[2,16384]{1,0:T(2,128)S(1)}, u32[]{:S(2)}, u32[]{:S(2)}) collective-permute-start(f32[2,16384]{1,0:T(2,128)S(1)} %get-tuple-element.42), channel_id=1, source_target_pairs={{4,0},{5,1},{12,8},{13,9},{20,4},{21,5},{28,12},{29,13},{0,16},{1,... | collective-permute-start | bytes 393224 | tf_op jit(solution)/shard_map/ppermute | solution.py:543

commit v3 on v2

--- a/solution.py
+++ b/solution.py
@@ -15,7 +15,7 @@
 kick_gain = 2.0
 block = 512
 window = 256
-pieces = 4
+pieces = 2
 piece_rows = HALF // pieces
 cube = ("q", "tx", "lo", "dom")
 vmem_limit = 48 * 1024 * 1024
@@ -39,6 +39,18 @@
     return (sine[:, 0::2], sine[:, 1::2], slope[:, 0::2], slope[:, 1::2])
 
 
+def folded_tables():
+    points = GRID + 1
+    number = np.arange(HALF) + 1
+    angles = 2 * np.pi * (number[:, None] * number[None, :] % points) / points
+    scaling = np.sqrt(2.0 / points)
+    return np.stack([part for table in (np.sin(angles), np.cos(angles)) for part in split_table(scaling * table)])
+
+
+def alternate(shape, dim):
+    return (1 - 2 * (lax.broadcasted_iota(jnp.int32, shape, dim) % 2)).astype(jnp.float32)
+
+
 def split(values):
     high = lax.reduce_precision(values, 8, 7)
     return (high.astype(jnp.bfloat16), (values - high).astype(jnp.bfloat16))
@@ -101,13 +113,19 @@
         )
 
     found = lax.fori_loop(0, first.shape[2], bounds, tuple((0, 0) for _ in group))
-    turns = functools.reduce(jnp.maximum, [high - low for low, high in found])
+    stride = max(4 // len(group), 1)
+    turns = (functools.reduce(jnp.maximum, [high - low for low, high in found]) + stride - 1) // stride
+    streams = [
+        (place * stride + ahead, which, low + ahead, high)
+        for place, (which, (low, high)) in enumerate(zip(group, found, strict=True))
+        for ahead in range(stride)
+    ]
 
     def one_turn(step, carry):
         more = []
-        for place, (which, (low, high)) in enumerate(zip(group, found, strict=True)):
-            valid = low + step < high
-            turn = jnp.minimum(low + step, first.shape[2] - 1)
+        for place, which, low, high in streams:
+            valid = low + step * stride < high
+            turn = jnp.minimum(low + step * stride, first.shape[2] - 1)
             at, count = windows(strips, start, first, last, which, turn)
             item(place, which, turn, pl.multiple_of(at, 128), valid)
             more.append((place, which, turn, at, jnp.where(valid, count, 0)))
@@ -123,10 +141,15 @@
     lax.fori_loop(0, turns, one_turn, 0)
 
 
-def cells_of(strips, scalars, lists, which, here, at, valid):
-    row = lists[which, 0:1, here].astype(jnp.int32) - at
+def values_of(lists, which, what, turn):
+    rows = block // 128
+    return jnp.concatenate([lists[which, what, pl.ds(turn * rows + i, 1)] for i in range(rows)], 1)
+
+
+def cells_of(strips, scalars, lists, which, turn, at, valid):
+    row = values_of(lists, which, 0, turn).astype(jnp.int32) - at
     row = jnp.where((row >= -1) & (row < window) & valid, row, -10)
-    col = lists[which, 1:2, here].astype(jnp.int32) - scalars[0]
+    col = values_of(lists, which, 1, turn).astype(jnp.int32) - scalars[0]
     col = jnp.where((col >= 0) & (col < strips), col, -10)
     return (row, col)
 
@@ -146,9 +169,8 @@
         return which // (count // 2)
 
     def item(place, which, turn, at, valid):
-        here = pl.ds(pl.multiple_of(turn * block, block), block)
-        row, col = cells_of(strips, scalars, lists, which, here, at, valid)
-        amount = lists[which, 2:3, here]
+        row, col = cells_of(strips, scalars, lists, which, turn, at, valid)
+        amount = values_of(lists, which, 2, turn)
         near, far = (weights[which, 2] * amount, weights[which, 3] * amount)
         near_high, far_high = (near.astype(jnp.bfloat16), far.astype(jnp.bfloat16))
         near_low = (near - near_high.astype(jnp.float32)).astype(jnp.bfloat16)
@@ -185,7 +207,7 @@
         here = pl.ds(pl.multiple_of(turn * block, block), block)
         half = scalars[1 + which]
         kick = kicks[which - begin]
-        row, col = cells_of(strips, scalars, lists, which, here, at, valid)
+        row, col = cells_of(strips, scalars, lists, which, turn, at, valid)
         rows = pair_weights(short(row), short(weights[which, 0]), short(weights[which, 1]), window)
         fields = jnp.concatenate([field_high[half, :, pl.ds(at, window)], field_low[half, :, pl.ds(at, window)]], 1)
         near = dot(fields, jnp.concatenate([rows, rows], 0), ((1,), (0,)))
@@ -198,36 +220,39 @@
         each_window(strips, scalars, first, last, group, item)
 
 
-def fetch(stored, tables, arrived, order):
-    copies = {}
-    for number, (part, piece) in enumerate(order):
+def fetch(stored, tables, arrived, parts):
+    copies = {part: [] for part in parts}
+    for number, (part, piece) in enumerate((part, piece) for part in parts for piece in range(pieces)):
         rows = pl.ds(piece * piece_rows, piece_rows)
-        copies[part, piece] = pltpu.make_async_copy(stored.at[part, rows], tables.at[part, rows], arrived.at[number])
-        copies[part, piece].start()
-
-    def table(part, piece):
-        copies[part, piece].wait()
-        return tables[part, piece * piece_rows : (piece + 1) * piece_rows]
+        copies[part].append(pltpu.make_async_copy(stored.at[part, rows], tables.at[part, rows], arrived.at[number]))
+        copies[part][-1].start()
+
+    def table(part, begin=0, end=pieces):
+        for copy in copies[part][begin:end] + copies[part + 1][begin:end]:
+            copy.wait()
+        rows = slice(begin * piece_rows, end * piece_rows)
+        return (tables[part, rows], tables[part + 1, rows])
 
     return table
 
 
 def modes_kernel(strips, scalars, first, last, weights, lists, stored, by_mode, charge, tables, arrived, *parts):
-    table = fetch(stored, tables, arrived, [(part, piece) for part in range(4) for piece in range(pieces)])
+    table = fetch(stored, tables, arrived, (0, 1))
     deposit_body(strips, scalars, first, last, weights, lists, charge, parts)
-    devices, _, modes = by_mode.shape
+    devices, pad_cols, modes = by_mode.shape
     near, far = (charge[0, :, :HALF], charge[1, :, :HALF])
-    for parity, part in enumerate((near + far, near - far)):
-        high, low = (jnp.concatenate([table(2 * parity + i, piece) for piece in range(pieces)], 0) for i in range(2))
-        done = dot_parts(high, low, part, ((1,), (0,)))
-        for turn in range(devices // 2):
-            by_mode[parity * (devices // 2) + turn] = done[:, turn * modes : (turn + 1) * modes]
-
-
-def columns_kernel(order, flipped, per_tile, strips, by_mode, lam, lam_mine, stored, halves, tables, arrived, back_x, back_y, sent):
-    forward = [(2 * parity + i, piece) for parity in range(2) for piece in range(pieces) for i in range(2)]
-    backward = [(part, piece) for piece in range(pieces) for part in range(4, 8)]
-    table = fetch(stored, tables, arrived, forward + backward)
+    high, low = table(0)
+    both = jnp.concatenate([(near + far) * alternate((1, HALF), 1), near - far], 0)
+    done = dot_parts(high, low, both, ((1,), (0,)))
+    for turn in range(devices // 2):
+        here = slice(turn * modes, (turn + 1) * modes)
+        by_mode[turn] = done[:pad_cols, here]
+        by_mode[devices // 2 + turn] = done[pad_cols:, here]
+
+
+def columns_kernel(order, flipped, per_tile, strips, by_mode, lam, wave, mine, stored, halves, tables, arrived, back_x, back_y, sent):
+    table = fetch(stored, tables, arrived, (0, 1, 2, 3))
+    sine_parts = table(0)
     modes = by_mode.shape[2]
     near, far = ([], [])
     for place in range(len(order)):
@@ -240,43 +265,39 @@
             pair.append(body)
         near.append(pair[0] + pair[1])
         far.append(pair[0] - pair[1])
-    hats = []
-    for parity, part in enumerate((near, far)):
-        part = jnp.concatenate(part, 0).T
-        spectrum = 0.0
-        for piece in range(pieces):
-            high, low = (table(2 * parity + i, piece) for i in range(2))
-            spectrum += dot_parts(high, low, part[:, piece * piece_rows : (piece + 1) * piece_rows], ((1,), (0,)))
-        hat = (spectrum * (1.0 / (lam[parity : parity + 1, :] + lam_mine[...]))).T
-        high = hat.astype(jnp.bfloat16)
-        hats.append((high, jnp.concatenate([high, (hat - high.astype(jnp.float32)).astype(jnp.bfloat16)], 1)))
-
-    def back(table_high, table_low, parity):
-        high, both = hats[parity]
-        done = dot(table_high, both, ((1,), (0,)))
-        return done[:, :modes] + done[:, modes:] + dot(table_low, high, ((1,), (0,)))
+    columns = jnp.concatenate([jnp.concatenate(near, 0).T * alternate((1, HALF), 1), jnp.concatenate(far, 0).T], 0)
+    spectrum = dot_parts(*sine_parts, columns, ((1,), (0,)))
+    lam_mine, wave_mine = (mine[:, 0:1], mine[:, 1:2])
+    hats = ([], [])
+    for parity in range(2):
+        this = slice(parity, parity + 1)
+        hat = spectrum[parity * modes : (parity + 1) * modes] * (1.0 / (lam[this, :] + lam_mine))
+        hats[0].append((hat * wave_mine).T)
+        hats[1].append((hat * wave[this, :]).T)
 
     copies = []
     for component, (outgoing, sign) in enumerate(((back_x, 1), (back_y, -1))):
+        hat = jnp.concatenate(hats[component], 1)
+        hat_high = hat.astype(jnp.bfloat16)
+        hat_both = jnp.concatenate([hat_high, (hat - hat_high.astype(jnp.float32)).astype(jnp.bfloat16)], 1)
+        parts = sine_parts if component == 0 else table(2)
         for piece in range(pieces):
-            if component == 0:
-                rows = slice(piece * piece_rows, (piece + 1) * piece_rows)
-                parts = [tables[i, rows] for i in range(4)]
-            else:
-                parts = [table(4 + i, piece) for i in range(4)]
-            even, odd = (back(parts[0], parts[1], 0), back(parts[2], parts[3], 1))
+            high, low = (part[piece * piece_rows : (piece + 1) * piece_rows] for part in parts)
+            done = dot(high, hat_both, ((1,), (0,)))
+            done = done[:, : 2 * modes] + done[:, 2 * modes :] + dot(low, hat_high, ((1,), (0,)))
+            even, odd = (done[:, :modes] * (sign * alternate((piece_rows, modes), 0)), done[:, modes:])
             for before, whose, value in (
                 (0, order, even + odd),
                 (len(order), flipped, even - odd if sign == 1 else odd - even),
             ):
                 for turn in range(piece_rows // strips):
                     place = piece * piece_rows // strips + turn
-                    mine = value[turn * strips : (turn + 1) * strips]
-                    outgoing[before + whose[place], :strips] = mine
+                    part = value[turn * strips : (turn + 1) * strips]
+                    outgoing[before + whose[place], :strips] = part
                     if place % per_tile:
-                        outgoing[before + whose[place - 1], strips:] = mine[:8]
+                        outgoing[before + whose[place - 1], strips:] = part[:8]
                     if place % per_tile == per_tile - 1:
-                        outgoing[before + whose[place], strips:] = jnp.zeros_like(mine[:8])
+                        outgoing[before + whose[place], strips:] = jnp.zeros_like(part[:8])
         copies.append(pltpu.make_async_copy(outgoing, halves.at[:, component], sent.at[component]))
         copies[-1].start()
     for copy in copies:
@@ -285,33 +306,26 @@
 
 def kicks_kernel(strips, scalars, first, last, weights, lists, halves, stored, *refs):
     kicks, (field_high, field_low, tables, arrived) = (refs[:-4], refs[-4:])
-    order = [(part, piece) for parts in ((4, 5, 6, 7), (0, 1, 2, 3)) for piece in range(pieces) for part in parts]
-    table = fetch(stored, tables, arrived, order)
+    table = fetch(stored, tables, arrived, (2, 3, 0, 1))
     devices, _, pad_cols, _ = halves.shape
     wide = 2 * pad_cols
     fields = {}
-    for component, (which, sign) in enumerate(((4, -1), (0, 1))):
-        sides = []
-        for start in (0, devices // 2):
-            part = jnp.concatenate([halves[start + turn, component] for turn in range(devices // 2)], 1)
-            high = part.astype(jnp.bfloat16)
-            low = part - high.astype(jnp.float32)
-            sides.append((jnp.concatenate([high.astype(jnp.float32), low], 0).astype(jnp.bfloat16), high))
+    for component, sign in enumerate((-1, 1)):
+        sides = [
+            jnp.concatenate([halves[start + turn, component] for turn in range(devices // 2)], 1) for start in (0, devices // 2)
+        ]
+        both = jnp.concatenate(sides, 0)
+        done = 0.0
         for piece in range(pieces):
-            pair = []
-            for parity, (both, high) in enumerate(sides):
-                table_high, table_low = (table(which + 2 * parity + i, piece) for i in range(2))
-                done = dot(both, table_high, ((1,), (1,)))
-                pair.append(done[:pad_cols] + done[pad_cols:] + dot(high, table_low, ((1,), (1,))))
-            even, odd = pair
-            fields[component, piece] = (even + odd, even - odd if sign == 1 else odd - even)
+            rows = slice(piece * piece_rows, (piece + 1) * piece_rows)
+            done += dot_parts(*table(2 - 2 * component, piece, piece + 1), both[:, rows], ((1,), (0,)))
+        even, odd = (done[:pad_cols] * (sign * alternate((1, HALF), 1)), done[pad_cols:])
+        fields[component] = (even + odd, even - odd if sign == 1 else odd - even)
     for half in range(2):
-        for piece in range(pieces):
-            here = slice(piece * piece_rows, (piece + 1) * piece_rows)
-            value = jnp.concatenate([fields[component, piece][half] for component in range(2)], 0)
-            high = value.astype(jnp.bfloat16)
-            field_high[half, :, here] = high
-            field_low[half, :, here] = (value - high.astype(jnp.float32)).astype(jnp.bfloat16)
+        value = jnp.concatenate([fields[component][half] for component in range(2)], 0)
+        high = value.astype(jnp.bfloat16)
+        field_high[half, :, :HALF] = high
+        field_low[half, :, :HALF] = (value - high.astype(jnp.float32)).astype(jnp.bfloat16)
         beyond = jnp.zeros((wide, window), jnp.bfloat16)
         field_high[half, :, HALF:] = beyond
         field_low[half, :, HALF:] = beyond
@@ -319,7 +333,8 @@
 
 
 def block_ends(lists):
-    ends = (lists[:, :2, 0::block], lists[:, :2, block - 1 :: block])
+    rows = block // 128
+    ends = (lists[:, :2, 0::rows, 0], lists[:, :2, rows - 1 :: rows, 127])
     return tuple(end.astype(jnp.int32) for end in ends)
 
 
@@ -436,14 +451,14 @@
     count = cell_row.shape[1]
     q, hi, lo, tx, dom = (lax.axis_index(name) for name in ("q", "hi", "lo", "tx", "dom"))
 
-    row, col, amount = (cell_row[0], cell_col[0], weights[0])
+    row, col, amount = (cell_row, cell_col, weights[0])
     row = jnp.where(tx >= n_tx // 2, (n_tx - 1 - tx) * tile_rows + (tile_rows - 2) - row, tx * tile_rows + row)
     col = jnp.where(hi == 1, tile_cols - 2 - col, col)
     key = (col // strips * HALF + row) * strips + col % strips
-    key, amount, order = lax.sort((key, amount, lax.iota(jnp.int32, count)), num_keys=1, is_stable=False)
+    key, amount, order = lax.sort((key.reshape(-1), amount, lax.iota(jnp.int32, count)), num_keys=1, is_stable=False)
     row = (key // strips) % HALF
     col = key // (strips * HALF) * strips + key % strips
-    row, col = (row.astype(jnp.float32), col.astype(jnp.float32))
+    row, col, amount = (values.astype(jnp.float32).reshape(-1, 128) for values in (row, col, amount))
 
     own_route = [(b * 2 + t, t * 2 + b) for b in range(2) for t in range(2)]
     other_route = [(b * 2 + t, t * 2 + 1 - b) for b in range(2) for t in range(2)]
@@ -480,9 +495,9 @@
     lam_k = lax.dynamic_slice_in_dim(jnp.asarray(np.concatenate([lam_e, lam_o])), lax.axis_index(cube) * modes, modes)
 
     if modes % 128 == 0 and strips % 8 == 0 and piece_rows % strips == 0:
-        stored = jnp.asarray(np.stack([part for table in basis_tables() for part in split_table(table)]))
+        stored = jnp.asarray(folded_tables())
         anywhere = pl.BlockSpec(memory_space=pl.ANY)
-        fetched = [pltpu.VMEM(stored.shape, stored.dtype), pltpu.SemaphoreType.DMA((8 * pieces,))]
+        fetched = [pltpu.VMEM(stored.shape, stored.dtype), pltpu.SemaphoreType.DMA((4 * pieces,))]
         outgoing = pltpu.VMEM((devices, pad_cols, modes), jnp.float32)
         by_mode = pl.pallas_call(
             functools.partial(modes_kernel, strips),
@@ -491,7 +506,7 @@
             out_specs=vmem,
             scratch_shapes=[
                 pltpu.VMEM(charge_shape, jnp.float32),
-                pltpu.VMEM((4, HALF, HALF), jnp.bfloat16),
+                pltpu.VMEM((2, HALF, HALF), jnp.bfloat16),
                 fetched[1],
                 *deposit_parts(lists, charge_shape),
             ],
@@ -501,18 +516,22 @@
         by_mode, *others = lax.optimization_barrier((by_mode, *others))
         other = jnp.stack(others)
         by_mode = lax.all_to_all(by_mode, cube, 0, 0, tiled=True)
+        order_k = np.concatenate([GRID - 2 - 2 * np.arange(HALF), 2 * np.arange(HALF) + 1])
+        wave = (-np.pi * (np.arange(GRID) + 1) / (GRID + 1)).astype(np.float32)
+        mine = jnp.asarray(np.stack([lam[order_k], wave[order_k]], 1))
+        mine = lax.dynamic_slice_in_dim(mine, lax.axis_index(cube) * modes, modes)
         natural = [(b, a * n_dom + c) for b in range(n_lo) for a in range(n_tx) for c in range(n_dom)]
         straight = [(j // n_dom * n_lo + b) * n_dom + j % n_dom for b, j in natural]
         flipped = [(j // n_dom * n_lo + n_lo - 1 - b) * n_dom + j % n_dom for b, j in natural]
         halves = pl.pallas_call(
             functools.partial(columns_kernel, straight, flipped, lists, strips),
             out_shape=jax.ShapeDtypeStruct((devices, 2, pad_cols, modes), jnp.float32),
-            in_specs=[vmem] * 3 + [anywhere],
+            in_specs=[vmem] * 4 + [anywhere],
             out_specs=anywhere,
             scratch_shapes=[*fetched, outgoing, outgoing, pltpu.SemaphoreType.DMA((2,))],
-            compiler_params=params,
+            compiler_params=pltpu.CompilerParams(vmem_limit_bytes=51 * 1024 * 1024),
             name="columns",
-        )(by_mode, jnp.asarray(np.stack([lam_e, lam_o])), lam_k[:, None], stored)
+        )(by_mode, *(jnp.asarray(values[order_k].reshape(2, HALF)) for values in (lam, wave)), mine, stored)
         halves = lax.all_to_all(halves, cube, 0, 0, tiled=True)
         to_sample = (other_scalars, *block_ends(other), other_pairs, other)
         fields_shape = jax.ShapeDtypeStruct((2, 2 * pad_cols, HALF + window), jnp.bfloat16)

time: 165 us -> 152 us (0.921)
  Pallas kernels: 47.3 us -> 36 us
  blocking collectives: 14.3 us -> 11.1 us
  starting transfers between devices: 31.8 us -> 33.6 us
    pallas_call x1, Pallas kernels: 17.1 us -> 11.4 us  [shards(): pl.pallas_call(functools.partial(kicks_kernel, strips), out_shape=[kick_s...]
    all_gather x1, blocking collectives: 14.3 us -> 11.1 us  [shards(): own = lax.all_gather(own, ('tx', 'dom'), axis=0)]
    pallas_call x1, Pallas kernels: 13.1 us -> 10.3 us  [shards(): pl.pallas_call(functools.partial(modes_kernel, strips), out_shape=jax.Sha...]
    all_to_all x1, starting transfers between devices: 7.16 us -> 9.43 us  [shards(): by_mode = lax.all_to_all(by_mode, cube, 0, 0, tiled=True)]
    pallas_call x1, Pallas kernels: 10.8 us -> 8.56 us  [shards(): pl.pallas_call(functools.partial(columns_kernel, straight, flipped, lists...]
  transfers between devices with their start and end apart: 11 -> 11, of which waited for: 5 -> 5; matrix products, arithmetic and copies ran while one was open for 2% -> 2% of each run, Pallas kernels for 12% -> 11%
where the time goes in v3:
time: 152 us; the launch traced here: 151 us
  waiting for transfers between devices  49.5 us (33%)
  Pallas kernels  36 us (24%)
  starting transfers between devices  33.6 us (22%)
  other arithmetic  18.6 us (12%)
  blocking collectives  11.1 us (7%)
  local copies, waits for them, and re-layouts  2.13 us (1%)
    all_to_all x1, waiting for transfers between devices, shards(): halves = lax.all_to_all(halves, cube, 0, 0, tiled=True)  26.4 us
    all_to_all x1, waiting for transfers between devices, shards(): by_mode = lax.all_to_all(by_mode, cube, 0, 0, tiled=True)  14.6 us
    pallas_call x1, Pallas kernels, shards(): pl.pallas_call(functools.partial(kicks_kernel, strips), out_shape=[kick_s...  11.4 us
    all_gather x1, blocking collectives, shards(): own = lax.all_gather(own, ('tx', 'dom'), axis=0)  11.1 us
    ppermute x1, starting transfers between devices, shards(): other = lax.ppermute(mine, ('q', 'hi'), other_route)  11 us
    pallas_call x1, Pallas kernels, shards(): pl.pallas_call(functools.partial(modes_kernel, strips), out_shape=jax.Sha...  10.3 us
    all_to_all x1, starting transfers between devices, shards(): by_mode = lax.all_to_all(by_mode, cube, 0, 0, tiled=True)  9.43 us
    pallas_call x1, Pallas kernels, shards(): pl.pallas_call(functools.partial(columns_kernel, straight, flipped, lists...  8.56 us
  transfers between devices with their start and end apart: 11, of which 5 were waited for; matrix products, arithmetic and copies ran while one was open for 2% of the time, Pallas kernels for 11%

profile of v3, /device:TPU:0, one launch (start us, length us, event | category | flops | bytes accessed | tf_op | source)
XLA Modules:
  0.0 151.2 jit_solution(1204862689695028690)
XLA Ops:
  0.0 1.5 %fusion.1 = s32[1,16384]{1,0:T(1,128)S(1)} fusion(pred[]{:T(512)S(6)} %ge.19, s32[1,16384]{1,0:T(1,128)} %param.14, s32[1,16384]{1,0:T(1,128)} %param.15, pred[]{:T(512)S(6)} %eq.16, s32[]{:T(128)S(6)} %mul.55, s32[]{:T(128)S(6)} %add.82), kind=kLoop, calls=%fused_computation.28 | loop fusion | flops 458752 | bytes 196618 | tf_op jit(solution)/shard_map/add | solution.py:457
  1.5 7.5 %sort.42 = (s32[16384]{0:T(1024)S(1)}, f32[16384]{0:T(1024)S(1)}, s32[16384]{0:T(1024)S(1)}) sort(s32[16384]{0:T(1024)S(1)} %bitcast.24, f32[16384]{0:T(1024)} %bitcast.31, s32[16384]{0:T(1024)S(1)} %iota.10), dimensions={0}, to_apply=%region_0.1 | sort | flops 229376 | bytes 393216 | tf_op jit(solution)/shard_map/sort | solution.py:458
  9.2 0.7 collective-permute-start
  10.3 11.0 %collective-permute-start.1 = (f32[2,128,128]{2,1,0:T(8,128)S(1)}, f32[2,128,128]{2,1,0:T(8,128)S(1)}, u32[]{:S(2)}, u32[]{:S(2)}) collective-permute-start(f32[2,128,128]{2,1,0:T(8,128)S(1)} %pad_maximum_fusion.2), channel_id=1, source_target_pairs={{0,4},{4,20},{16,0},{20,16},{1,5},{5,21},{17,1},{21,17},{2,6},{6,2... | collective-permute-start | bytes 393224 | tf_op jit(solution)/shard_map/ppermute | solution.py:467
  21.2 11.1 %all-gather = f32[12,128,128]{2,1,0:T(8,128)S(1)} all-gather(f32[3,128,128]{2,1,0:T(8,128)S(1)} %collective-permute-done), channel_id=2, replica_groups=mesh['q'=2,'tx'=2,'hi'=2,'lo'=2,'dom'=2] {'tx','dom'}, dimensions={0}, use_global_device_ids=true | all-gather | bytes 983040 | tf_op jit(solution)/shard_map/all_gather | solution.py:468
  32.4 1.9 %collective-permute-start.4 = (f32[2,128,128]{2,1,0:T(8,128)S(1)}, f32[2,128,128]{2,1,0:T(8,128)S(1)}, u32[]{:S(2)}, u32[]{:S(2)}) collective-permute-start(f32[2,128,128]{2,1,0:T(8,128)S(1)} %collective-permute-done.1), channel_id=1, source_target_pairs={{1,0},{0,1},{9,8},{8,9},{3,2},{2,3},{11,10},{10,11},{5,4},{4,5},{1... | collective-permute-start | bytes 393224 | tf_op jit(solution)/shard_map/ppermute | solution.py:471
  34.2 0.2 collective-permute-start.3
  34.5 1.5 collective-permute-start.2
  36.0 0.4 slice.19
  36.4 0.1 slice.18
  36.5 0.4 convert_reduce_fusion.2
  36.9 10.3 %modes.1 = f32[16,136,128]{2,1,0:T(8,128)} custom-call(s32[5]{0:T(128)S(1)} %pad_add_fusion.1.scalars, s32[4,2,32]{2,1,0:T(2,128)S(1)} %get-tuple-element.57.first, s32[4,2,32]{2,1,0:T(2,128)S(1)} %get-tuple-element.56.last, f32[4,4]{1,0:T(4,128)S(1)} %get-tuple-element.54.weights, f32[4,3,128,128]{3,2,1,0:T(8,128)S(1)} %bitcast.23, ...), custom_call_target="tpu_custom_call" | custom-call | tf_op jit(solution)/shard_map/modes/pallas_call | solution.py:502
  47.2 9.4 %all-to-all-start = ((f32[16,136,128]{2,1,0:T(8,128)}), f32[16,136,128]{2,1,0:T(8,128)S(1)}, u32[]{:S(2)}, u32[]{:S(2)}) async-start(f32[16,136,128]{2,1,0:T(8,128)} %modes.1), calls=%async_computation | async-start | bytes 2228224 | tf_op jit(solution)/shard_map/all_to_all | solution.py:518
  56.7 0.9 constant_dynamic-slice_fusion.mine
  57.5 14.6 %all-to-all-done.by_mode = f32[16,136,128]{2,1,0:T(8,128)S(1)} async-done(((f32[16,136,128]{2,1,0:T(8,128)}), f32[16,136,128]{2,1,0:T(8,128)S(1)}, u32[]{:S(2)}, u32[]{:S(2)}) %all-to-all-start) | async-done | bytes 1114144 | tf_op jit(solution)/shard_map/all_to_all | solution.py:518
  72.2 8.6 %columns.1 = f32[16,2,136,128]{3,2,1,0:T(8,128)} custom-call(f32[16,136,128]{2,1,0:T(8,128)S(1)} %all-to-all-done.by_mode, f32[2,1024]{1,0:T(2,128)S(1)} %copy-done.1, f32[2,1024]{1,0:T(2,128)S(1)} %copy-done, f32[128,2]{1,0:T(8,128)S(1)} %constant_dynamic-slice_fusion.mine, bf16[4,1024,1024]{2,1,0:T(8,128)(2,1)} %constant.156.clone.stored), custom_call_target="tpu_custom_call" | custom-call | tf_op jit(solution)/shard_map/columns/pallas_call | solution.py:526
  80.7 3.7 %all-to-all-start.1 = ((f32[16,2,136,128]{3,2,1,0:T(8,128)}), f32[16,2,136,128]{3,2,1,0:T(8,128)S(1)}, u32[]{:S(2)}, u32[]{:S(2)}) async-start(f32[16,2,136,128]{3,2,1,0:T(8,128)} %columns.1), calls=%async_computation.1 | async-start | bytes 4456448 | tf_op jit(solution)/shard_map/all_to_all | solution.py:535
  84.6 0.4 slice.21
  85.0 0.1 slice.20
  85.1 0.2 convert_reduce_fusion.last
  85.3 0.2 convert_reduce_fusion.1.first
  85.6 26.4 %all-to-all-done.1.halves = f32[16,2,136,128]{3,2,1,0:T(8,128)S(1)} async-done(((f32[16,2,136,128]{3,2,1,0:T(8,128)}), f32[16,2,136,128]{3,2,1,0:T(8,128)S(1)}, u32[]{:S(2)}, u32[]{:S(2)}) %all-to-all-start.1) | async-done | bytes 2228256 | tf_op jit(solution)/shard_map/all_to_all | solution.py:535
  111.9 11.4 %kicks.1 = (f32[2,16384]{1,0:T(2,128)S(1)}, f32[2,16384]{1,0:T(2,128)S(1)}, bf16[2,272,1280]{2,1,0:T(8,128)(2,1)S(1)}, bf16[2,272,1280]{2,1,0:T(8,128)(2,1)S(1)}) custom-call(s32[5]{0:T(128)S(1)} %pad_add_fusion.scalars, s32[4,2,32]{2,1,0:T(2,128)S(1)} %convert_reduce_fusion.1.first, s32[4,2,32]{2,1,0:T(2,128)S(1)} %convert_reduce_fusion.last, ...), custom_call_target="tpu_custom_call" | custom-call | tf_op jit(solution)/shard_map/kicks/pallas_call | solution.py:539
  123.4 3.6 %collective-permute-start.5 = (f32[2,16384]{1,0:T(2,128)S(1)}, f32[2,16384]{1,0:T(2,128)S(1)}, u32[]{:S(2)}, u32[]{:S(2)}) collective-permute-start(f32[2,16384]{1,0:T(2,128)S(1)} %get-tuple-element.37), channel_id=1, source_target_pairs={{4,9},{5,8},{12,1},{13,0},{20,13},{21,12},{28,5},{29,4},{0,25},{1,... | collective-permute-start | bytes 393224 | tf_op jit(solution)/shard_map/ppermute | solution.py:562
  127.0 5.8 %sample.1 = (f32[2,16384]{1,0:T(2,128)S(1)}, f32[2,16384]{1,0:T(2,128)S(1)}) custom-call(s32[5]{0:T(128)S(1)} %pad_add_fusion.scalars, s32[4,2,32]{2,1,0:T(2,128)S(1)} %convert_reduce_fusion.1.first, s32[4,2,32]{2,1,0:T(2,128)S(1)} %convert_reduce_fusion.last, f32[4,4]{1,0:T(4,128)S(1)} %get-tuple-element.53.weights, ...), custom_call_target="tpu_custom_call" | custom-call | tf_op jit(solution)/shard_map/sample/pallas_call | solution.py:548
  132.7 1.4 collective-permute-start.7
  134.1 0.2 collective-permute-start.8
  134.4 2.8 %collective-permute-done.6 = f32[2,16384]{1,0:T(2,128)S(1)} collective-permute-done((f32[2,16384]{1,0:T(2,128)S(1)}, f32[2,16384]{1,0:T(2,128)S(1)}, u32[]{:S(2)}, u32[]{:S(2)}) %collective-permute-start.6) | collective-permute-done | bytes 131104 | tf_op jit(solution)/shard_map/ppermute | solution.py:562
  137.1 5.2 %collective-permute-done.7 = f32[2,16384]{1,0:T(2,128)S(1)} collective-permute-done((f32[2,16384]{1,0:T(2,128)S(1)}, f32[2,16384]{1,0:T(2,128)S(1)}, u32[]{:S(2)}, u32[]{:S(2)}) %collective-permute-start.7) | collective-permute-done | bytes 131104 | tf_op jit(solution)/shard_map/ppermute | solution.py:562
  142.4 0.5 collective-permute-done.8
  143.1 7.3 %sort.43 = (s32[16384]{0:T(1024)}, f32[16384]{0:T(1024)S(1)}, f32[16384]{0:T(1024)S(1)}) sort(s32[16384]{0:T(1024)S(1)} %get-tuple-element.25, f32[16384]{0:T(1024)S(1)} %bitcast.26, f32[16384]{0:T(1024)S(1)} %bitcast.25), dimensions={0}, to_apply=%region_1.2 | sort | flops 229376 | bytes 393216 | tf_op jit(solution)/shard_map/sort | solution.py:566
  150.4 0.8 fusion
  (36 shorter events, 0.9 us)
Async XLA Ops:
  0.0 10.0 %copy-start.5 = (f32[1,2]{1,0:T(1,128)S(1)}, f32[1,2]{1,0:T(1,128)}, u32[]{:S(2)}) copy-start(f32[1,2]{1,0:T(1,128)} %constant.153.clone) | copy-start | bytes 28
  0.0 10.0 %copy-start.6 = (f32[1,2]{1,0:T(1,128)S(1)}, f32[1,2]{1,0:T(1,128)}, u32[]{:S(2)}) copy-start(f32[1,2]{1,0:T(1,128)} %constant.152.clone) | copy-start | bytes 28
  0.0 10.1 %copy-start.3 = (f32[2]{0:T(128)S(1)}, f32[2]{0:T(128)}, u32[]{:S(2)}) copy-start(f32[2]{0:T(128)} %constant.165) | copy-start | bytes 28
  0.0 10.1 %copy-start.4 = (f32[2]{0:T(128)S(1)}, f32[2]{0:T(128)}, u32[]{:S(2)}) copy-start(f32[2]{0:T(128)} %constant.164) | copy-start | bytes 28
  9.2 1.0 collective-permute-start
  10.3 22.1 %collective-permute-start.1 = (f32[2,128,128]{2,1,0:T(8,128)S(1)}, f32[2,128,128]{2,1,0:T(8,128)S(1)}, u32[]{:S(2)}, u32[]{:S(2)}) collective-permute-start(f32[2,128,128]{2,1,0:T(8,128)S(1)} %pad_maximum_fusion.2), channel_id=1, source_target_pairs={{0,4},{4,20},{16,0},{20,16},{1,5},{5,21},{17,1},{21,17},{2,6},{6,2... | collective-permute-start | bytes 393224 | tf_op jit(solution)/shard_map/ppermute | solution.py:467
  32.4 14.8 %collective-permute-start.4 = (f32[2,128,128]{2,1,0:T(8,128)S(1)}, f32[2,128,128]{2,1,0:T(8,128)S(1)}, u32[]{:S(2)}, u32[]{:S(2)}) collective-permute-start(f32[2,128,128]{2,1,0:T(8,128)S(1)} %collective-permute-done.1), channel_id=1, source_target_pairs={{1,0},{0,1},{9,8},{8,9},{3,2},{2,3},{11,10},{10,11},{5,4},{4,5},{1... | collective-permute-start | bytes 393224 | tf_op jit(solution)/shard_map/ppermute | solution.py:471
  34.2 13.0 %collective-permute-start.3 = (f32[2,128,128]{2,1,0:T(8,128)S(1)}, f32[2,128,128]{2,1,0:T(8,128)S(1)}, u32[]{:S(2)}, u32[]{:S(2)}) collective-permute-start(f32[2,128,128]{2,1,0:T(8,128)S(1)} %collective-permute-done.1), channel_id=1, source_target_pairs={{8,0},{9,1},{0,8},{1,9},{10,2},{11,3},{2,10},{3,11},{12,4},{13,5},... | collective-permute-start | bytes 393224 | tf_op jit(solution)/shard_map/ppermute | solution.py:471
  34.5 12.8 %collective-permute-start.2 = (f32[2,128,128]{2,1,0:T(8,128)S(1)}, f32[2,128,128]{2,1,0:T(8,128)S(1)}, u32[]{:S(2)}, u32[]{:S(2)}) collective-permute-start(f32[2,128,128]{2,1,0:T(8,128)S(1)} %collective-permute-done.1), channel_id=1, source_target_pairs={{9,0},{8,1},{1,8},{0,9},{11,2},{10,3},{3,10},{2,11},{13,4},{12,5},... | collective-permute-start | bytes 393224 | tf_op jit(solution)/shard_map/ppermute | solution.py:471
  47.2 25.0 %copy-start = (f32[2,1024]{1,0:T(2,128)S(1)}, f32[2,1024]{1,0:T(2,128)}, u32[]{:S(2)}) copy-start(f32[2,1024]{1,0:T(2,128)} %constant.159.clone.wave) | copy-start | bytes 24580
  47.2 25.0 %copy-start.1 = (f32[2,1024]{1,0:T(2,128)S(1)}, f32[2,1024]{1,0:T(2,128)}, u32[]{:S(2)}) copy-start(f32[2,1024]{1,0:T(2,128)} %constant.158.clone.lam) | copy-start | bytes 24580
  47.2 24.9 %all-to-all-start = ((f32[16,136,128]{2,1,0:T(8,128)}), f32[16,136,128]{2,1,0:T(8,128)S(1)}, u32[]{:S(2)}, u32[]{:S(2)}) async-start(f32[16,136,128]{2,1,0:T(8,128)} %modes.1), calls=%async_computation | async-start | bytes 2228224 | tf_op jit(solution)/shard_map/all_to_all | solution.py:518
  80.7 31.2 %all-to-all-start.1 = ((f32[16,2,136,128]{3,2,1,0:T(8,128)}), f32[16,2,136,128]{3,2,1,0:T(8,128)S(1)}, u32[]{:S(2)}, u32[]{:S(2)}) async-start(f32[16,2,136,128]{3,2,1,0:T(8,128)} %columns.1), calls=%async_computation.1 | async-start | bytes 4456448 | tf_op jit(solution)/shard_map/all_to_all | solution.py:535
  123.4 11.0 %collective-permute-start.5 = (f32[2,16384]{1,0:T(2,128)S(1)}, f32[2,16384]{1,0:T(2,128)S(1)}, u32[]{:S(2)}, u32[]{:S(2)}) collective-permute-start(f32[2,16384]{1,0:T(2,128)S(1)} %get-tuple-element.37), channel_id=1, source_target_pairs={{4,9},{5,8},{12,1},{13,0},{20,13},{21,12},{28,5},{29,4},{0,25},{1,... | collective-permute-start | bytes 393224 | tf_op jit(solution)/shard_map/ppermute | solution.py:562
  127.0 10.2 %collective-permute-start.6 = (f32[2,16384]{1,0:T(2,128)S(1)}, f32[2,16384]{1,0:T(2,128)S(1)}, u32[]{:S(2)}, u32[]{:S(2)}) collective-permute-start(f32[2,16384]{1,0:T(2,128)S(1)} %get-tuple-element.38), channel_id=1, source_target_pairs={{4,8},{5,9},{12,0},{13,1},{20,12},{21,13},{28,4},{29,5},{0,24},{1,... | collective-permute-start | bytes 393224 | tf_op jit(solution)/shard_map/ppermute | solution.py:562
  127.0 23.4 %copy-start.2 = (f32[1,2,16384]{2,1,0:T(2,128)S(1)}, f32[1,2,16384]{2,1,0:T(2,128)}, u32[]{:S(2)}) copy-start(f32[1,2,16384]{2,1,0:T(2,128)} %param.17) | copy-start | bytes 393220
  132.7 9.6 %collective-permute-start.7 = (f32[2,16384]{1,0:T(2,128)S(1)}, f32[2,16384]{1,0:T(2,128)S(1)}, u32[]{:S(2)}, u32[]{:S(2)}) collective-permute-start(f32[2,16384]{1,0:T(2,128)S(1)} %get-tuple-element.41), channel_id=1, source_target_pairs={{4,1},{5,0},{12,9},{13,8},{20,5},{21,4},{28,13},{29,12},{0,17},{1,... | collective-permute-start | bytes 393224 | tf_op jit(solution)/shard_map/ppermute | solution.py:562
  134.1 8.7 %collective-permute-start.8 = (f32[2,16384]{1,0:T(2,128)S(1)}, f32[2,16384]{1,0:T(2,128)S(1)}, u32[]{:S(2)}, u32[]{:S(2)}) collective-permute-start(f32[2,16384]{1,0:T(2,128)S(1)} %get-tuple-element.42), channel_id=1, source_target_pairs={{4,0},{5,1},{12,8},{13,9},{20,4},{21,5},{28,12},{29,13},{0,16},{1,... | collective-permute-start | bytes 393224 | tf_op jit(solution)/shard_map/ppermute | solution.py:562

commit v4 on v3

--- a/solution.py
+++ b/solution.py
@@ -100,7 +100,7 @@
     return (least, (most + 1 - least) // window + 1)
 
 
-def each_window(strips, scalars, first, last, group, item):
+def strip_blocks(strips, scalars, first, last, group):
     start = scalars[0]
 
     def bounds(turn, found):
@@ -112,7 +112,11 @@
             for which, (low, high) in zip(group, found, strict=True)
         )
 
-    found = lax.fori_loop(0, first.shape[2], bounds, tuple((0, 0) for _ in group))
+    return lax.fori_loop(0, first.shape[2], bounds, tuple((0, 0) for _ in group), unroll=8)
+
+
+def each_window(strips, scalars, first, last, group, found, item):
+    start = scalars[0]
     stride = max(4 // len(group), 1)
     turns = (functools.reduce(jnp.maximum, [high - low for low, high in found]) + stride - 1) // stride
     streams = [
@@ -185,7 +189,7 @@
         parts[place][half, :, pl.ds(at, window)] += both[:pad_cols] + both[tall : tall + pad_cols]
 
     for group in groups_of(count):
-        each_window(strips, scalars, first, last, group, item)
+        each_window(strips, scalars, first, last, group, strip_blocks(strips, scalars, first, last, group), item)
     for half in range(2):
         if count > 4:
             used = [part[half] for part in parts]
@@ -198,13 +202,17 @@
     return [pltpu.VMEM((2 if count > 4 else 1, *charge_shape[1:]), jnp.float32)] * min(count, 4)
 
 
-def sample_body(strips, scalars, first, last, weights, lists, field_high, field_low, kicks, begin):
-    pad_cols = field_high.shape[1] // 2
+def sample_start(strips, scalars, first, last, kicks, begin):
     for kick in kicks:
         kick[...] = jnp.zeros_like(kick)
+    groups = [tuple(begin + which for which in group) for group in groups_of(len(kicks))]
+    return [(group, strip_blocks(strips, scalars, first, last, group)) for group in groups]
+
+
+def sample_body(strips, scalars, first, last, weights, lists, field_high, field_low, kicks, begin, started):
+    pad_cols = field_high.shape[1] // 2
 
     def item(place, which, turn, at, valid):
-        here = pl.ds(pl.multiple_of(turn * block, block), block)
         half = scalars[1 + which]
         kick = kicks[which - begin]
         row, col = cells_of(strips, scalars, lists, which, turn, at, valid)
@@ -212,12 +220,13 @@
         fields = jnp.concatenate([field_high[half, :, pl.ds(at, window)], field_low[half, :, pl.ds(at, window)]], 1)
         near = dot(fields, jnp.concatenate([rows, rows], 0), ((1,), (0,)))
         cols = pair_weights(col.astype(jnp.float32), weights[which, 2], weights[which, 3], pad_cols)
-        kick[0:1, here] += jnp.sum(near[:pad_cols] * cols, axis=0, keepdims=True)
-        kick[1:2, here] += jnp.sum(near[pad_cols:] * cols, axis=0, keepdims=True)
-
-    for group in groups_of(len(kicks)):
-        group = tuple(begin + which for which in group)
-        each_window(strips, scalars, first, last, group, item)
+        for component, part in enumerate((near[:pad_cols], near[pad_cols:])):
+            total = jnp.sum(part * cols, axis=0, keepdims=True)
+            for i in range(block // 128):
+                kick[component, pl.ds(turn * (block // 128) + i, 1)] += total[:, i * 128 : (i + 1) * 128]
+
+    for group, found in started:
+        each_window(strips, scalars, first, last, group, found, item)
 
 
 def fetch(stored, tables, arrived, parts):
@@ -236,21 +245,30 @@
     return table
 
 
-def modes_kernel(strips, scalars, first, last, weights, lists, stored, by_mode, charge, tables, arrived, *parts):
+def modes_kernel(strips, scalars, first, last, weights, lists, stored, sent_modes, charge, tables, arrived, by_mode, sent, *parts):
     table = fetch(stored, tables, arrived, (0, 1))
     deposit_body(strips, scalars, first, last, weights, lists, charge, parts)
     devices, pad_cols, modes = by_mode.shape
     near, far = (charge[0, :, :HALF], charge[1, :, :HALF])
     high, low = table(0)
     both = jnp.concatenate([(near + far) * alternate((1, HALF), 1), near - far], 0)
-    done = dot_parts(high, low, both, ((1,), (0,)))
-    for turn in range(devices // 2):
-        here = slice(turn * modes, (turn + 1) * modes)
-        by_mode[turn] = done[:pad_cols, here]
-        by_mode[devices // 2 + turn] = done[pad_cols:, here]
-
-
-def columns_kernel(order, flipped, per_tile, strips, by_mode, lam, wave, mine, stored, halves, tables, arrived, back_x, back_y, sent):
+    copies = []
+    quarter = devices // 4
+    for part in range(2):
+        done = dot_parts(high[:, part * HALF // 2 : (part + 1) * HALF // 2], low[:, part * HALF // 2 : (part + 1) * HALF // 2], both, ((1,), (0,)))
+        for turn in range(quarter):
+            here = slice(turn * modes, (turn + 1) * modes)
+            by_mode[part * quarter + turn] = done[:pad_cols, here]
+            by_mode[devices // 2 + part * quarter + turn] = done[pad_cols:, here]
+        for parity in range(2):
+            here = pl.ds(parity * (devices // 2) + part * quarter, quarter)
+            copies.append(pltpu.make_async_copy(by_mode.at[here], sent_modes.at[here], sent.at[2 * part + parity]))
+            copies[-1].start()
+    for copy in copies:
+        copy.wait()
+
+
+def columns_kernel(order, flipped, per_tile, strips, by_mode, lam, wave, mine, stored, halves, tables, arrived, outgoing, sent):
     table = fetch(stored, tables, arrived, (0, 1, 2, 3))
     sine_parts = table(0)
     modes = by_mode.shape[2]
@@ -276,7 +294,9 @@
         hats[1].append((hat * wave[this, :]).T)
 
     copies = []
-    for component, (outgoing, sign) in enumerate(((back_x, 1), (back_y, -1))):
+    wide = 2 * strips
+    outgoing[:, wide:] = jnp.zeros((outgoing.shape[0], 8, modes), jnp.float32)
+    for component, sign in enumerate((1, -1)):
         hat = jnp.concatenate(hats[component], 1)
         hat_high = hat.astype(jnp.bfloat16)
         hat_both = jnp.concatenate([hat_high, (hat - hat_high.astype(jnp.float32)).astype(jnp.bfloat16)], 1)
@@ -293,12 +313,11 @@
                 for turn in range(piece_rows // strips):
                     place = piece * piece_rows // strips + turn
                     part = value[turn * strips : (turn + 1) * strips]
-                    outgoing[before + whose[place], :strips] = part
+                    outgoing[before + whose[place], component * strips : (component + 1) * strips] = part
                     if place % per_tile:
-                        outgoing[before + whose[place - 1], strips:] = part[:8]
-                    if place % per_tile == per_tile - 1:
-                        outgoing[before + whose[place], strips:] = jnp.zeros_like(part[:8])
-        copies.append(pltpu.make_async_copy(outgoing, halves.at[:, component], sent.at[component]))
+                        outgoing[before + whose[place - 1], wide + component : wide + component + 1] = part[:1]
+        here = pl.ds(0, strips) if component == 0 else pl.ds(strips, strips + 8)
+        copies.append(pltpu.make_async_copy(outgoing.at[:, here], halves.at[:, here], sent.at[component]))
         copies[-1].start()
     for copy in copies:
         copy.wait()
@@ -307,13 +326,18 @@
 def kicks_kernel(strips, scalars, first, last, weights, lists, halves, stored, *refs):
     kicks, (field_high, field_low, tables, arrived) = (refs[:-4], refs[-4:])
     table = fetch(stored, tables, arrived, (2, 3, 0, 1))
-    devices, _, pad_cols, _ = halves.shape
+    started = sample_start(strips, scalars, first, last, kicks, 0)
+    devices = halves.shape[0]
+    pad_cols = strips + 8
     wide = 2 * pad_cols
     fields = {}
     for component, sign in enumerate((-1, 1)):
-        sides = [
-            jnp.concatenate([halves[start + turn, component] for turn in range(devices // 2)], 1) for start in (0, devices // 2)
-        ]
+        sides = []
+        for start in (0, devices // 2):
+            for here in (slice(component * strips, (component + 1) * strips), slice(2 * strips, 2 * strips + 8)):
+                sides.append(jnp.concatenate([halves[start + turn, here] for turn in range(devices // 2)], 1))
+            after = jnp.broadcast_to(sides[-1][component : component + 1], sides[-1].shape)
+            sides[-1] = jnp.where(lax.broadcasted_iota(jnp.int32, after.shape, 0) == 0, after, 0.0)
         both = jnp.concatenate(sides, 0)
         done = 0.0
         for piece in range(pieces):
@@ -329,7 +353,7 @@
         beyond = jnp.zeros((wide, window), jnp.bfloat16)
         field_high[half, :, HALF:] = beyond
         field_low[half, :, HALF:] = beyond
-    sample_body(strips, scalars, first, last, weights, lists, field_high, field_low, kicks, 0)
+    sample_body(strips, scalars, first, last, weights, lists, field_high, field_low, kicks, 0, started)
 
 
 def block_ends(lists):
@@ -343,7 +367,8 @@
 
 
 def sample_alone(strips, begin, scalars, first, last, weights, lists, field_high, field_low, *kicks):
-    sample_body(strips, scalars, first, last, weights, lists, field_high, field_low, kicks, begin)
+    started = sample_start(strips, scalars, first, last, kicks, begin)
+    sample_body(strips, scalars, first, last, weights, lists, field_high, field_low, kicks, begin, started)
 
 
 def shifted(n_tx, n_dom, shift):
@@ -487,7 +512,7 @@
 
     to_deposit = (own_scalars, *block_ends(own), own_pairs, own)
     charge_shape = (2, pad_cols, HALF + window)
-    kick_shape = jax.ShapeDtypeStruct((2, count), jnp.float32)
+    kick_shape = jax.ShapeDtypeStruct((2, count // 128, 128), jnp.float32)
 
     angles = np.pi * (np.arange(GRID) + 1) / (2 * (GRID + 1))
     lam = (4.0 * np.sin(angles) ** 2).astype(np.float32)
@@ -498,16 +523,18 @@
         stored = jnp.asarray(folded_tables())
         anywhere = pl.BlockSpec(memory_space=pl.ANY)
         fetched = [pltpu.VMEM(stored.shape, stored.dtype), pltpu.SemaphoreType.DMA((4 * pieces,))]
-        outgoing = pltpu.VMEM((devices, pad_cols, modes), jnp.float32)
+        outgoing = pltpu.VMEM((devices, 2 * strips + 8, modes), jnp.float32)
         by_mode = pl.pallas_call(
             functools.partial(modes_kernel, strips),
             out_shape=jax.ShapeDtypeStruct((devices, pad_cols, modes), jnp.float32),
             in_specs=[smem] * 4 + [vmem, anywhere],
-            out_specs=vmem,
+            out_specs=anywhere,
             scratch_shapes=[
                 pltpu.VMEM(charge_shape, jnp.float32),
                 pltpu.VMEM((2, HALF, HALF), jnp.bfloat16),
                 fetched[1],
+                pltpu.VMEM((devices, pad_cols, modes), jnp.float32),
+                pltpu.SemaphoreType.DMA((4,)),
                 *deposit_parts(lists, charge_shape),
             ],
             compiler_params=params,
@@ -525,10 +552,10 @@
         flipped = [(j // n_dom * n_lo + n_lo - 1 - b) * n_dom + j % n_dom for b, j in natural]
         halves = pl.pallas_call(
             functools.partial(columns_kernel, straight, flipped, lists, strips),
-            out_shape=jax.ShapeDtypeStruct((devices, 2, pad_cols, modes), jnp.float32),
+            out_shape=jax.ShapeDtypeStruct(outgoing.shape, jnp.float32),
             in_specs=[vmem] * 4 + [anywhere],
             out_specs=anywhere,
-            scratch_shapes=[*fetched, outgoing, outgoing, pltpu.SemaphoreType.DMA((2,))],
+            scratch_shapes=[*fetched, outgoing, pltpu.SemaphoreType.DMA((2,))],
             compiler_params=pltpu.CompilerParams(vmem_limit_bytes=51 * 1024 * 1024),
             name="columns",
         )(by_mode, *(jnp.asarray(values[order_k].reshape(2, HALF)) for values in (lam, wave)), mine, stored)
@@ -563,7 +590,7 @@
         for kick, shift in zip(kicks, shifts, strict=True)
     ]
     kicks = functools.reduce(jnp.add, kicks)
-    _, kick_x, kick_y = lax.sort((order, kicks[0], kicks[1]), num_keys=1, is_stable=False)
+    _, kick_x, kick_y = lax.sort((order, kicks[0].reshape(-1), kicks[1].reshape(-1)), num_keys=1, is_stable=False)
     return momenta + kick_gain * jnp.stack([kick_x, kick_y])[None]
 
 

time: 152 us -> 150 us (0.987)
  no operation moved by 1% of the time
where the time goes in v4:
time: 150 us
  waiting for transfers between devices  49.9 us (33%)
  Pallas kernels  35.5 us (24%)
  starting transfers between devices  33 us (22%)
  other arithmetic  18.5 us (12%)
  blocking collectives  11.1 us (7%)
  local copies, waits for them, and re-layouts  2.04 us (1%)
    all_to_all x1, waiting for transfers between devices, shards(): halves = lax.all_to_all(halves, cube, 0, 0, tiled=True)  25.7 us
    all_to_all x1, waiting for transfers between devices, shards(): by_mode = lax.all_to_all(by_mode, cube, 0, 0, tiled=True)  14.6 us
    all_gather x1, blocking collectives, shards(): own = lax.all_gather(own, ('tx', 'dom'), axis=0)  11.1 us
    ppermute x1, starting transfers between devices, shards(): other = lax.ppermute(mine, ('q', 'hi'), other_route)  11 us
    pallas_call x1, Pallas kernels, shards(): pl.pallas_call(functools.partial(modes_kernel, strips), out_shape=jax.Sha...  10.7 us
    pallas_call x1, Pallas kernels, shards(): pl.pallas_call(functools.partial(kicks_kernel, strips), out_shape=[kick_s...  10.6 us
    ppermute x4, waiting for transfers between devices, shards(): lax.ppermute(kick, ('q', 'tx', 'hi', 'dom'), returned(other_route, n_tx,...  9.6 us
    pallas_call x1, Pallas kernels, shards(): pl.pallas_call(functools.partial(columns_kernel, straight, flipped, lists...  8.59 us
  transfers between devices with their start and end apart: 11, of which 5 were waited for; matrix products, arithmetic and copies ran while one was open for 2% of the time, Pallas kernels for 11%

profile of v4, /device:TPU:0, one launch (start us, length us, event | category | flops | bytes accessed | tf_op | source)
XLA Modules:
  0.0 150.3 jit_solution(8121525473303146305)
XLA Ops:
  0.0 1.5 %fusion.1 = s32[1,16384]{1,0:T(1,128)S(1)} fusion(pred[]{:T(512)S(6)} %ge.19, s32[1,16384]{1,0:T(1,128)} %param.14, s32[1,16384]{1,0:T(1,128)} %param.15, pred[]{:T(512)S(6)} %eq.16, s32[]{:T(128)S(6)} %mul.55, s32[]{:T(128)S(6)} %add.82), kind=kLoop, calls=%fused_computation.28 | loop fusion | flops 458752 | bytes 196618 | tf_op jit(solution)/shard_map/add | solution.py:482
  1.5 7.5 %sort.42 = (s32[16384]{0:T(1024)S(1)}, f32[16384]{0:T(1024)S(1)}, s32[16384]{0:T(1024)S(1)}) sort(s32[16384]{0:T(1024)S(1)} %bitcast.26, f32[16384]{0:T(1024)} %bitcast.31, s32[16384]{0:T(1024)S(1)} %iota.10), dimensions={0}, to_apply=%region_0.1 | sort | flops 229376 | bytes 393216 | tf_op jit(solution)/shard_map/sort | solution.py:483
  9.1 0.1 fusion.4
  9.2 0.7 collective-permute-start
  10.3 11.0 %collective-permute-start.1 = (f32[2,128,128]{2,1,0:T(8,128)S(1)}, f32[2,128,128]{2,1,0:T(8,128)S(1)}, u32[]{:S(2)}, u32[]{:S(2)}) collective-permute-start(f32[2,128,128]{2,1,0:T(8,128)S(1)} %pad_maximum_fusion.2), channel_id=1, source_target_pairs={{0,4},{4,20},{16,0},{20,16},{1,5},{5,21},{17,1},{21,17},{2,6},{6,2... | collective-permute-start | bytes 393224 | tf_op jit(solution)/shard_map/ppermute | solution.py:492
  21.2 11.1 %all-gather = f32[12,128,128]{2,1,0:T(8,128)S(1)} all-gather(f32[3,128,128]{2,1,0:T(8,128)S(1)} %collective-permute-done), channel_id=2, replica_groups=mesh['q'=2,'tx'=2,'hi'=2,'lo'=2,'dom'=2] {'tx','dom'}, dimensions={0}, use_global_device_ids=true | all-gather | bytes 983040 | tf_op jit(solution)/shard_map/all_gather | solution.py:493
  32.4 1.9 %collective-permute-start.4 = (f32[2,128,128]{2,1,0:T(8,128)S(1)}, f32[2,128,128]{2,1,0:T(8,128)S(1)}, u32[]{:S(2)}, u32[]{:S(2)}) collective-permute-start(f32[2,128,128]{2,1,0:T(8,128)S(1)} %collective-permute-done.1), channel_id=1, source_target_pairs={{1,0},{0,1},{9,8},{8,9},{3,2},{2,3},{11,10},{10,11},{5,4},{4,5},{1... | collective-permute-start | bytes 393224 | tf_op jit(solution)/shard_map/ppermute | solution.py:496
  34.2 0.2 collective-permute-start.3
  34.5 1.5 collective-permute-start.2
  36.0 0.4 slice.19
  36.4 0.2 slice.18
  36.5 0.4 convert_reduce_fusion.2
  36.9 10.7 %modes.1 = f32[16,136,128]{2,1,0:T(8,128)} custom-call(s32[5]{0:T(128)S(1)} %pad_add_fusion.1.scalars, s32[4,2,32]{2,1,0:T(2,128)S(1)} %get-tuple-element.57.first, s32[4,2,32]{2,1,0:T(2,128)S(1)} %get-tuple-element.56.last, f32[4,4]{1,0:T(4,128)S(1)} %get-tuple-element.54.weights, f32[4,3,128,128]{3,2,1,0:T(8,128)S(1)} %bitcast.25, ...), custom_call_target="tpu_custom_call" | custom-call | tf_op jit(solution)/shard_map/modes/pallas_call | solution.py:527
  47.7 8.2 %all-to-all-start = ((f32[16,136,128]{2,1,0:T(8,128)}), f32[16,136,128]{2,1,0:T(8,128)S(1)}, u32[]{:S(2)}, u32[]{:S(2)}) async-start(f32[16,136,128]{2,1,0:T(8,128)} %modes.1), calls=%async_computation | async-start | bytes 2228224 | tf_op jit(solution)/shard_map/all_to_all | solution.py:545
  55.9 0.9 constant_dynamic-slice_fusion.mine
  56.7 14.6 %all-to-all-done.by_mode = f32[16,136,128]{2,1,0:T(8,128)S(1)} async-done(((f32[16,136,128]{2,1,0:T(8,128)}), f32[16,136,128]{2,1,0:T(8,128)S(1)}, u32[]{:S(2)}, u32[]{:S(2)}) %all-to-all-start) | async-done | bytes 1114144 | tf_op jit(solution)/shard_map/all_to_all | solution.py:545
  71.4 8.6 %columns.1 = f32[16,264,128]{2,1,0:T(8,128)} custom-call(f32[16,136,128]{2,1,0:T(8,128)S(1)} %all-to-all-done.by_mode, f32[2,1024]{1,0:T(2,128)S(1)} %copy-done.1, f32[2,1024]{1,0:T(2,128)S(1)} %copy-done, f32[128,2]{1,0:T(8,128)S(1)} %constant_dynamic-slice_fusion.mine, bf16[4,1024,1024]{2,1,0:T(8,128)(2,1)} %constant.156.clone.stored), custom_call_target="tpu_custom_call" | custom-call | tf_op jit(solution)/shard_map/columns/pallas_call | solution.py:553
  80.0 3.7 %all-to-all-start.1 = ((f32[16,264,128]{2,1,0:T(8,128)}), f32[16,264,128]{2,1,0:T(8,128)S(1)}, u32[]{:S(2)}, u32[]{:S(2)}) async-start(f32[16,264,128]{2,1,0:T(8,128)} %columns.1), calls=%async_computation.1 | async-start | bytes 4325376 | tf_op jit(solution)/shard_map/all_to_all | solution.py:562
  83.8 0.4 slice.21
  84.2 0.1 slice.20
  84.4 0.2 convert_reduce_fusion.last
  84.6 0.2 convert_reduce_fusion.1.first
  84.8 25.7 %all-to-all-done.1.halves = f32[16,264,128]{2,1,0:T(8,128)S(1)} async-done(((f32[16,264,128]{2,1,0:T(8,128)}), f32[16,264,128]{2,1,0:T(8,128)S(1)}, u32[]{:S(2)}, u32[]{:S(2)}) %all-to-all-start.1) | async-done | bytes 2162720 | tf_op jit(solution)/shard_map/all_to_all | solution.py:562
  110.5 10.6 %kicks.1 = (f32[2,128,128]{2,1,0:T(8,128)S(1)}, f32[2,128,128]{2,1,0:T(8,128)S(1)}, bf16[2,272,1280]{2,1,0:T(8,128)(2,1)S(1)}, bf16[2,272,1280]{2,1,0:T(8,128)(2,1)S(1)}) custom-call(s32[5]{0:T(128)S(1)} %pad_add_fusion.scalars, s32[4,2,32]{2,1,0:T(2,128)S(1)} %convert_reduce_fusion.1.first, s32[4,2,32]{2,1,0:T(2,128)S(1)} %convert_reduce_fusion.last, ...), custom_call_target="tpu_custom_call" | custom-call | tf_op jit(solution)/shard_map/kicks/pallas_call | solution.py:566
  121.1 5.6 %collective-permute-start.5 = (f32[2,128,128]{2,1,0:T(8,128)S(1)}, f32[2,128,128]{2,1,0:T(8,128)S(1)}, u32[]{:S(2)}, u32[]{:S(2)}) collective-permute-start(f32[2,128,128]{2,1,0:T(8,128)S(1)} %get-tuple-element.37), channel_id=1, source_target_pairs={{4,9},{5,8},{12,1},{13,0},{20,13},{21,12},{28,5},{29,4},{0,25},{1,... | collective-permute-start | bytes 393224 | tf_op jit(solution)/shard_map/ppermute | solution.py:589
  126.6 5.5 %sample.1 = (f32[2,128,128]{2,1,0:T(8,128)S(1)}, f32[2,128,128]{2,1,0:T(8,128)S(1)}) custom-call(s32[5]{0:T(128)S(1)} %pad_add_fusion.scalars, s32[4,2,32]{2,1,0:T(2,128)S(1)} %convert_reduce_fusion.1.first, s32[4,2,32]{2,1,0:T(2,128)S(1)} %convert_reduce_fusion.last, f32[4,4]{1,0:T(4,128)S(1)} %get-tuple-element.53.weights, ...), custom_call_target="tpu_custom_call" | custom-call | tf_op jit(solution)/shard_map/sample/pallas_call | solution.py:575
  132.2 0.3 collective-permute-start.7
  132.6 2.4 %collective-permute-done.6 = f32[2,128,128]{2,1,0:T(8,128)S(1)} collective-permute-done((f32[2,128,128]{2,1,0:T(8,128)S(1)}, f32[2,128,128]{2,1,0:T(8,128)S(1)}, u32[]{:S(2)}, u32[]{:S(2)}) %collective-permute-start.6) | collective-permute-done | bytes 131104 | tf_op jit(solution)/shard_map/ppermute | solution.py:589
  135.0 6.0 %collective-permute-done.7 = f32[2,128,128]{2,1,0:T(8,128)S(1)} collective-permute-done((f32[2,128,128]{2,1,0:T(8,128)S(1)}, f32[2,128,128]{2,1,0:T(8,128)S(1)}, u32[]{:S(2)}, u32[]{:S(2)}) %collective-permute-start.7) | collective-permute-done | bytes 131104 | tf_op jit(solution)/shard_map/ppermute | solution.py:589
  141.0 1.1 collective-permute-done.8
  142.2 7.3 %sort.43 = (s32[16384]{0:T(1024)}, f32[16384]{0:T(1024)S(1)}, f32[16384]{0:T(1024)S(1)}) sort(s32[16384]{0:T(1024)S(1)} %get-tuple-element.25, f32[16384]{0:T(1024)S(1)} %get-tuple-element.48, f32[16384]{0:T(1024)S(1)} %get-tuple-element.47), dimensions={0}, to_apply=%region_1.2 | sort | flops 229376 | bytes 393216 | tf_op jit(solution)/shard_map/sort | solution.py:593
  149.5 0.8 fusion
  (36 shorter events, 0.6 us)
Async XLA Ops:
  0.0 10.0 %copy-start.5 = (f32[1,2]{1,0:T(1,128)S(1)}, f32[1,2]{1,0:T(1,128)}, u32[]{:S(2)}) copy-start(f32[1,2]{1,0:T(1,128)} %constant.153.clone) | copy-start | bytes 28
  0.0 10.0 %copy-start.6 = (f32[1,2]{1,0:T(1,128)S(1)}, f32[1,2]{1,0:T(1,128)}, u32[]{:S(2)}) copy-start(f32[1,2]{1,0:T(1,128)} %constant.152.clone) | copy-start | bytes 28
  0.0 10.1 %copy-start.3 = (f32[2]{0:T(128)S(1)}, f32[2]{0:T(128)}, u32[]{:S(2)}) copy-start(f32[2]{0:T(128)} %constant.165) | copy-start | bytes 28
  0.0 10.1 %copy-start.4 = (f32[2]{0:T(128)S(1)}, f32[2]{0:T(128)}, u32[]{:S(2)}) copy-start(f32[2]{0:T(128)} %constant.164) | copy-start | bytes 28
  9.2 1.0 collective-permute-start
  10.3 22.1 %collective-permute-start.1 = (f32[2,128,128]{2,1,0:T(8,128)S(1)}, f32[2,128,128]{2,1,0:T(8,128)S(1)}, u32[]{:S(2)}, u32[]{:S(2)}) collective-permute-start(f32[2,128,128]{2,1,0:T(8,128)S(1)} %pad_maximum_fusion.2), channel_id=1, source_target_pairs={{0,4},{4,20},{16,0},{20,16},{1,5},{5,21},{17,1},{21,17},{2,6},{6,2... | collective-permute-start | bytes 393224 | tf_op jit(solution)/shard_map/ppermute | solution.py:492
  32.4 15.3 %collective-permute-start.4 = (f32[2,128,128]{2,1,0:T(8,128)S(1)}, f32[2,128,128]{2,1,0:T(8,128)S(1)}, u32[]{:S(2)}, u32[]{:S(2)}) collective-permute-start(f32[2,128,128]{2,1,0:T(8,128)S(1)} %collective-permute-done.1), channel_id=1, source_target_pairs={{1,0},{0,1},{9,8},{8,9},{3,2},{2,3},{11,10},{10,11},{5,4},{4,5},{1... | collective-permute-start | bytes 393224 | tf_op jit(solution)/shard_map/ppermute | solution.py:496
  34.2 13.5 %collective-permute-start.3 = (f32[2,128,128]{2,1,0:T(8,128)S(1)}, f32[2,128,128]{2,1,0:T(8,128)S(1)}, u32[]{:S(2)}, u32[]{:S(2)}) collective-permute-start(f32[2,128,128]{2,1,0:T(8,128)S(1)} %collective-permute-done.1), channel_id=1, source_target_pairs={{8,0},{9,1},{0,8},{1,9},{10,2},{11,3},{2,10},{3,11},{12,4},{13,5},... | collective-permute-start | bytes 393224 | tf_op jit(solution)/shard_map/ppermute | solution.py:496
  34.5 13.2 %collective-permute-start.2 = (f32[2,128,128]{2,1,0:T(8,128)S(1)}, f32[2,128,128]{2,1,0:T(8,128)S(1)}, u32[]{:S(2)}, u32[]{:S(2)}) collective-permute-start(f32[2,128,128]{2,1,0:T(8,128)S(1)} %collective-permute-done.1), channel_id=1, source_target_pairs={{9,0},{8,1},{1,8},{0,9},{11,2},{10,3},{3,10},{2,11},{13,4},{12,5},... | collective-permute-start | bytes 393224 | tf_op jit(solution)/shard_map/ppermute | solution.py:496
  47.7 23.7 %copy-start = (f32[2,1024]{1,0:T(2,128)S(1)}, f32[2,1024]{1,0:T(2,128)}, u32[]{:S(2)}) copy-start(f32[2,1024]{1,0:T(2,128)} %constant.159.clone.wave) | copy-start | bytes 24580
  47.7 23.7 %copy-start.1 = (f32[2,1024]{1,0:T(2,128)S(1)}, f32[2,1024]{1,0:T(2,128)}, u32[]{:S(2)}) copy-start(f32[2,1024]{1,0:T(2,128)} %constant.158.clone.lam) | copy-start | bytes 24580
  47.7 23.6 %all-to-all-start = ((f32[16,136,128]{2,1,0:T(8,128)}), f32[16,136,128]{2,1,0:T(8,128)S(1)}, u32[]{:S(2)}, u32[]{:S(2)}) async-start(f32[16,136,128]{2,1,0:T(8,128)} %modes.1), calls=%async_computation | async-start | bytes 2228224 | tf_op jit(solution)/shard_map/all_to_all | solution.py:545
  80.0 30.5 %all-to-all-start.1 = ((f32[16,264,128]{2,1,0:T(8,128)}), f32[16,264,128]{2,1,0:T(8,128)S(1)}, u32[]{:S(2)}, u32[]{:S(2)}) async-start(f32[16,264,128]{2,1,0:T(8,128)} %columns.1), calls=%async_computation.1 | async-start | bytes 4325376 | tf_op jit(solution)/shard_map/all_to_all | solution.py:562
  121.1 11.5 %collective-permute-start.5 = (f32[2,128,128]{2,1,0:T(8,128)S(1)}, f32[2,128,128]{2,1,0:T(8,128)S(1)}, u32[]{:S(2)}, u32[]{:S(2)}) collective-permute-start(f32[2,128,128]{2,1,0:T(8,128)S(1)} %get-tuple-element.37), channel_id=1, source_target_pairs={{4,9},{5,8},{12,1},{13,0},{20,13},{21,12},{28,5},{29,4},{0,25},{1,... | collective-permute-start | bytes 393224 | tf_op jit(solution)/shard_map/ppermute | solution.py:589
  126.6 8.4 %collective-permute-start.6 = (f32[2,128,128]{2,1,0:T(8,128)S(1)}, f32[2,128,128]{2,1,0:T(8,128)S(1)}, u32[]{:S(2)}, u32[]{:S(2)}) collective-permute-start(f32[2,128,128]{2,1,0:T(8,128)S(1)} %get-tuple-element.38), channel_id=1, source_target_pairs={{4,8},{5,9},{12,0},{13,1},{20,12},{21,13},{28,4},{29,5},{0,24},{1,... | collective-permute-start | bytes 393224 | tf_op jit(solution)/shard_map/ppermute | solution.py:589
  126.6 22.9 %copy-start.2 = (f32[1,2,16384]{2,1,0:T(2,128)S(1)}, f32[1,2,16384]{2,1,0:T(2,128)}, u32[]{:S(2)}) copy-start(f32[1,2,16384]{2,1,0:T(2,128)} %param.17) | copy-start | bytes 393220
  132.2 8.8 %collective-permute-start.7 = (f32[2,128,128]{2,1,0:T(8,128)S(1)}, f32[2,128,128]{2,1,0:T(8,128)S(1)}, u32[]{:S(2)}, u32[]{:S(2)}) collective-permute-start(f32[2,128,128]{2,1,0:T(8,128)S(1)} %get-tuple-element.41), channel_id=1, source_target_pairs={{4,1},{5,0},{12,9},{13,8},{20,5},{21,4},{28,13},{29,12},{0,17},{1,... | collective-permute-start | bytes 393224 | tf_op jit(solution)/shard_map/ppermute | solution.py:589
  132.5 9.7 %collective-permute-start.8 = (f32[2,128,128]{2,1,0:T(8,128)S(1)}, f32[2,128,128]{2,1,0:T(8,128)S(1)}, u32[]{:S(2)}, u32[]{:S(2)}) collective-permute-start(f32[2,128,128]{2,1,0:T(8,128)S(1)} %get-tuple-element.42), channel_id=1, source_target_pairs={{4,0},{5,1},{12,8},{13,9},{20,4},{21,5},{28,12},{29,13},{0,16},{1,... | collective-permute-start | bytes 393224 | tf_op jit(solution)/shard_map/ppermute | solution.py:589

commit v5 on v4

--- a/solution.py
+++ b/solution.py
@@ -476,13 +476,15 @@
     count = cell_row.shape[1]
     q, hi, lo, tx, dom = (lax.axis_index(name) for name in ("q", "hi", "lo", "tx", "dom"))
 
-    row, col, amount = (cell_row, cell_col, weights[0])
+    row, col = lax.optimization_barrier((cell_row.reshape(-1, 128), cell_col.reshape(-1, 128)))
+    amount = weights[0]
     row = jnp.where(tx >= n_tx // 2, (n_tx - 1 - tx) * tile_rows + (tile_rows - 2) - row, tx * tile_rows + row)
     col = jnp.where(hi == 1, tile_cols - 2 - col, col)
-    key = (col // strips * HALF + row) * strips + col % strips
+    strip_bits = strips.bit_length() - 1
+    key = ((lax.shift_right_logical(col, strip_bits) * HALF + row) << strip_bits) + (col & (strips - 1))
     key, amount, order = lax.sort((key.reshape(-1), amount, lax.iota(jnp.int32, count)), num_keys=1, is_stable=False)
-    row = (key // strips) % HALF
-    col = key // (strips * HALF) * strips + key % strips
+    row = lax.shift_right_logical(key, strip_bits) & (HALF - 1)
+    col = (key // (strips * HALF) << strip_bits) + (key & (strips - 1))
     row, col, amount = (values.astype(jnp.float32).reshape(-1, 128) for values in (row, col, amount))
 
     own_route = [(b * 2 + t, t * 2 + b) for b in range(2) for t in range(2)]

time: 150 us -> 150 us (level)
    add x1 -> x0, other arithmetic: 1.52 us -> none  [shards(): key = (col // strips * HALF + row) * strips + col % strips]
  transfers between devices with their start and end apart: 11 -> 11, of which waited for: 5 -> 5; matrix products, arithmetic and copies ran while one was open for 2% -> 2% of each run, Pallas kernels for 11% -> 10%
where the time goes in v5:
time: 150 us
  waiting for transfers between devices  49.1 us (33%)
  Pallas kernels  34.8 us (23%)
  starting transfers between devices  34.4 us (23%)
  other arithmetic  17.9 us (12%)
  blocking collectives  11.1 us (7%)
  local copies, waits for them, and re-layouts  2.04 us (1%)
    all_to_all x1, waiting for transfers between devices, shards(): halves = lax.all_to_all(halves, cube, 0, 0, tiled=True)  25.7 us
    all_to_all x1, waiting for transfers between devices, shards(): by_mode = lax.all_to_all(by_mode, cube, 0, 0, tiled=True)  14.6 us
    all_gather x1, blocking collectives, shards(): own = lax.all_gather(own, ('tx', 'dom'), axis=0)  11.1 us
    ppermute x1, starting transfers between devices, shards(): other = lax.ppermute(mine, ('q', 'hi'), other_route)  11 us
    pallas_call x1, Pallas kernels, shards(): pl.pallas_call(functools.partial(kicks_kernel, strips), out_shape=[kick_s...  10.6 us
    pallas_call x1, Pallas kernels, shards(): pl.pallas_call(functools.partial(modes_kernel, strips), out_shape=jax.Sha...  10.5 us
    ppermute x4, waiting for transfers between devices, shards(): lax.ppermute(kick, ('q', 'tx', 'hi', 'dom'), returned(other_route, n_tx,...  8.86 us
    all_to_all x1, starting transfers between devices, shards(): by_mode = lax.all_to_all(by_mode, cube, 0, 0, tiled=True)  8.73 us
  transfers between devices with their start and end apart: 11, of which 5 were waited for; matrix products, arithmetic and copies ran while one was open for 2% of the time, Pallas kernels for 10%

profile of v5, /device:TPU:0, one launch (start us, length us, event | category | flops | bytes accessed | tf_op | source)
XLA Modules:
  0.0 149.7 jit_solution(6341606658681981992)
XLA Ops:
  0.0 1.0 add_bitcast_fusion
  1.0 7.5 %sort.42 = (s32[16384]{0:T(1024)S(1)}, f32[16384]{0:T(1024)S(1)}, s32[16384]{0:T(1024)S(1)}) sort(s32[16384]{0:T(1024)S(1)} %add_bitcast_fusion, f32[16384]{0:T(1024)} %bitcast.35, s32[16384]{0:T(1024)S(1)} %iota.10), dimensions={0}, to_apply=%region_0.1 | sort | flops 229376 | bytes 393216 | tf_op jit(solution)/shard_map/sort | solution.py:485
  8.6 0.7 collective-permute-start
  9.4 0.1 fusion.10
  9.6 11.0 %collective-permute-start.1 = (f32[2,128,128]{2,1,0:T(8,128)S(1)}, f32[2,128,128]{2,1,0:T(8,128)S(1)}, u32[]{:S(2)}, u32[]{:S(2)}) collective-permute-start(f32[2,128,128]{2,1,0:T(8,128)S(1)} %pad_maximum_fusion.2), channel_id=1, source_target_pairs={{0,4},{4,20},{16,0},{20,16},{1,5},{5,21},{17,1},{21,17},{2,6},{6,2... | collective-permute-start | bytes 393224 | tf_op jit(solution)/shard_map/ppermute | solution.py:494
  20.6 11.1 %all-gather = f32[12,128,128]{2,1,0:T(8,128)S(1)} all-gather(f32[3,128,128]{2,1,0:T(8,128)S(1)} %collective-permute-done), channel_id=2, replica_groups=mesh['q'=2,'tx'=2,'hi'=2,'lo'=2,'dom'=2] {'tx','dom'}, dimensions={0}, use_global_device_ids=true | all-gather | bytes 983040 | tf_op jit(solution)/shard_map/all_gather | solution.py:495
  31.7 1.9 %collective-permute-start.4 = (f32[2,128,128]{2,1,0:T(8,128)S(1)}, f32[2,128,128]{2,1,0:T(8,128)S(1)}, u32[]{:S(2)}, u32[]{:S(2)}) collective-permute-start(f32[2,128,128]{2,1,0:T(8,128)S(1)} %collective-permute-done.1), channel_id=1, source_target_pairs={{1,0},{0,1},{9,8},{8,9},{3,2},{2,3},{11,10},{10,11},{5,4},{4,5},{1... | collective-permute-start | bytes 393224 | tf_op jit(solution)/shard_map/ppermute | solution.py:498
  33.6 0.2 collective-permute-start.3
  33.8 1.5 collective-permute-start.2
  35.4 0.4 slice.19
  35.8 0.2 slice.18
  35.9 0.4 convert_reduce_fusion.2
  36.3 10.5 %modes.1 = f32[16,136,128]{2,1,0:T(8,128)} custom-call(s32[5]{0:T(128)S(1)} %pad_add_fusion.1.scalars, s32[4,2,32]{2,1,0:T(2,128)S(1)} %get-tuple-element.61.first, s32[4,2,32]{2,1,0:T(2,128)S(1)} %get-tuple-element.60.last, f32[4,4]{1,0:T(4,128)S(1)} %get-tuple-element.58.weights, f32[4,3,128,128]{3,2,1,0:T(8,128)S(1)} %bitcast.28, ...), custom_call_target="tpu_custom_call" | custom-call | tf_op jit(solution)/shard_map/modes/pallas_call | solution.py:529
  46.8 8.7 %all-to-all-start = ((f32[16,136,128]{2,1,0:T(8,128)}), f32[16,136,128]{2,1,0:T(8,128)S(1)}, u32[]{:S(2)}, u32[]{:S(2)}) async-start(f32[16,136,128]{2,1,0:T(8,128)} %modes.1), calls=%async_computation | async-start | bytes 2228224 | tf_op jit(solution)/shard_map/all_to_all | solution.py:547
  55.6 0.9 constant_dynamic-slice_fusion.mine
  56.4 14.6 %all-to-all-done.by_mode = f32[16,136,128]{2,1,0:T(8,128)S(1)} async-done(((f32[16,136,128]{2,1,0:T(8,128)}), f32[16,136,128]{2,1,0:T(8,128)S(1)}, u32[]{:S(2)}, u32[]{:S(2)}) %all-to-all-start) | async-done | bytes 1114144 | tf_op jit(solution)/shard_map/all_to_all | solution.py:547
  71.0 8.6 %columns.1 = f32[16,264,128]{2,1,0:T(8,128)} custom-call(f32[16,136,128]{2,1,0:T(8,128)S(1)} %all-to-all-done.by_mode, f32[2,1024]{1,0:T(2,128)S(1)} %copy-done.1, f32[2,1024]{1,0:T(2,128)S(1)} %copy-done, f32[128,2]{1,0:T(8,128)S(1)} %constant_dynamic-slice_fusion.mine, bf16[4,1024,1024]{2,1,0:T(8,128)(2,1)} %constant.115.clone.stored), custom_call_target="tpu_custom_call" | custom-call | tf_op jit(solution)/shard_map/columns/pallas_call | solution.py:555
  79.6 3.7 %all-to-all-start.1 = ((f32[16,264,128]{2,1,0:T(8,128)}), f32[16,264,128]{2,1,0:T(8,128)S(1)}, u32[]{:S(2)}, u32[]{:S(2)}) async-start(f32[16,264,128]{2,1,0:T(8,128)} %columns.1), calls=%async_computation.1 | async-start | bytes 4325376 | tf_op jit(solution)/shard_map/all_to_all | solution.py:564
  83.5 0.4 slice.21
  83.9 0.1 slice.20
  84.0 0.2 convert_reduce_fusion.last
  84.3 0.2 convert_reduce_fusion.1.first
  84.5 25.7 %all-to-all-done.1.halves = f32[16,264,128]{2,1,0:T(8,128)S(1)} async-done(((f32[16,264,128]{2,1,0:T(8,128)}), f32[16,264,128]{2,1,0:T(8,128)S(1)}, u32[]{:S(2)}, u32[]{:S(2)}) %all-to-all-start.1) | async-done | bytes 2162720 | tf_op jit(solution)/shard_map/all_to_all | solution.py:564
  110.1 10.6 %kicks.1 = (f32[2,128,128]{2,1,0:T(8,128)S(1)}, f32[2,128,128]{2,1,0:T(8,128)S(1)}, bf16[2,272,1280]{2,1,0:T(8,128)(2,1)S(1)}, bf16[2,272,1280]{2,1,0:T(8,128)(2,1)S(1)}) custom-call(s32[5]{0:T(128)S(1)} %pad_add_fusion.scalars, s32[4,2,32]{2,1,0:T(2,128)S(1)} %convert_reduce_fusion.1.first, s32[4,2,32]{2,1,0:T(2,128)S(1)} %convert_reduce_fusion.last, ...), custom_call_target="tpu_custom_call" | custom-call | tf_op jit(solution)/shard_map/kicks/pallas_call | solution.py:568
  120.8 3.7 %collective-permute-start.5 = (f32[2,128,128]{2,1,0:T(8,128)S(1)}, f32[2,128,128]{2,1,0:T(8,128)S(1)}, u32[]{:S(2)}, u32[]{:S(2)}) collective-permute-start(f32[2,128,128]{2,1,0:T(8,128)S(1)} %get-tuple-element.41), channel_id=1, source_target_pairs={{4,9},{5,8},{12,1},{13,0},{20,13},{21,12},{28,5},{29,4},{0,25},{1,... | collective-permute-start | bytes 393224 | tf_op jit(solution)/shard_map/ppermute | solution.py:591
  124.5 5.2 %sample.1 = (f32[2,128,128]{2,1,0:T(8,128)S(1)}, f32[2,128,128]{2,1,0:T(8,128)S(1)}) custom-call(s32[5]{0:T(128)S(1)} %pad_add_fusion.scalars, s32[4,2,32]{2,1,0:T(2,128)S(1)} %convert_reduce_fusion.1.first, s32[4,2,32]{2,1,0:T(2,128)S(1)} %convert_reduce_fusion.last, f32[4,4]{1,0:T(4,128)S(1)} %get-tuple-element.57.weights, ...), custom_call_target="tpu_custom_call" | custom-call | tf_op jit(solution)/shard_map/sample/pallas_call | solution.py:577
  129.7 3.0 %collective-permute-start.7 = (f32[2,128,128]{2,1,0:T(8,128)S(1)}, f32[2,128,128]{2,1,0:T(8,128)S(1)}, u32[]{:S(2)}, u32[]{:S(2)}) collective-permute-start(f32[2,128,128]{2,1,0:T(8,128)S(1)} %get-tuple-element.45), channel_id=1, source_target_pairs={{4,1},{5,0},{12,9},{13,8},{20,5},{21,4},{28,13},{29,12},{0,17},{1,... | collective-permute-start | bytes 393224 | tf_op jit(solution)/shard_map/ppermute | solution.py:591
  132.6 1.7 %collective-permute-done.6 = f32[2,128,128]{2,1,0:T(8,128)S(1)} collective-permute-done((f32[2,128,128]{2,1,0:T(8,128)S(1)}, f32[2,128,128]{2,1,0:T(8,128)S(1)}, u32[]{:S(2)}, u32[]{:S(2)}) %collective-permute-start.6) | collective-permute-done | bytes 131104 | tf_op jit(solution)/shard_map/ppermute | solution.py:591
  134.3 6.0 %collective-permute-done.7 = f32[2,128,128]{2,1,0:T(8,128)S(1)} collective-permute-done((f32[2,128,128]{2,1,0:T(8,128)S(1)}, f32[2,128,128]{2,1,0:T(8,128)S(1)}, u32[]{:S(2)}, u32[]{:S(2)}) %collective-permute-start.7) | collective-permute-done | bytes 131104 | tf_op jit(solution)/shard_map/ppermute | solution.py:591
  140.3 1.2 collective-permute-done.8
  141.6 7.3 %sort.43 = (s32[16384]{0:T(1024)}, f32[16384]{0:T(1024)S(1)}, f32[16384]{0:T(1024)S(1)}) sort(s32[16384]{0:T(1024)S(1)} %get-tuple-element.29, f32[16384]{0:T(1024)S(1)} %get-tuple-element.52, f32[16384]{0:T(1024)S(1)} %get-tuple-element.51), dimensions={0}, to_apply=%region_1.2 | sort | flops 229376 | bytes 393216 | tf_op jit(solution)/shard_map/sort | solution.py:595
  148.9 0.8 fusion
  (36 shorter events, 0.5 us)
Async XLA Ops:
  0.0 9.3 %copy-start.5 = (f32[1,2]{1,0:T(1,128)S(1)}, f32[1,2]{1,0:T(1,128)}, u32[]{:S(2)}) copy-start(f32[1,2]{1,0:T(1,128)} %constant.112.clone) | copy-start | bytes 28
  0.0 9.3 %copy-start.6 = (f32[1,2]{1,0:T(1,128)S(1)}, f32[1,2]{1,0:T(1,128)}, u32[]{:S(2)}) copy-start(f32[1,2]{1,0:T(1,128)} %constant.111.clone) | copy-start | bytes 28
  0.0 9.5 %copy-start.3 = (f32[2]{0:T(128)S(1)}, f32[2]{0:T(128)}, u32[]{:S(2)}) copy-start(f32[2]{0:T(128)} %constant.124) | copy-start | bytes 28
  0.0 9.5 %copy-start.4 = (f32[2]{0:T(128)S(1)}, f32[2]{0:T(128)}, u32[]{:S(2)}) copy-start(f32[2]{0:T(128)} %constant.123) | copy-start | bytes 28
  8.6 1.0 collective-permute-start
  9.6 22.1 %collective-permute-start.1 = (f32[2,128,128]{2,1,0:T(8,128)S(1)}, f32[2,128,128]{2,1,0:T(8,128)S(1)}, u32[]{:S(2)}, u32[]{:S(2)}) collective-permute-start(f32[2,128,128]{2,1,0:T(8,128)S(1)} %pad_maximum_fusion.2), channel_id=1, source_target_pairs={{0,4},{4,20},{16,0},{20,16},{1,5},{5,21},{17,1},{21,17},{2,6},{6,2... | collective-permute-start | bytes 393224 | tf_op jit(solution)/shard_map/ppermute | solution.py:494
  31.7 15.0 %collective-permute-start.4 = (f32[2,128,128]{2,1,0:T(8,128)S(1)}, f32[2,128,128]{2,1,0:T(8,128)S(1)}, u32[]{:S(2)}, u32[]{:S(2)}) collective-permute-start(f32[2,128,128]{2,1,0:T(8,128)S(1)} %collective-permute-done.1), channel_id=1, source_target_pairs={{1,0},{0,1},{9,8},{8,9},{3,2},{2,3},{11,10},{10,11},{5,4},{4,5},{1... | collective-permute-start | bytes 393224 | tf_op jit(solution)/shard_map/ppermute | solution.py:498
  33.6 13.2 %collective-permute-start.3 = (f32[2,128,128]{2,1,0:T(8,128)S(1)}, f32[2,128,128]{2,1,0:T(8,128)S(1)}, u32[]{:S(2)}, u32[]{:S(2)}) collective-permute-start(f32[2,128,128]{2,1,0:T(8,128)S(1)} %collective-permute-done.1), channel_id=1, source_target_pairs={{8,0},{9,1},{0,8},{1,9},{10,2},{11,3},{2,10},{3,11},{12,4},{13,5},... | collective-permute-start | bytes 393224 | tf_op jit(solution)/shard_map/ppermute | solution.py:498
  33.8 13.0 %collective-permute-start.2 = (f32[2,128,128]{2,1,0:T(8,128)S(1)}, f32[2,128,128]{2,1,0:T(8,128)S(1)}, u32[]{:S(2)}, u32[]{:S(2)}) collective-permute-start(f32[2,128,128]{2,1,0:T(8,128)S(1)} %collective-permute-done.1), channel_id=1, source_target_pairs={{9,0},{8,1},{1,8},{0,9},{11,2},{10,3},{3,10},{2,11},{13,4},{12,5},... | collective-permute-start | bytes 393224 | tf_op jit(solution)/shard_map/ppermute | solution.py:498
  46.8 24.3 %copy-start = (f32[2,1024]{1,0:T(2,128)S(1)}, f32[2,1024]{1,0:T(2,128)}, u32[]{:S(2)}) copy-start(f32[2,1024]{1,0:T(2,128)} %constant.118.clone.wave) | copy-start | bytes 24580
  46.8 24.3 %copy-start.1 = (f32[2,1024]{1,0:T(2,128)S(1)}, f32[2,1024]{1,0:T(2,128)}, u32[]{:S(2)}) copy-start(f32[2,1024]{1,0:T(2,128)} %constant.117.clone.lam) | copy-start | bytes 24580
  46.8 24.2 %all-to-all-start = ((f32[16,136,128]{2,1,0:T(8,128)}), f32[16,136,128]{2,1,0:T(8,128)S(1)}, u32[]{:S(2)}, u32[]{:S(2)}) async-start(f32[16,136,128]{2,1,0:T(8,128)} %modes.1), calls=%async_computation | async-start | bytes 2228224 | tf_op jit(solution)/shard_map/all_to_all | solution.py:547
  79.6 30.5 %all-to-all-start.1 = ((f32[16,264,128]{2,1,0:T(8,128)}), f32[16,264,128]{2,1,0:T(8,128)S(1)}, u32[]{:S(2)}, u32[]{:S(2)}) async-start(f32[16,264,128]{2,1,0:T(8,128)} %columns.1), calls=%async_computation.1 | async-start | bytes 4325376 | tf_op jit(solution)/shard_map/all_to_all | solution.py:564
  120.8 11.9 %collective-permute-start.5 = (f32[2,128,128]{2,1,0:T(8,128)S(1)}, f32[2,128,128]{2,1,0:T(8,128)S(1)}, u32[]{:S(2)}, u32[]{:S(2)}) collective-permute-start(f32[2,128,128]{2,1,0:T(8,128)S(1)} %get-tuple-element.41), channel_id=1, source_target_pairs={{4,9},{5,8},{12,1},{13,0},{20,13},{21,12},{28,5},{29,4},{0,25},{1,... | collective-permute-start | bytes 393224 | tf_op jit(solution)/shard_map/ppermute | solution.py:591
  124.5 9.8 %collective-permute-start.6 = (f32[2,128,128]{2,1,0:T(8,128)S(1)}, f32[2,128,128]{2,1,0:T(8,128)S(1)}, u32[]{:S(2)}, u32[]{:S(2)}) collective-permute-start(f32[2,128,128]{2,1,0:T(8,128)S(1)} %get-tuple-element.42), channel_id=1, source_target_pairs={{4,8},{5,9},{12,0},{13,1},{20,12},{21,13},{28,4},{29,5},{0,24},{1,... | collective-permute-start | bytes 393224 | tf_op jit(solution)/shard_map/ppermute | solution.py:591
  124.5 24.4 %copy-start.2 = (f32[1,2,16384]{2,1,0:T(2,128)S(1)}, f32[1,2,16384]{2,1,0:T(2,128)}, u32[]{:S(2)}) copy-start(f32[1,2,16384]{2,1,0:T(2,128)} %param.17) | copy-start | bytes 393220
  129.7 10.6 %collective-permute-start.7 = (f32[2,128,128]{2,1,0:T(8,128)S(1)}, f32[2,128,128]{2,1,0:T(8,128)S(1)}, u32[]{:S(2)}, u32[]{:S(2)}) collective-permute-start(f32[2,128,128]{2,1,0:T(8,128)S(1)} %get-tuple-element.45), channel_id=1, source_target_pairs={{4,1},{5,0},{12,9},{13,8},{20,5},{21,4},{28,13},{29,12},{0,17},{1,... | collective-permute-start | bytes 393224 | tf_op jit(solution)/shard_map/ppermute | solution.py:591
  132.6 8.9 %collective-permute-start.8 = (f32[2,128,128]{2,1,0:T(8,128)S(1)}, f32[2,128,128]{2,1,0:T(8,128)S(1)}, u32[]{:S(2)}, u32[]{:S(2)}) collective-permute-start(f32[2,128,128]{2,1,0:T(8,128)S(1)} %get-tuple-element.46), channel_id=1, source_target_pairs={{4,0},{5,1},{12,8},{13,9},{20,4},{21,5},{28,12},{29,13},{0,16},{1,... | collective-permute-start | bytes 393224 | tf_op jit(solution)/shard_map/ppermute | solution.py:591

commit v6 on v5

--- a/solution.py
+++ b/solution.py
@@ -186,7 +186,7 @@
         rows = pair_weights(short(row), short(weights[which, 0]), short(weights[which, 1]), window)
         both = dot(cols, rows, ((1,), (1,)))
         half = half_of(which) if count > 4 else 0
-        parts[place][half, :, pl.ds(at, window)] += both[:pad_cols] + both[tall : tall + pad_cols]
+        parts[place if count > 4 else half_of(which)][half, :, pl.ds(at, window)] += both[:pad_cols] + both[tall : tall + pad_cols]
 
     for group in groups_of(count):
         each_window(strips, scalars, first, last, group, strip_blocks(strips, scalars, first, last, group), item)
@@ -194,12 +194,12 @@
         if count > 4:
             used = [part[half] for part in parts]
         else:
-            used = [part[0] for which, part in enumerate(parts) if half_of(which) == half]
+            used = [parts[half][0]]
         charge[half] = functools.reduce(jnp.add, used)
 
 
 def deposit_parts(count, charge_shape):
-    return [pltpu.VMEM((2 if count > 4 else 1, *charge_shape[1:]), jnp.float32)] * min(count, 4)
+    return [pltpu.VMEM((2 if count > 4 else 1, *charge_shape[1:]), jnp.float32)] * (4 if count > 4 else 2)
 
 
 def sample_start(strips, scalars, first, last, kicks, begin):

time: 150 us -> 149 us (level)
  starting transfers between devices: 34.4 us -> 32.1 us
  Pallas kernels: 34.8 us -> 36.9 us
    ppermute x4, starting transfers between devices: 6.69 us -> 5.07 us  [shards(): lax.ppermute(kick, ('q', 'tx', 'hi', 'dom'), returned(other_route, n_tx,...]
  transfers between devices with their start and end apart: 11 -> 11, of which waited for: 5 -> 5; matrix products, arithmetic and copies ran while one was open for 2% -> 2% of each run, Pallas kernels for 10% -> 11%
where the time goes in v6:
time: 149 us; the launch traced here: 148 us
  waiting for transfers between devices  48 us (32%)
  Pallas kernels  36.9 us (25%)
  starting transfers between devices  32.1 us (22%)
  other arithmetic  17.9 us (12%)
  blocking collectives  11.1 us (7%)
  local copies, waits for them, and re-layouts  2.04 us (1%)
    all_to_all x1, waiting for transfers between devices, shards(): halves = lax.all_to_all(halves, cube, 0, 0, tiled=True)  25.7 us
    all_to_all x1, waiting for transfers between devices, shards(): by_mode = lax.all_to_all(by_mode, cube, 0, 0, tiled=True)  14.6 us
    pallas_call x1, Pallas kernels, shards(): pl.pallas_call(functools.partial(kicks_kernel, strips), out_shape=[kick_s...  11.4 us
    all_gather x1, blocking collectives, shards(): own = lax.all_gather(own, ('tx', 'dom'), axis=0)  11.1 us
    ppermute x1, starting transfers between devices, shards(): other = lax.ppermute(mine, ('q', 'hi'), other_route)  11 us
    pallas_call x1, Pallas kernels, shards(): pl.pallas_call(functools.partial(modes_kernel, strips), out_shape=jax.Sha...  10.7 us
    pallas_call x1, Pallas kernels, shards(): pl.pallas_call(functools.partial(columns_kernel, straight, flipped, lists...  8.61 us
    all_to_all x1, starting transfers between devices, shards(): by_mode = lax.all_to_all(by_mode, cube, 0, 0, tiled=True)  8.11 us
  transfers between devices with their start and end apart: 11, of which 5 were waited for; matrix products, arithmetic and copies ran while one was open for 2% of the time, Pallas kernels for 11%

profile of v6, /device:TPU:0, one launch (start us, length us, event | category | flops | bytes accessed | tf_op | source)
XLA Modules:
  0.0 148.4 jit_solution(10424178854276478886)
XLA Ops:
  0.0 1.0 add_bitcast_fusion
  1.0 7.5 %sort.42 = (s32[16384]{0:T(1024)S(1)}, f32[16384]{0:T(1024)S(1)}, s32[16384]{0:T(1024)S(1)}) sort(s32[16384]{0:T(1024)S(1)} %add_bitcast_fusion, f32[16384]{0:T(1024)} %bitcast.35, s32[16384]{0:T(1024)S(1)} %iota.10), dimensions={0}, to_apply=%region_0.1 | sort | flops 229376 | bytes 393216 | tf_op jit(solution)/shard_map/sort | solution.py:485
  8.6 0.7 collective-permute-start
  9.4 0.1 fusion.10
  9.6 11.0 %collective-permute-start.1 = (f32[2,128,128]{2,1,0:T(8,128)S(1)}, f32[2,128,128]{2,1,0:T(8,128)S(1)}, u32[]{:S(2)}, u32[]{:S(2)}) collective-permute-start(f32[2,128,128]{2,1,0:T(8,128)S(1)} %pad_maximum_fusion.2), channel_id=1, source_target_pairs={{0,4},{4,20},{16,0},{20,16},{1,5},{5,21},{17,1},{21,17},{2,6},{6,2... | collective-permute-start | bytes 393224 | tf_op jit(solution)/shard_map/ppermute | solution.py:494
  20.6 11.1 %all-gather = f32[12,128,128]{2,1,0:T(8,128)S(1)} all-gather(f32[3,128,128]{2,1,0:T(8,128)S(1)} %collective-permute-done), channel_id=2, replica_groups=mesh['q'=2,'tx'=2,'hi'=2,'lo'=2,'dom'=2] {'tx','dom'}, dimensions={0}, use_global_device_ids=true | all-gather | bytes 983040 | tf_op jit(solution)/shard_map/all_gather | solution.py:495
  31.7 1.9 %collective-permute-start.4 = (f32[2,128,128]{2,1,0:T(8,128)S(1)}, f32[2,128,128]{2,1,0:T(8,128)S(1)}, u32[]{:S(2)}, u32[]{:S(2)}) collective-permute-start(f32[2,128,128]{2,1,0:T(8,128)S(1)} %collective-permute-done.1), channel_id=1, source_target_pairs={{1,0},{0,1},{9,8},{8,9},{3,2},{2,3},{11,10},{10,11},{5,4},{4,5},{1... | collective-permute-start | bytes 393224 | tf_op jit(solution)/shard_map/ppermute | solution.py:498
  33.6 0.2 collective-permute-start.3
  33.8 1.5 collective-permute-start.2
  35.4 0.4 slice.19
  35.8 0.2 slice.18
  35.9 0.4 convert_reduce_fusion.2
  36.3 10.7 %modes.1 = f32[16,136,128]{2,1,0:T(8,128)} custom-call(s32[5]{0:T(128)S(1)} %pad_add_fusion.1.scalars, s32[4,2,32]{2,1,0:T(2,128)S(1)} %get-tuple-element.61.first, s32[4,2,32]{2,1,0:T(2,128)S(1)} %get-tuple-element.60.last, f32[4,4]{1,0:T(4,128)S(1)} %get-tuple-element.58.weights, f32[4,3,128,128]{3,2,1,0:T(8,128)S(1)} %bitcast.28, ...), custom_call_target="tpu_custom_call" | custom-call | tf_op jit(solution)/shard_map/modes/pallas_call | solution.py:529
  47.0 8.1 %all-to-all-start = ((f32[16,136,128]{2,1,0:T(8,128)}), f32[16,136,128]{2,1,0:T(8,128)S(1)}, u32[]{:S(2)}, u32[]{:S(2)}) async-start(f32[16,136,128]{2,1,0:T(8,128)} %modes.1), calls=%async_computation | async-start | bytes 2228224 | tf_op jit(solution)/shard_map/all_to_all | solution.py:547
  55.1 0.9 constant_dynamic-slice_fusion.mine
  56.0 14.6 %all-to-all-done.by_mode = f32[16,136,128]{2,1,0:T(8,128)S(1)} async-done(((f32[16,136,128]{2,1,0:T(8,128)}), f32[16,136,128]{2,1,0:T(8,128)S(1)}, u32[]{:S(2)}, u32[]{:S(2)}) %all-to-all-start) | async-done | bytes 1114144 | tf_op jit(solution)/shard_map/all_to_all | solution.py:547
  70.6 8.6 %columns.1 = f32[16,264,128]{2,1,0:T(8,128)} custom-call(f32[16,136,128]{2,1,0:T(8,128)S(1)} %all-to-all-done.by_mode, f32[2,1024]{1,0:T(2,128)S(1)} %copy-done.1, f32[2,1024]{1,0:T(2,128)S(1)} %copy-done, f32[128,2]{1,0:T(8,128)S(1)} %constant_dynamic-slice_fusion.mine, bf16[4,1024,1024]{2,1,0:T(8,128)(2,1)} %constant.115.clone.stored), custom_call_target="tpu_custom_call" | custom-call | tf_op jit(solution)/shard_map/columns/pallas_call | solution.py:555
  79.2 3.7 %all-to-all-start.1 = ((f32[16,264,128]{2,1,0:T(8,128)}), f32[16,264,128]{2,1,0:T(8,128)S(1)}, u32[]{:S(2)}, u32[]{:S(2)}) async-start(f32[16,264,128]{2,1,0:T(8,128)} %columns.1), calls=%async_computation.1 | async-start | bytes 4325376 | tf_op jit(solution)/shard_map/all_to_all | solution.py:564
  83.1 0.4 slice.21
  83.5 0.1 slice.20
  83.6 0.2 convert_reduce_fusion.last
  83.9 0.2 convert_reduce_fusion.1.first
  84.1 25.7 %all-to-all-done.1.halves = f32[16,264,128]{2,1,0:T(8,128)S(1)} async-done(((f32[16,264,128]{2,1,0:T(8,128)}), f32[16,264,128]{2,1,0:T(8,128)S(1)}, u32[]{:S(2)}, u32[]{:S(2)}) %all-to-all-start.1) | async-done | bytes 2162720 | tf_op jit(solution)/shard_map/all_to_all | solution.py:564
  109.7 11.4 %kicks.1 = (f32[2,128,128]{2,1,0:T(8,128)S(1)}, f32[2,128,128]{2,1,0:T(8,128)S(1)}, bf16[2,272,1280]{2,1,0:T(8,128)(2,1)S(1)}, bf16[2,272,1280]{2,1,0:T(8,128)(2,1)S(1)}) custom-call(s32[5]{0:T(128)S(1)} %pad_add_fusion.scalars, s32[4,2,32]{2,1,0:T(2,128)S(1)} %convert_reduce_fusion.1.first, s32[4,2,32]{2,1,0:T(2,128)S(1)} %convert_reduce_fusion.last, ...), custom_call_target="tpu_custom_call" | custom-call | tf_op jit(solution)/shard_map/kicks/pallas_call | solution.py:568
  121.2 4.7 %collective-permute-start.5 = (f32[2,128,128]{2,1,0:T(8,128)S(1)}, f32[2,128,128]{2,1,0:T(8,128)S(1)}, u32[]{:S(2)}, u32[]{:S(2)}) collective-permute-start(f32[2,128,128]{2,1,0:T(8,128)S(1)} %get-tuple-element.41), channel_id=1, source_target_pairs={{4,9},{5,8},{12,1},{13,0},{20,13},{21,12},{28,5},{29,4},{0,25},{1,... | collective-permute-start | bytes 393224 | tf_op jit(solution)/shard_map/ppermute | solution.py:591
  125.9 6.2 %sample.1 = (f32[2,128,128]{2,1,0:T(8,128)S(1)}, f32[2,128,128]{2,1,0:T(8,128)S(1)}) custom-call(s32[5]{0:T(128)S(1)} %pad_add_fusion.scalars, s32[4,2,32]{2,1,0:T(2,128)S(1)} %convert_reduce_fusion.1.first, s32[4,2,32]{2,1,0:T(2,128)S(1)} %convert_reduce_fusion.last, f32[4,4]{1,0:T(4,128)S(1)} %get-tuple-element.57.weights, ...), custom_call_target="tpu_custom_call" | custom-call | tf_op jit(solution)/shard_map/sample/pallas_call | solution.py:577
  132.1 0.3 collective-permute-start.7
  132.5 1.4 collective-permute-done.6
  133.9 5.5 %collective-permute-done.7 = f32[2,128,128]{2,1,0:T(8,128)S(1)} collective-permute-done((f32[2,128,128]{2,1,0:T(8,128)S(1)}, f32[2,128,128]{2,1,0:T(8,128)S(1)}, u32[]{:S(2)}, u32[]{:S(2)}) %collective-permute-start.7) | collective-permute-done | bytes 131104 | tf_op jit(solution)/shard_map/ppermute | solution.py:591
  139.4 0.8 collective-permute-done.8
  140.2 7.3 %sort.43 = (s32[16384]{0:T(1024)}, f32[16384]{0:T(1024)S(1)}, f32[16384]{0:T(1024)S(1)}) sort(s32[16384]{0:T(1024)S(1)} %get-tuple-element.29, f32[16384]{0:T(1024)S(1)} %get-tuple-element.52, f32[16384]{0:T(1024)S(1)} %get-tuple-element.51), dimensions={0}, to_apply=%region_1.2 | sort | flops 229376 | bytes 393216 | tf_op jit(solution)/shard_map/sort | solution.py:595
  147.6 0.8 fusion
  (36 shorter events, 0.6 us)
Async XLA Ops:
  0.0 9.3 %copy-start.5 = (f32[1,2]{1,0:T(1,128)S(1)}, f32[1,2]{1,0:T(1,128)}, u32[]{:S(2)}) copy-start(f32[1,2]{1,0:T(1,128)} %constant.112.clone) | copy-start | bytes 28
  0.0 9.3 %copy-start.6 = (f32[1,2]{1,0:T(1,128)S(1)}, f32[1,2]{1,0:T(1,128)}, u32[]{:S(2)}) copy-start(f32[1,2]{1,0:T(1,128)} %constant.111.clone) | copy-start | bytes 28
  0.0 9.5 %copy-start.3 = (f32[2]{0:T(128)S(1)}, f32[2]{0:T(128)}, u32[]{:S(2)}) copy-start(f32[2]{0:T(128)} %constant.124) | copy-start | bytes 28
  0.0 9.5 %copy-start.4 = (f32[2]{0:T(128)S(1)}, f32[2]{0:T(128)}, u32[]{:S(2)}) copy-start(f32[2]{0:T(128)} %constant.123) | copy-start | bytes 28
  8.6 1.0 collective-permute-start
  9.6 22.1 %collective-permute-start.1 = (f32[2,128,128]{2,1,0:T(8,128)S(1)}, f32[2,128,128]{2,1,0:T(8,128)S(1)}, u32[]{:S(2)}, u32[]{:S(2)}) collective-permute-start(f32[2,128,128]{2,1,0:T(8,128)S(1)} %pad_maximum_fusion.2), channel_id=1, source_target_pairs={{0,4},{4,20},{16,0},{20,16},{1,5},{5,21},{17,1},{21,17},{2,6},{6,2... | collective-permute-start | bytes 393224 | tf_op jit(solution)/shard_map/ppermute | solution.py:494
  31.7 15.2 %collective-permute-start.4 = (f32[2,128,128]{2,1,0:T(8,128)S(1)}, f32[2,128,128]{2,1,0:T(8,128)S(1)}, u32[]{:S(2)}, u32[]{:S(2)}) collective-permute-start(f32[2,128,128]{2,1,0:T(8,128)S(1)} %collective-permute-done.1), channel_id=1, source_target_pairs={{1,0},{0,1},{9,8},{8,9},{3,2},{2,3},{11,10},{10,11},{5,4},{4,5},{1... | collective-permute-start | bytes 393224 | tf_op jit(solution)/shard_map/ppermute | solution.py:498
  33.6 13.4 %collective-permute-start.3 = (f32[2,128,128]{2,1,0:T(8,128)S(1)}, f32[2,128,128]{2,1,0:T(8,128)S(1)}, u32[]{:S(2)}, u32[]{:S(2)}) collective-permute-start(f32[2,128,128]{2,1,0:T(8,128)S(1)} %collective-permute-done.1), channel_id=1, source_target_pairs={{8,0},{9,1},{0,8},{1,9},{10,2},{11,3},{2,10},{3,11},{12,4},{13,5},... | collective-permute-start | bytes 393224 | tf_op jit(solution)/shard_map/ppermute | solution.py:498
  33.8 13.2 %collective-permute-start.2 = (f32[2,128,128]{2,1,0:T(8,128)S(1)}, f32[2,128,128]{2,1,0:T(8,128)S(1)}, u32[]{:S(2)}, u32[]{:S(2)}) collective-permute-start(f32[2,128,128]{2,1,0:T(8,128)S(1)} %collective-permute-done.1), channel_id=1, source_target_pairs={{9,0},{8,1},{1,8},{0,9},{11,2},{10,3},{3,10},{2,11},{13,4},{12,5},... | collective-permute-start | bytes 393224 | tf_op jit(solution)/shard_map/ppermute | solution.py:498
  47.0 23.7 %copy-start = (f32[2,1024]{1,0:T(2,128)S(1)}, f32[2,1024]{1,0:T(2,128)}, u32[]{:S(2)}) copy-start(f32[2,1024]{1,0:T(2,128)} %constant.118.clone.wave) | copy-start | bytes 24580
  47.0 23.7 %copy-start.1 = (f32[2,1024]{1,0:T(2,128)S(1)}, f32[2,1024]{1,0:T(2,128)}, u32[]{:S(2)}) copy-start(f32[2,1024]{1,0:T(2,128)} %constant.117.clone.lam) | copy-start | bytes 24580
  47.0 23.6 %all-to-all-start = ((f32[16,136,128]{2,1,0:T(8,128)}), f32[16,136,128]{2,1,0:T(8,128)S(1)}, u32[]{:S(2)}, u32[]{:S(2)}) async-start(f32[16,136,128]{2,1,0:T(8,128)} %modes.1), calls=%async_computation | async-start | bytes 2228224 | tf_op jit(solution)/shard_map/all_to_all | solution.py:547
  79.2 30.5 %all-to-all-start.1 = ((f32[16,264,128]{2,1,0:T(8,128)}), f32[16,264,128]{2,1,0:T(8,128)S(1)}, u32[]{:S(2)}, u32[]{:S(2)}) async-start(f32[16,264,128]{2,1,0:T(8,128)} %columns.1), calls=%async_computation.1 | async-start | bytes 4325376 | tf_op jit(solution)/shard_map/all_to_all | solution.py:564
  121.2 11.3 %collective-permute-start.5 = (f32[2,128,128]{2,1,0:T(8,128)S(1)}, f32[2,128,128]{2,1,0:T(8,128)S(1)}, u32[]{:S(2)}, u32[]{:S(2)}) collective-permute-start(f32[2,128,128]{2,1,0:T(8,128)S(1)} %get-tuple-element.41), channel_id=1, source_target_pairs={{4,9},{5,8},{12,1},{13,0},{20,13},{21,12},{28,5},{29,4},{0,25},{1,... | collective-permute-start | bytes 393224 | tf_op jit(solution)/shard_map/ppermute | solution.py:591
  125.9 8.0 %collective-permute-start.6 = (f32[2,128,128]{2,1,0:T(8,128)S(1)}, f32[2,128,128]{2,1,0:T(8,128)S(1)}, u32[]{:S(2)}, u32[]{:S(2)}) collective-permute-start(f32[2,128,128]{2,1,0:T(8,128)S(1)} %get-tuple-element.42), channel_id=1, source_target_pairs={{4,8},{5,9},{12,0},{13,1},{20,12},{21,13},{28,4},{29,5},{0,24},{1,... | collective-permute-start | bytes 393224 | tf_op jit(solution)/shard_map/ppermute | solution.py:591
  125.9 21.7 %copy-start.2 = (f32[1,2,16384]{2,1,0:T(2,128)S(1)}, f32[1,2,16384]{2,1,0:T(2,128)}, u32[]{:S(2)}) copy-start(f32[1,2,16384]{2,1,0:T(2,128)} %param.17) | copy-start | bytes 393220
  132.1 7.3 %collective-permute-start.7 = (f32[2,128,128]{2,1,0:T(8,128)S(1)}, f32[2,128,128]{2,1,0:T(8,128)S(1)}, u32[]{:S(2)}, u32[]{:S(2)}) collective-permute-start(f32[2,128,128]{2,1,0:T(8,128)S(1)} %get-tuple-element.45), channel_id=1, source_target_pairs={{4,1},{5,0},{12,9},{13,8},{20,5},{21,4},{28,13},{29,12},{0,17},{1,... | collective-permute-start | bytes 393224 | tf_op jit(solution)/shard_map/ppermute | solution.py:591
  132.4 7.8 %collective-permute-start.8 = (f32[2,128,128]{2,1,0:T(8,128)S(1)}, f32[2,128,128]{2,1,0:T(8,128)S(1)}, u32[]{:S(2)}, u32[]{:S(2)}) collective-permute-start(f32[2,128,128]{2,1,0:T(8,128)S(1)} %get-tuple-element.46), channel_id=1, source_target_pairs={{4,0},{5,1},{12,8},{13,9},{20,4},{21,5},{28,12},{29,13},{0,16},{1,... | collective-permute-start | bytes 393224 | tf_op jit(solution)/shard_map/ppermute | solution.py:591

commit v7 on v6

--- a/solution.py
+++ b/solution.py
@@ -270,7 +270,6 @@
 
 def columns_kernel(order, flipped, per_tile, strips, by_mode, lam, wave, mine, stored, halves, tables, arrived, outgoing, sent):
     table = fetch(stored, tables, arrived, (0, 1, 2, 3))
-    sine_parts = table(0)
     modes = by_mode.shape[2]
     near, far = ([], [])
     for place in range(len(order)):
@@ -284,6 +283,7 @@
         near.append(pair[0] + pair[1])
         far.append(pair[0] - pair[1])
     columns = jnp.concatenate([jnp.concatenate(near, 0).T * alternate((1, HALF), 1), jnp.concatenate(far, 0).T], 0)
+    sine_parts = table(0)
     spectrum = dot_parts(*sine_parts, columns, ((1,), (0,)))
     lam_mine, wave_mine = (mine[:, 0:1], mine[:, 1:2])
     hats = ([], [])

time: 149 us -> 150 us (level)
  starting transfers between devices: 32.1 us -> 34.1 us
  Pallas kernels: 36.9 us -> 35.1 us
    pallas_call x1, Pallas kernels: 6.18 us -> 4.57 us  [shards(): pl.pallas_call(functools.partial(sample_alone, strips, early), out_shape=...]
  transfers between devices with their start and end apart: 11 -> 11, of which waited for: 5 -> 5; matrix products, arithmetic and copies ran while one was open for 2% -> 2% of each run, Pallas kernels for 11% -> 10%
where the time goes in v7:
time: 150 us
  waiting for transfers between devices  49.2 us (33%)
  Pallas kernels  35.1 us (23%)
  starting transfers between devices  34.1 us (23%)
  other arithmetic  17.9 us (12%)
  blocking collectives  11.1 us (7%)
  local copies, waits for them, and re-layouts  2.04 us (1%)
    all_to_all x1, waiting for transfers between devices, shards(): halves = lax.all_to_all(halves, cube, 0, 0, tiled=True)  25.7 us
    all_to_all x1, waiting for transfers between devices, shards(): by_mode = lax.all_to_all(by_mode, cube, 0, 0, tiled=True)  14.6 us
    pallas_call x1, Pallas kernels, shards(): pl.pallas_call(functools.partial(kicks_kernel, strips), out_shape=[kick_s...  11.4 us
    all_gather x1, blocking collectives, shards(): own = lax.all_gather(own, ('tx', 'dom'), axis=0)  11.1 us
    ppermute x1, starting transfers between devices, shards(): other = lax.ppermute(mine, ('q', 'hi'), other_route)  11 us
    pallas_call x1, Pallas kernels, shards(): pl.pallas_call(functools.partial(modes_kernel, strips), out_shape=jax.Sha...  10.4 us
    ppermute x4, waiting for transfers between devices, shards(): lax.ppermute(kick, ('q', 'tx', 'hi', 'dom'), returned(other_route, n_tx,...  8.91 us
    pallas_call x1, Pallas kernels, shards(): pl.pallas_call(functools.partial(columns_kernel, straight, flipped, lists...  8.77 us
  transfers between devices with their start and end apart: 11, of which 5 were waited for; matrix products, arithmetic and copies ran while one was open for 2% of the time, Pallas kernels for 10%

profile of v7, /device:TPU:0, one launch (start us, length us, event | category | flops | bytes accessed | tf_op | source)
XLA Modules:
  0.0 149.7 jit_solution(14755522217031099263)
XLA Ops:
  0.0 1.0 add_bitcast_fusion
  1.0 7.5 %sort.42 = (s32[16384]{0:T(1024)S(1)}, f32[16384]{0:T(1024)S(1)}, s32[16384]{0:T(1024)S(1)}) sort(s32[16384]{0:T(1024)S(1)} %add_bitcast_fusion, f32[16384]{0:T(1024)} %bitcast.35, s32[16384]{0:T(1024)S(1)} %iota.10), dimensions={0}, to_apply=%region_0.1 | sort | flops 229376 | bytes 393216 | tf_op jit(solution)/shard_map/sort | solution.py:485
  8.6 0.7 collective-permute-start
  9.6 11.0 %collective-permute-start.1 = (f32[2,128,128]{2,1,0:T(8,128)S(1)}, f32[2,128,128]{2,1,0:T(8,128)S(1)}, u32[]{:S(2)}, u32[]{:S(2)}) collective-permute-start(f32[2,128,128]{2,1,0:T(8,128)S(1)} %pad_maximum_fusion.2), channel_id=1, source_target_pairs={{0,4},{4,20},{16,0},{20,16},{1,5},{5,21},{17,1},{21,17},{2,6},{6,2... | collective-permute-start | bytes 393224 | tf_op jit(solution)/shard_map/ppermute | solution.py:494
  20.6 11.1 %all-gather = f32[12,128,128]{2,1,0:T(8,128)S(1)} all-gather(f32[3,128,128]{2,1,0:T(8,128)S(1)} %collective-permute-done), channel_id=2, replica_groups=mesh['q'=2,'tx'=2,'hi'=2,'lo'=2,'dom'=2] {'tx','dom'}, dimensions={0}, use_global_device_ids=true | all-gather | bytes 983040 | tf_op jit(solution)/shard_map/all_gather | solution.py:495
  31.7 1.9 %collective-permute-start.4 = (f32[2,128,128]{2,1,0:T(8,128)S(1)}, f32[2,128,128]{2,1,0:T(8,128)S(1)}, u32[]{:S(2)}, u32[]{:S(2)}) collective-permute-start(f32[2,128,128]{2,1,0:T(8,128)S(1)} %collective-permute-done.1), channel_id=1, source_target_pairs={{1,0},{0,1},{9,8},{8,9},{3,2},{2,3},{11,10},{10,11},{5,4},{4,5},{1... | collective-permute-start | bytes 393224 | tf_op jit(solution)/shard_map/ppermute | solution.py:498
  33.6 0.2 collective-permute-start.3
  33.8 1.5 collective-permute-start.2
  35.4 0.4 slice.19
  35.8 0.2 slice.18
  35.9 0.4 convert_reduce_fusion.2
  36.3 10.4 %modes.1 = f32[16,136,128]{2,1,0:T(8,128)} custom-call(s32[5]{0:T(128)S(1)} %pad_add_fusion.1.scalars, s32[4,2,32]{2,1,0:T(2,128)S(1)} %get-tuple-element.61.first, s32[4,2,32]{2,1,0:T(2,128)S(1)} %get-tuple-element.60.last, f32[4,4]{1,0:T(4,128)S(1)} %get-tuple-element.58.weights, f32[4,3,128,128]{3,2,1,0:T(8,128)S(1)} %bitcast.28, ...), custom_call_target="tpu_custom_call" | custom-call | tf_op jit(solution)/shard_map/modes/pallas_call | solution.py:529
  46.7 8.7 %all-to-all-start = ((f32[16,136,128]{2,1,0:T(8,128)}), f32[16,136,128]{2,1,0:T(8,128)S(1)}, u32[]{:S(2)}, u32[]{:S(2)}) async-start(f32[16,136,128]{2,1,0:T(8,128)} %modes.1), calls=%async_computation | async-start | bytes 2228224 | tf_op jit(solution)/shard_map/all_to_all | solution.py:547
  55.4 0.9 constant_dynamic-slice_fusion.mine
  56.3 14.6 %all-to-all-done.by_mode = f32[16,136,128]{2,1,0:T(8,128)S(1)} async-done(((f32[16,136,128]{2,1,0:T(8,128)}), f32[16,136,128]{2,1,0:T(8,128)S(1)}, u32[]{:S(2)}, u32[]{:S(2)}) %all-to-all-start) | async-done | bytes 1114144 | tf_op jit(solution)/shard_map/all_to_all | solution.py:547
  70.9 8.8 %columns.1 = f32[16,264,128]{2,1,0:T(8,128)} custom-call(f32[16,136,128]{2,1,0:T(8,128)S(1)} %all-to-all-done.by_mode, f32[2,1024]{1,0:T(2,128)S(1)} %copy-done.1, f32[2,1024]{1,0:T(2,128)S(1)} %copy-done, f32[128,2]{1,0:T(8,128)S(1)} %constant_dynamic-slice_fusion.mine, bf16[4,1024,1024]{2,1,0:T(8,128)(2,1)} %constant.115.clone.stored), custom_call_target="tpu_custom_call" | custom-call | tf_op jit(solution)/shard_map/columns/pallas_call | solution.py:555
  79.7 3.7 %all-to-all-start.1 = ((f32[16,264,128]{2,1,0:T(8,128)}), f32[16,264,128]{2,1,0:T(8,128)S(1)}, u32[]{:S(2)}, u32[]{:S(2)}) async-start(f32[16,264,128]{2,1,0:T(8,128)} %columns.1), calls=%async_computation.1 | async-start | bytes 4325376 | tf_op jit(solution)/shard_map/all_to_all | solution.py:564
  83.5 0.4 slice.21
  84.1 0.2 convert_reduce_fusion.last
  84.3 0.2 convert_reduce_fusion.1.first
  84.5 25.7 %all-to-all-done.1.halves = f32[16,264,128]{2,1,0:T(8,128)S(1)} async-done(((f32[16,264,128]{2,1,0:T(8,128)}), f32[16,264,128]{2,1,0:T(8,128)S(1)}, u32[]{:S(2)}, u32[]{:S(2)}) %all-to-all-start.1) | async-done | bytes 2162720 | tf_op jit(solution)/shard_map/all_to_all | solution.py:564
  110.2 11.4 %kicks.1 = (f32[2,128,128]{2,1,0:T(8,128)S(1)}, f32[2,128,128]{2,1,0:T(8,128)S(1)}, bf16[2,272,1280]{2,1,0:T(8,128)(2,1)S(1)}, bf16[2,272,1280]{2,1,0:T(8,128)(2,1)S(1)}) custom-call(s32[5]{0:T(128)S(1)} %pad_add_fusion.scalars, s32[4,2,32]{2,1,0:T(2,128)S(1)} %convert_reduce_fusion.1.first, s32[4,2,32]{2,1,0:T(2,128)S(1)} %convert_reduce_fusion.last, ...), custom_call_target="tpu_custom_call" | custom-call | tf_op jit(solution)/shard_map/kicks/pallas_call | solution.py:568
  121.6 2.9 %collective-permute-start.5 = (f32[2,128,128]{2,1,0:T(8,128)S(1)}, f32[2,128,128]{2,1,0:T(8,128)S(1)}, u32[]{:S(2)}, u32[]{:S(2)}) collective-permute-start(f32[2,128,128]{2,1,0:T(8,128)S(1)} %get-tuple-element.41), channel_id=1, source_target_pairs={{4,9},{5,8},{12,1},{13,0},{20,13},{21,12},{28,5},{29,4},{0,25},{1,... | collective-permute-start | bytes 393224 | tf_op jit(solution)/shard_map/ppermute | solution.py:591
  124.5 0.9 collective-permute-start.6
  125.4 4.6 %sample.1 = (f32[2,128,128]{2,1,0:T(8,128)S(1)}, f32[2,128,128]{2,1,0:T(8,128)S(1)}) custom-call(s32[5]{0:T(128)S(1)} %pad_add_fusion.scalars, s32[4,2,32]{2,1,0:T(2,128)S(1)} %convert_reduce_fusion.1.first, s32[4,2,32]{2,1,0:T(2,128)S(1)} %convert_reduce_fusion.last, f32[4,4]{1,0:T(4,128)S(1)} %get-tuple-element.57.weights, ...), custom_call_target="tpu_custom_call" | custom-call | tf_op jit(solution)/shard_map/sample/pallas_call | solution.py:577
  130.0 1.4 collective-permute-start.7
  131.4 1.2 collective-permute-start.8
  132.6 5.9 %collective-permute-done.6 = f32[2,128,128]{2,1,0:T(8,128)S(1)} collective-permute-done((f32[2,128,128]{2,1,0:T(8,128)S(1)}, f32[2,128,128]{2,1,0:T(8,128)S(1)}, u32[]{:S(2)}, u32[]{:S(2)}) %collective-permute-start.6) | collective-permute-done | bytes 131104 | tf_op jit(solution)/shard_map/ppermute | solution.py:591
  138.5 1.3 collective-permute-done.7
  139.8 1.7 %collective-permute-done.8 = f32[2,128,128]{2,1,0:T(8,128)S(1)} collective-permute-done((f32[2,128,128]{2,1,0:T(8,128)S(1)}, f32[2,128,128]{2,1,0:T(8,128)S(1)}, u32[]{:S(2)}, u32[]{:S(2)}) %collective-permute-start.8) | collective-permute-done | bytes 131104 | tf_op jit(solution)/shard_map/ppermute | solution.py:591
  141.6 7.3 %sort.43 = (s32[16384]{0:T(1024)}, f32[16384]{0:T(1024)S(1)}, f32[16384]{0:T(1024)S(1)}) sort(s32[16384]{0:T(1024)S(1)} %get-tuple-element.29, f32[16384]{0:T(1024)S(1)} %get-tuple-element.52, f32[16384]{0:T(1024)S(1)} %get-tuple-element.51), dimensions={0}, to_apply=%region_1.2 | sort | flops 229376 | bytes 393216 | tf_op jit(solution)/shard_map/sort | solution.py:595
  148.9 0.8 fusion
  (36 shorter events, 0.8 us)
Async XLA Ops:
  0.0 9.3 %copy-start.5 = (f32[1,2]{1,0:T(1,128)S(1)}, f32[1,2]{1,0:T(1,128)}, u32[]{:S(2)}) copy-start(f32[1,2]{1,0:T(1,128)} %constant.112.clone) | copy-start | bytes 28
  0.0 9.3 %copy-start.6 = (f32[1,2]{1,0:T(1,128)S(1)}, f32[1,2]{1,0:T(1,128)}, u32[]{:S(2)}) copy-start(f32[1,2]{1,0:T(1,128)} %constant.111.clone) | copy-start | bytes 28
  0.0 9.5 %copy-start.3 = (f32[2]{0:T(128)S(1)}, f32[2]{0:T(128)}, u32[]{:S(2)}) copy-start(f32[2]{0:T(128)} %constant.124) | copy-start | bytes 28
  0.0 9.5 %copy-start.4 = (f32[2]{0:T(128)S(1)}, f32[2]{0:T(128)}, u32[]{:S(2)}) copy-start(f32[2]{0:T(128)} %constant.123) | copy-start | bytes 28
  8.6 1.0 collective-permute-start
  9.6 22.1 %collective-permute-start.1 = (f32[2,128,128]{2,1,0:T(8,128)S(1)}, f32[2,128,128]{2,1,0:T(8,128)S(1)}, u32[]{:S(2)}, u32[]{:S(2)}) collective-permute-start(f32[2,128,128]{2,1,0:T(8,128)S(1)} %pad_maximum_fusion.2), channel_id=1, source_target_pairs={{0,4},{4,20},{16,0},{20,16},{1,5},{5,21},{17,1},{21,17},{2,6},{6,2... | collective-permute-start | bytes 393224 | tf_op jit(solution)/shard_map/ppermute | solution.py:494
  31.7 15.0 %collective-permute-start.4 = (f32[2,128,128]{2,1,0:T(8,128)S(1)}, f32[2,128,128]{2,1,0:T(8,128)S(1)}, u32[]{:S(2)}, u32[]{:S(2)}) collective-permute-start(f32[2,128,128]{2,1,0:T(8,128)S(1)} %collective-permute-done.1), channel_id=1, source_target_pairs={{1,0},{0,1},{9,8},{8,9},{3,2},{2,3},{11,10},{10,11},{5,4},{4,5},{1... | collective-permute-start | bytes 393224 | tf_op jit(solution)/shard_map/ppermute | solution.py:498
  33.6 13.1 %collective-permute-start.3 = (f32[2,128,128]{2,1,0:T(8,128)S(1)}, f32[2,128,128]{2,1,0:T(8,128)S(1)}, u32[]{:S(2)}, u32[]{:S(2)}) collective-permute-start(f32[2,128,128]{2,1,0:T(8,128)S(1)} %collective-permute-done.1), channel_id=1, source_target_pairs={{8,0},{9,1},{0,8},{1,9},{10,2},{11,3},{2,10},{3,11},{12,4},{13,5},... | collective-permute-start | bytes 393224 | tf_op jit(solution)/shard_map/ppermute | solution.py:498
  33.8 12.9 %collective-permute-start.2 = (f32[2,128,128]{2,1,0:T(8,128)S(1)}, f32[2,128,128]{2,1,0:T(8,128)S(1)}, u32[]{:S(2)}, u32[]{:S(2)}) collective-permute-start(f32[2,128,128]{2,1,0:T(8,128)S(1)} %collective-permute-done.1), channel_id=1, source_target_pairs={{9,0},{8,1},{1,8},{0,9},{11,2},{10,3},{3,10},{2,11},{13,4},{12,5},... | collective-permute-start | bytes 393224 | tf_op jit(solution)/shard_map/ppermute | solution.py:498
  46.7 24.2 %copy-start = (f32[2,1024]{1,0:T(2,128)S(1)}, f32[2,1024]{1,0:T(2,128)}, u32[]{:S(2)}) copy-start(f32[2,1024]{1,0:T(2,128)} %constant.118.clone.wave) | copy-start | bytes 24580
  46.7 24.2 %copy-start.1 = (f32[2,1024]{1,0:T(2,128)S(1)}, f32[2,1024]{1,0:T(2,128)}, u32[]{:S(2)}) copy-start(f32[2,1024]{1,0:T(2,128)} %constant.117.clone.lam) | copy-start | bytes 24580
  46.7 24.2 %all-to-all-start = ((f32[16,136,128]{2,1,0:T(8,128)}), f32[16,136,128]{2,1,0:T(8,128)S(1)}, u32[]{:S(2)}, u32[]{:S(2)}) async-start(f32[16,136,128]{2,1,0:T(8,128)} %modes.1), calls=%async_computation | async-start | bytes 2228224 | tf_op jit(solution)/shard_map/all_to_all | solution.py:547
  79.7 30.5 %all-to-all-start.1 = ((f32[16,264,128]{2,1,0:T(8,128)}), f32[16,264,128]{2,1,0:T(8,128)S(1)}, u32[]{:S(2)}, u32[]{:S(2)}) async-start(f32[16,264,128]{2,1,0:T(8,128)} %columns.1), calls=%async_computation.1 | async-start | bytes 4325376 | tf_op jit(solution)/shard_map/all_to_all | solution.py:564
  121.6 11.0 %collective-permute-start.5 = (f32[2,128,128]{2,1,0:T(8,128)S(1)}, f32[2,128,128]{2,1,0:T(8,128)S(1)}, u32[]{:S(2)}, u32[]{:S(2)}) collective-permute-start(f32[2,128,128]{2,1,0:T(8,128)S(1)} %get-tuple-element.41), channel_id=1, source_target_pairs={{4,9},{5,8},{12,1},{13,0},{20,13},{21,12},{28,5},{29,4},{0,25},{1,... | collective-permute-start | bytes 393224 | tf_op jit(solution)/shard_map/ppermute | solution.py:591
  124.5 14.0 %collective-permute-start.6 = (f32[2,128,128]{2,1,0:T(8,128)S(1)}, f32[2,128,128]{2,1,0:T(8,128)S(1)}, u32[]{:S(2)}, u32[]{:S(2)}) collective-permute-start(f32[2,128,128]{2,1,0:T(8,128)S(1)} %get-tuple-element.42), channel_id=1, source_target_pairs={{4,8},{5,9},{12,0},{13,1},{20,12},{21,13},{28,4},{29,5},{0,24},{1,... | collective-permute-start | bytes 393224 | tf_op jit(solution)/shard_map/ppermute | solution.py:591
  125.4 23.5 %copy-start.2 = (f32[1,2,16384]{2,1,0:T(2,128)S(1)}, f32[1,2,16384]{2,1,0:T(2,128)}, u32[]{:S(2)}) copy-start(f32[1,2,16384]{2,1,0:T(2,128)} %param.17) | copy-start | bytes 393220
  130.0 9.8 %collective-permute-start.7 = (f32[2,128,128]{2,1,0:T(8,128)S(1)}, f32[2,128,128]{2,1,0:T(8,128)S(1)}, u32[]{:S(2)}, u32[]{:S(2)}) collective-permute-start(f32[2,128,128]{2,1,0:T(8,128)S(1)} %get-tuple-element.45), channel_id=1, source_target_pairs={{4,1},{5,0},{12,9},{13,8},{20,5},{21,4},{28,13},{29,12},{0,17},{1,... | collective-permute-start | bytes 393224 | tf_op jit(solution)/shard_map/ppermute | solution.py:591
  131.4 10.2 %collective-permute-start.8 = (f32[2,128,128]{2,1,0:T(8,128)S(1)}, f32[2,128,128]{2,1,0:T(8,128)S(1)}, u32[]{:S(2)}, u32[]{:S(2)}) collective-permute-start(f32[2,128,128]{2,1,0:T(8,128)S(1)} %get-tuple-element.46), channel_id=1, source_target_pairs={{4,0},{5,1},{12,8},{13,9},{20,4},{21,5},{28,12},{29,13},{0,16},{1,... | collective-permute-start | bytes 393224 | tf_op jit(solution)/shard_map/ppermute | solution.py:591
